TPU v7x, 128 devices: a whole 4x4x4 slice. The times are simulated.
128 devices in a mesh: score: 8 (over z, core), mp: 16 (over y, x).
Axes of the slice: x: 4, y: 4, z: 4, core: 2. Of those that a mesh axis runs over, the one named last changes fastest.
Arguments:
- tokens: bfloat16 [48, 256, 3584], P('score', 'mp'), may hold values from -150 to 150
- gain: float32 [3584], replicated, may hold values from 0.1 to 1.9
- w_query: bfloat16 [3584, 2048], P(None, 'mp'), may hold values from -0.09375 to 0.09375
- b_query: float32 [2048], P('mp'), may hold values from -3 to 3
- w_key: bfloat16 [3584, 512], replicated, may hold values from -0.1875 to 0.1875
- b_key: float32 [512], replicated, may hold values from -3 to 3
- w_value: bfloat16 [3584, 512], replicated, may hold values from -0.75 to 0.75
- b_value: float32 [512], replicated, may hold values from -12 to 12
- rubric_cache: bfloat16 [8, 4, 2048, 256], P('score', None, 'mp'), may hold values from -420 to 420
- dest_of: int32 [48], replicated, may hold values from 0 to 7, as said below
- lengths: int32 [48], replicated, may hold values from 64 to 256
Outputs:
- rubric_attention: bfloat16 [8, 8, 256, 2048], P('score', None, None, 'mp')
Inputs may be any that keep to these rules, and one draw needn't show every extreme that they name: `dest_of`: the 6 responses of one rollout group go to 6 different scorer groups. In every draw one scorer group receives a response from every rollout group, and each of those has 256 tokens.
All inputs are finite; a program needn't handle non-finite values.
Results may differ from a plain program's by a relative error of at most 0.013.
The roundings to bfloat16 on the way count: a program that leaves them out, or rounds other values in their place, can miss the bound.
Values may be sent and summed in bfloat16 or wider, within the bound.
No kernel may reach another device: no remote copies, remote signals or barrier semaphores. Data moves between devices by JAX's collectives and lax.ppermute only.
A program may use at most 128 MiB of HBM per device.

v0:
```python
import math

import jax
import jax.numpy as jnp
from jax import lax
from jax.sharding import PartitionSpec as P

KV_HEADS = 4
HD = 128
LEN_MAX = 256
PROMPT = 2048


THETA = 1000000.0
EPSILON = 1e-06


def broadcast(block, axis, holder):
    block = jnp.where(lax.axis_index(axis) == holder, block, jnp.zeros_like(block))
    return lax.psum(block, axis)


def rotate(vectors, positions):
    half_width = vectors.shape[-1] // 2
    frequency = jnp.exp(
        jnp.arange(half_width, dtype=jnp.float32) * (-2.0 * math.log(THETA) / vectors.shape[-1])
    )
    angles = positions.astype(jnp.float32)[:, None] * frequency[None, :]
    cosine = jnp.cos(angles)[:, None, :]
    sine = jnp.sin(angles)[:, None, :]
    first = vectors[..., :half_width]
    second = vectors[..., half_width:]
    return jnp.concatenate(
        [first * cosine - second * sine, second * cosine + first * sine], axis=-1
    )


def attend(queries, keys_self, values_self, slot_lengths, rubric_keys, rubric_values):
    head_width = queries.shape[-1]
    slot_span = queries.shape[1]
    score_scale = 1.0 / math.sqrt(head_width)
    rubric_scores = (
        jnp.einsum("blhe,pe->blhp", queries, rubric_keys, preferred_element_type=jnp.float32)
        * score_scale
    )
    self_scores = (
        jnp.einsum("blhe,bke->blhk", queries, keys_self, preferred_element_type=jnp.float32)
        * score_scale
    )
    positions = jnp.arange(slot_span)
    allowed = (positions[None, :] <= positions[:, None])[None, :, None, :] & (
        positions[None, :] < slot_lengths[:, None]
    )[:, None, None, :]
    self_scores = jnp.where(allowed, self_scores, -jnp.inf)
    row_max = jnp.maximum(jnp.max(rubric_scores, axis=-1), jnp.max(self_scores, axis=-1))
    rubric_exp = jnp.exp(rubric_scores - row_max[..., None])
    self_exp = jnp.exp(self_scores - row_max[..., None])
    denominator = jnp.sum(rubric_exp, axis=-1) + jnp.sum(self_exp, axis=-1)
    rubric_weights = (rubric_exp / denominator[..., None]).astype(jnp.bfloat16)
    self_weights = (self_exp / denominator[..., None]).astype(jnp.bfloat16)
    mixed = jnp.einsum(
        "blhp,pe->blhe", rubric_weights, rubric_values, preferred_element_type=jnp.float32
    )
    mixed = mixed + jnp.einsum(
        "blhk,bke->blhe", self_weights, values_self, preferred_element_type=jnp.float32
    )
    live_rows = positions[None, :] < slot_lengths[:, None]
    mixed = jnp.where(live_rows[:, :, None, None], mixed, jnp.zeros_like(mixed))
    return mixed.reshape(queries.shape[0], slot_span, -1).astype(jnp.bfloat16)


def on_device(
    tokens, gain, w_query, b_query, w_key, b_key, w_value, b_value, rubric_cache, dest_of, lengths
):
    groups = lax.axis_size("score")
    shard_count = lax.axis_size("mp")
    group_index = lax.axis_index("score")
    resp_count = tokens.shape[0]
    owner_group = dest_of[0]
    targets = dest_of.reshape(groups, resp_count)
    lengths_all = lengths.reshape(groups, resp_count)
    own_targets = lax.dynamic_index_in_dim(targets, group_index, 0, keepdims=False)
    picker = (own_targets[None, :] == jnp.arange(groups, dtype=jnp.int32)[:, None]).astype(
        jnp.bfloat16
    )
    arrived_hit = targets == group_index
    slot_lengths = jnp.sum(jnp.where(arrived_hit, lengths_all, 0), axis=1)
    outgoing = jnp.einsum("gr,rld->gld", picker, tokens, preferred_element_type=jnp.float32).astype(
        jnp.bfloat16
    )
    arrived = lax.all_to_all(outgoing, "score", split_axis=0, concat_axis=0, tiled=True)
    slots = lax.all_gather(arrived, "mp", axis=1, tiled=True)
    wide = slots.reshape(groups * LEN_MAX, -1).astype(jnp.float32)
    normed = (
        wide * lax.rsqrt(jnp.mean(wide * wide, axis=-1, keepdims=True) + EPSILON) * gain
    ).astype(jnp.bfloat16)
    positions = PROMPT + jnp.arange(LEN_MAX, dtype=jnp.int32)
    heads_here = w_query.shape[1] // HD
    query_raw = jnp.dot(normed, w_query, preferred_element_type=jnp.float32) + b_query
    queries = rotate(query_raw.reshape(groups, LEN_MAX, heads_here, HD), positions).astype(
        jnp.bfloat16
    )
    kv_index = lax.axis_index("mp") // (shard_count // KV_HEADS)
    key_cols = lax.dynamic_slice_in_dim(w_key, kv_index * HD, HD, 1)
    key_bias = lax.dynamic_slice_in_dim(b_key, kv_index * HD, HD, 0)
    value_cols = lax.dynamic_slice_in_dim(w_value, kv_index * HD, HD, 1)
    value_bias = lax.dynamic_slice_in_dim(b_value, kv_index * HD, HD, 0)
    key_raw = jnp.dot(normed, key_cols, preferred_element_type=jnp.float32) + key_bias
    keys_self = rotate(key_raw.reshape(groups, LEN_MAX, 1, HD), positions)[:, :, 0, :].astype(
        jnp.bfloat16
    )
    value_raw = jnp.dot(normed, value_cols, preferred_element_type=jnp.float32) + value_bias
    values_self = value_raw.astype(jnp.bfloat16).reshape(groups, LEN_MAX, HD)
    local_cache = rubric_cache[0]
    everywhere = broadcast(local_cache, "score", owner_group)
    full_cache = lax.all_gather(everywhere, "mp", axis=1, tiled=True)
    head_cache = lax.dynamic_index_in_dim(full_cache, kv_index, 0, keepdims=False)
    rubric_keys = head_cache[:, :HD]
    rubric_values = head_cache[:, HD:]
    pair_count = groups // 2

    def attend_pair(members):
        return attend(members[0], members[1], members[2], members[3], rubric_keys, rubric_values)

    result = lax.map(
        attend_pair,
        (
            queries.reshape(pair_count, 2, LEN_MAX, heads_here, HD),
            keys_self.reshape(pair_count, 2, LEN_MAX, HD),
            values_self.reshape(pair_count, 2, LEN_MAX, HD),
            slot_lengths.reshape(pair_count, 2),
        ),
    )
    return result.reshape(1, groups, LEN_MAX, heads_here * HD)


def solution(mesh):
    in_specs = (
        P("score", "mp", None),
        P(),
        P(None, "mp"),
        P("mp"),
        P(),
        P(),
        P(),
        P(),
        P("score", None, "mp", None),
        P(),
        P(),
    )
    out_specs = P("score", None, None, "mp")
    return jax.shard_map(
        on_device, mesh=mesh, in_specs=in_specs, out_specs=out_specs, check_vma=False
    )
```

profile of v0, /device:TPU:1, one launch (start us, length us, event | category | flops | bytes accessed | tf_op | source)
XLA Modules:
  0.0 304.1 jit_solution(3071575133799913858)
XLA Ops:
  7.3 0.7 select_bitcast_fusion
  8.1 62.8 %all-reduce.2.cloned.1.call-done = bf16[4,128,256]{2,1,0:T(8,128)(2,1)} async-done(((bf16[4,128,256]{2,1,0:T(8,128)(2,1)}), bf16[4,128,256]{2,1,0:T(8,128)(2,1)}) %all-reduce.2.cloned.1.call-update) | async-done | bytes 262160 | tf_op jit(solution)/shard_map/psum | solution.py:20
  71.0 0.7 reshape.282
  71.7 1.7 convolution_convert_fusion
  73.4 0.3 copy.32
  73.7 18.9 %all_to_all.5 = bf16[8,16,3584]{2,1,0:T(8,128)(2,1)S(1)} all-to-all(bf16[8,16,3584]{2,1,0:T(8,128)(2,1)S(1)} %copy.32), channel_id=1, replica_groups=mesh['score'=8,'mp'=16] {'score'}, dimensions={0} | all-to-all | bytes 1835008 | tf_op jit(solution)/shard_map/all_to_all | solution.py:91
  92.6 1.4 copy.33
  94.1 0.8 dynamic_slice.38
  94.9 0.8 dynamic_slice.40
  95.7 0.1 select_reduce_fusion
  96.0 0.5 multiply_cosine_fusion
  96.5 29.3 %all-gather.5.cloned.1.call-done = bf16[4,2048,256]{2,1,0:T(8,128)(2,1)} async-done(((bf16[4,128,256]{2,1,0:T(8,128)(2,1)}), bf16[4,2048,256]{2,1,0:T(8,128)(2,1)}) %all-gather.5.cloned.1.call-update) | async-done | bytes 4194320 | tf_op jit(solution)/shard_map/all_gather | solution.py:116
  125.8 1.3 dynamic-slice_bitcast_fusion
  127.2 101.2 %all-gather.3.cloned.1.call-done = bf16[8,256,3584]{2,0,1:T(8,128)(2,1)} async-done(((bf16[8,16,3584]{2,0,1:T(8,128)(2,1)}), bf16[8,256,3584]{2,0,1:T(8,128)(2,1)}) %all-gather.3.cloned.1.call-update) | async-done | bytes 14680080 | tf_op jit(solution)/shard_map/all_gather | solution.py:92
  228.4 13.2 %multiply_reduce_fusion.1 = f32[8,256]{1,0:T(8,128)S(1)} fusion(bf16[8,256,3584]{2,0,1:T(8,128)(2,1)} %all-gather.3.cloned.1.call-done), kind=kLoop, calls=%fused_computation.39 | loop fusion | flops 22018048 | bytes 14688256 | tf_op jit(solution)/shard_map/reduce_sum | solution.py:95
  241.6 10.8 %copy_convert_fusion = f32[8,256,3584]{2,1,0:T(8,128)S(1)} fusion(bf16[8,256,3584]{2,0,1:T(8,128)(2,1)} %all-gather.3.cloned.1.call-done), kind=kLoop, calls=%fused_computation.40 | loop fusion | flops 7340032 | bytes 44040192 | tf_op jit(solution)/shard_map/convert_element_type | solution.py:93
  252.4 7.8 %fusion.27 = bf16[2048,3584]{1,0:T(8,128)(2,1)} fusion(f32[8,256,3584]{2,1,0:T(8,128)S(1)} %copy_convert_fusion, f32[3584]{0:T(1024)S(1)} %copy-done.3, f32[2048]{0:T(1024)S(1)} %bitcast.83), kind=kLoop, calls=%fused_computation.38 | loop fusion | flops 22020096 | bytes 44062720 | tf_op jit(solution)/shard_map/convert_element_type | solution.py:96
  260.2 9.0 %convolution_add_fusion.2 = f32[2048,128]{1,0:T(8,128)S(1)} fusion(bf16[2048,3584]{1,0:T(8,128)(2,1)} %fusion.27, bf16[3584,512]{1,0:T(8,128)(2,1)} %param.17, s32[]{:T(128)S(6)} %select_n.51, f32[128]{0:T(128)S(1)} %dynamic_slice.38), kind=kOutput, calls=%fused_computation.44 | convolution fusion | flops 1879310336 | bytes 16646660 | tf_op jit(solution)/shard_map/dot_general | solution.py:108
  269.2 0.6 copy-done.2
  269.9 4.0 %convolution_add_fusion.3 = f32[2048,128]{1,0:T(8,128)S(1)} fusion(bf16[2048,3584]{1,0:T(8,128)(2,1)S(1)} %copy-done.2, bf16[3584,128]{1,0:T(8,128)(2,1)S(1)} %copy-done, f32[128]{0:T(128)S(1)} %copy-done.5), kind=kOutput, calls=%fused_computation.45 | convolution fusion | flops 1879310336 | bytes 16646656 | tf_op jit(solution)/shard_map/dot_general | solution.py:99
  273.8 0.7 subtract_convert_fusion
  274.6 0.3 pad_maximum_fusion.1
  274.9 0.3 pad_maximum_fusion
  275.2 5.3 %fusion.28 = bf16[2048,128]{1,0:T(8,128)(2,1)S(1)} fusion(bf16[2048,3584]{1,0:T(8,128)(2,1)S(1)} %copy-done.2, bf16[3584,512]{1,0:T(8,128)(2,1)} %param.19, s32[]{:T(128)S(6)} %select_n.51, f32[128]{0:T(128)S(1)} %dynamic_slice.40), kind=kOutput, calls=%fused_computation.43 | convolution fusion | flops 1879572480 | bytes 16122372 | tf_op jit(solution)/shard_map/dot_general | solution.py:112
  280.5 15.7 %while.10 = (s32[]{:T(128)}, bf16[4,2,256,128]{3,2,1,0:T(8,128)(2,1)S(1)}, s32[4,2]{1,0:T(4,128)S(1)}, bf16[4,2,256,1,128]{4,2,1,3,0:T(8,128)(2,1)S(1)}, bf16[20...) while((s32[]{:T(128)}, ...), condition=%wide.region_8.9_spmd, body=%wide.region_3.8_spmd.sunk | while | flops 614858240 | bytes 16552573 | solution.py:125
  280.9 0.3 fusion.55
  281.2 0.8 multiply_reduce_fusion.3
  282.0 0.1 fusion.57
  282.1 0.8 fusion.56
  282.9 1.4 fusion.58
  284.3 0.4 fusion.59
  284.8 0.3 fusion.55
  285.0 0.8 multiply_reduce_fusion.3
  285.9 0.8 fusion.56
  286.8 1.4 fusion.58
  288.1 0.4 fusion.59
  288.6 0.3 fusion.55
  288.9 0.8 multiply_reduce_fusion.3
  289.8 0.8 fusion.56
  290.6 1.4 fusion.58
  292.0 0.4 fusion.59
  292.5 0.3 fusion.55
  292.8 0.8 multiply_reduce_fusion.3
  293.7 0.8 fusion.56
  294.5 1.4 fusion.58
  295.9 0.4 fusion.59
  296.3 0.8 copy-done.6
  297.0 0.6 copy-done.1
  (49 shorter events, 1.2 us)
Async XLA Ops:
  6.5 262.7 %copy-start = (bf16[3584,128]{1,0:T(8,128)(2,1)S(1)}, bf16[3584,128]{1,0:T(8,128)(2,1)}, u32[]{:S(2)}) copy-start(bf16[3584,128]{1,0:T(8,128)(2,1)} %param.15) | copy-start | bytes 2752516
  6.5 64.4 %all-reduce.2.cloned.1.call-start = ((), (), s32[]{:S(2)}) async-start(), calls=%async_computation.2 | async-start | bytes 524288 | tf_op jit(solution)/shard_map/psum | solution.py:20
  8.0 117.8 %all-gather.5.cloned.1.call-start = ((), (), s32[]{:S(2)}) async-start(), calls=%async_computation.3 | async-start | bytes 4456448 | tf_op jit(solution)/shard_map/all_gather | solution.py:116
  70.9 24.7 %copy-start.4 = (s32[48]{0:T(128)S(1)}, s32[48]{0:T(128)}, u32[]{:S(2)}) copy-start(s32[48]{0:T(128)} %param.23) | copy-start | bytes 580
  71.0 157.4 %all-gather.3.cloned.1.call-start = ((), (), s32[]{:S(2)}) async-start(), calls=%async_computation.1 | async-start | bytes 15597568 | tf_op jit(solution)/shard_map/all_gather | solution.py:92
  241.6 10.8 %copy-start.3 = (f32[3584]{0:T(1024)S(1)}, f32[3584]{0:T(1024)}, u32[]{:S(2)}) copy-start(f32[3584]{0:T(1024)} %param.14) | copy-start | bytes 43012
  260.2 9.6 %copy-start.2 = (bf16[2048,3584]{1,0:T(8,128)(2,1)S(1)}, bf16[2048,3584]{1,0:T(8,128)(2,1)}, u32[]{:S(2)}) copy-start(bf16[2048,3584]{1,0:T(8,128)(2,1)} %fusion.27) | copy-start | bytes 44040196
  260.2 9.6 %copy-start.5 = (f32[128]{0:T(128)S(1)}, f32[128]{0:T(128)}, u32[]{:S(2)}) copy-start(f32[128]{0:T(128)} %param.16) | copy-start | bytes 1540
  296.2 0.8 copy-start.6
  296.2 1.4 copy-start.1
Sparse Core Ops, SparseCore 0:
  9.7 61.1 all-reduce.1
  73.3 52.5 all-gather.4
  128.2 100.1 all-gather.2
where the time goes:
time: 305 us; the launch traced here: 304 us
  waiting for transfers between devices  193 us (63%)
  other arithmetic  38.6 us (13%)
  matrix products  31.1 us (10%)
  blocking collectives  18.9 us (6%)
  between operations  14 us (5%)
  local copies, waits for them, and re-layouts  7.57 us (2%)
    all_gather x1, waiting for transfers between devices, on_device(): slots = lax.all_gather(arrived, 'mp', axis=1, tiled=True)  101 us
    psum x1, waiting for transfers between devices, broadcast(): return lax.psum(block, axis)  62.8 us
    all_gather x1, waiting for transfers between devices, on_device(): full_cache = lax.all_gather(everywhere, 'mp', axis=1, tiled=True)  29.3 us
    all_to_all x1, blocking collectives, on_device(): lax.all_to_all(outgoing, 'score', split_axis=0, concat_axis=0, tiled=True)  18.9 us
    reduce_sum x1, other arithmetic, on_device(): jnp.mean(wide * wide, axis=-1, keepdims=True) + EPSILON  13.2 us
    convert_element_type x1, other arithmetic, on_device(): wide = slots.reshape(groups * LEN_MAX, -1).astype(jnp.float32)  10.8 us
    dot_general x1, matrix products, on_device(): jnp.dot(normed, key_cols, preferred_element_type=jnp.float32) + key_bias  8.96 us
    convert_element_type x1, other arithmetic, on_device(): normed = (wide * lax.rsqrt(jnp.mean(wide * wide, axis=-1, keepdims=True)...  7.78 us
  transfers between devices with their start and end apart: 3, of which 3 were waited for; matrix products, arithmetic and copies ran while one was open for 3% of the time, Pallas kernels for 0%

commit v1 on v0

v1 whole, which is shorter than its diff:
```python
import math

import jax
import jax.numpy as jnp
from jax import lax
from jax.experimental import pallas as pl
from jax.experimental.pallas import tpu as pltpu
from jax.sharding import PartitionSpec as P

D = 3584
KV_HEADS = 4
HD = 128
LEN_MAX = 256
PROMPT = 2048
RESP = 6
GROUPS = 8
HALF_D = D // 2
BIAS_ROWS = 16
CHUNK = RESP * 16
THETA = 1000000.0
EPSILON = 1e-06
SCALE = 1.0 / math.sqrt(HD)
LOG2E = math.log2(math.e)
AXES = ("score", "mp")
VMEM_LIMIT = 48 * 1024 * 1024


def device_number(x, y, z, c):
    return (z * 2 + c) * 16 + y * 4 + x


def shift(v, dx=0, dy=0, dz=0, flip=0):
    pairs = []
    for x in range(4):
        for y in range(4):
            for z in range(4):
                for c in range(2):
                    target = device_number((x + dx) % 4, (y + dy) % 4, (z + dz) % 4, c ^ flip)
                    pairs.append((device_number(x, y, z, c), target))
    return lax.ppermute(v, AXES, pairs)


X_GROUPS = [[y * 4 + x for x in range(4)] for y in range(4)]
SCORE_X_GROUPS = [[s * 16 + y * 4 + x for s in range(8) for x in range(4)] for y in range(4)]


def params():
    return pltpu.CompilerParams(vmem_limit_bytes=VMEM_LIMIT)


VMEM_SPEC = pl.BlockSpec(memory_space=pltpu.VMEM)
SMEM_SPEC = pl.BlockSpec(memory_space=pltpu.SMEM)


def norm_kernel(tokens_ref, gain_ref, out_ref):
    wide = tokens_ref[...].astype(jnp.float32)
    mean = jnp.mean(wide * wide, axis=-1, keepdims=True)
    out_ref[...] = (wide * lax.rsqrt(mean + EPSILON) * gain_ref[...]).astype(jnp.bfloat16)


def norm_rows(tokens, gain):
    return pl.pallas_call(
        norm_kernel,
        out_shape=jax.ShapeDtypeStruct((CHUNK, D), jnp.bfloat16),
        in_specs=[VMEM_SPEC, VMEM_SPEC],
        out_specs=VMEM_SPEC,
        compiler_params=params(),
        name="norm_rows",
    )(tokens, gain)


def rope(v, cos, sin):
    return v * cos + pltpu.roll(v, 64, axis=1) * sin


def chunk_y(y, j):
    return lax.rem(y + (0, 3, 1, 2)[j], 4)


def fill_rows(rows, own, before, after, far_a, far_b):
    rows[pl.ds(0, CHUNK), :] = own[...]
    rows[pl.ds(CHUNK, CHUNK), :] = before[...]
    rows[pl.ds(2 * CHUNK, CHUNK), :] = after[...]
    rows[pl.ds(3 * CHUNK, CHUNK // 2), :] = far_a[...]
    rows[pl.ds(3 * CHUNK + CHUNK // 2, CHUNK // 2), :] = far_b[...]


def kv_kernel(meta, own, before, after, far_a, far_b, wk, wv, bk, bv, cos_ref, sin_ref, out, rows):
    y = meta[0]
    fill_rows(rows, own, before, after, far_a, far_b)
    w = jnp.concatenate([wk[...], wv[...]], axis=1)
    both = jnp.dot(rows[...], w, preferred_element_type=jnp.float32)
    key_bias = bk[...]
    value_bias = bv[...]
    for j in range(4):
        base = pl.multiple_of(chunk_y(y, j) * 16, 16)
        cos = cos_ref[pl.ds(base, 16), :]
        sin = sin_ref[pl.ds(base, 16), :]
        for i in range(RESP):
            part = both[j * CHUNK + i * 16 : j * CHUNK + i * 16 + 16, :]
            key = rope(part[:, :HD] + key_bias, cos, sin).astype(jnp.bfloat16)
            value = (part[:, HD:] + value_bias).astype(jnp.bfloat16)
            out[i, pl.ds(base, 16), 0:HD] = key
            out[i, pl.ds(base, 16), HD : 2 * HD] = value


def own_keys_values(meta, chunks, w_key, w_value, b_key, b_value, cos, sin):
    whole = lambda shape: pl.BlockSpec(shape, lambda s, m: (0,) * len(shape))
    column = lambda rows: pl.BlockSpec((rows, HD), lambda s, m: (0, m[0]))
    return pl.pallas_call(
        kv_kernel,
        out_shape=jax.ShapeDtypeStruct((RESP, 64, 2 * HD), jnp.bfloat16),
        grid_spec=pltpu.PrefetchScalarGridSpec(
            num_scalar_prefetch=1,
            grid=(1,),
            in_specs=[whole(c.shape) for c in chunks]
            + [column(D), column(D), column(1), column(1), whole((64, HD)), whole((64, HD))],
            out_specs=whole((RESP, 64, 2 * HD)),
            scratch_shapes=[pltpu.VMEM((4 * CHUNK, D), jnp.bfloat16)],
        ),
        compiler_params=params(),
        name="keys_values",
    )(meta, *chunks, w_key, w_value, b_key, b_value, cos, sin)


def query_kernel(
    meta, own, before, after, far_a, far_b, w_mine, w_other, cos_ref, sin_ref, c_mine, c_other,
    q_out, acc_out, stat_out, rows,
):
    y = meta[0]
    c = meta[1]
    fill_rows(rows, own, before, after, far_a, far_b)
    mine_at = pl.multiple_of(c * HALF_D, 128)
    other_at = pl.multiple_of((1 - c) * HALF_D, 128)
    for pair in range(2):
        lo, hi = 2 * pair, 2 * pair + 1
        wm = jnp.concatenate([w_mine[lo, :HALF_D, :], w_mine[hi, :HALF_D, :]], axis=1)
        wo = jnp.concatenate([w_other[lo, :HALF_D, :], w_other[hi, :HALF_D, :]], axis=1)
        both = jnp.dot(rows[:, pl.ds(mine_at, HALF_D)], wm, preferred_element_type=jnp.float32)
        both = both + jnp.dot(rows[:, pl.ds(other_at, HALF_D)], wo, preferred_element_type=jnp.float32)
        for h in (lo, hi):
            tail = w_mine[h, HALF_D : HALF_D + BIAS_ROWS, :].astype(jnp.float32)
            bias = tail[0:1, :] + tail[1:2, :] + tail[2:3, :]
            raw = both[:, (h - lo) * HD : (h - lo + 1) * HD] + bias
            for j in range(4):
                base = pl.multiple_of(chunk_y(y, j) * 16, 16)
                cos = cos_ref[pl.ds(base, 16), :]
                sin = sin_ref[pl.ds(base, 16), :]
                for i in range(RESP):
                    part = raw[j * CHUNK + i * 16 : j * CHUNK + i * 16 + 16, :]
                    q_out[i, h, pl.ds(base, 16), :] = rope(part, cos, sin).astype(jnp.bfloat16)

    def step(i, carry):
        q = q_out[i].reshape(4 * 64, HD)
        keys = jnp.concatenate([c_mine[:, :HD], c_other[:, :HD]], axis=0)
        scores = lax.dot_general(q, keys, (((1,), (1,)), ((), ())), preferred_element_type=jnp.float32)
        top = jnp.max(scores, axis=-1, keepdims=True)
        weights = jnp.exp2(scores * (SCALE * LOG2E) - top * (SCALE * LOG2E))
        total = jnp.sum(weights, axis=-1, keepdims=True)
        values = jnp.concatenate([c_mine[:, HD:], c_other[:, HD:]], axis=0)
        acc_out[i] = jnp.dot(weights.astype(jnp.bfloat16), values, preferred_element_type=jnp.float32)
        lane = lax.broadcasted_iota(jnp.int32, (4 * 64, HD), 1)
        stat_out[i] = jnp.where(lane < 64, top, total)
        return carry

    lax.fori_loop(0, RESP, step, 0)


def rubric_part(meta, chunks, w_mine, w_other, cos, sin, c_mine, c_other):
    return pl.pallas_call(
        query_kernel,
        out_shape=(
            jax.ShapeDtypeStruct((RESP, 4, 64, HD), jnp.bfloat16),
            jax.ShapeDtypeStruct((RESP, 256, HD), jnp.float32),
            jax.ShapeDtypeStruct((RESP, 256, HD), jnp.float32),
        ),
        in_specs=[SMEM_SPEC] + [VMEM_SPEC] * 11,
        out_specs=(VMEM_SPEC, VMEM_SPEC, VMEM_SPEC),
        scratch_shapes=[pltpu.VMEM((4 * CHUNK, D), jnp.bfloat16)],
        compiler_params=params(),
        cost_estimate=pl.CostEstimate(
            flops=3_000_000_000, bytes_accessed=12_000_000, transcendentals=3_200_000
        ),
        name="rubric_part",
    )(meta, *chunks, w_mine, w_other, cos, sin, c_mine, c_other)


def self_kernel(meta, dest, lengths, q_ref, acc_ref, stat_ref, kv0, kv1, kv2, kv3, out):
    x = meta[2]
    g = meta[3]
    out[...] = jnp.zeros_like(out)
    row = lax.broadcasted_iota(jnp.int32, (256, 256), 0)
    col = lax.broadcasted_iota(jnp.int32, (256, 256), 1)
    slot_row = lax.rem(row, 64)
    row_pos = (slot_row // 16) * 64 + x * 16 + lax.rem(slot_row, 16)
    slot_col = lax.rem(col, 64)
    which = col // 64
    offset = jnp.where(which == 0, 0, jnp.where(which == 1, 3, jnp.where(which == 2, 1, 2)))
    col_x = lax.rem(x + offset, 4)
    col_pos = (slot_col // 16) * 64 + col_x * 16 + lax.rem(slot_col, 16)
    causal = col_pos <= row_pos
    one_pos = row_pos[:, 0:HD]
    for i in range(RESP):
        length = lengths[g * RESP + i]
        q = q_ref[i].reshape(256, HD)
        keys = jnp.concatenate([kv0[i, :, :HD], kv1[i, :, :HD], kv2[i, :, :HD], kv3[i, :, :HD]], axis=0)
        values = jnp.concatenate([kv0[i, :, HD:], kv1[i, :, HD:], kv2[i, :, HD:], kv3[i, :, HD:]], axis=0)
        scores = lax.dot_general(q, keys, (((1,), (1,)), ((), ())), preferred_element_type=jnp.float32)
        scores = jnp.where(causal & (col_pos < length), scores, -jnp.inf)
        far_top = stat_ref[i, :, 0:1]
        far_total = stat_ref[i, :, 64:65]
        top = jnp.maximum(jnp.max(scores, axis=-1, keepdims=True), far_top)
        weights = jnp.exp2((scores - top) * (SCALE * LOG2E))
        factor = jnp.exp2((far_top - top) * (SCALE * LOG2E))
        total = jnp.sum(weights, axis=-1, keepdims=True) + far_total * factor
        near = jnp.dot(weights.astype(jnp.bfloat16), values, preferred_element_type=jnp.float32)
        mixed = (acc_ref[i] * factor + near) / total
        mixed = jnp.where(one_pos < length, mixed, 0.0).astype(jnp.bfloat16)
        out[dest[g * RESP + i]] = mixed.reshape(4, 64, HD)


def self_part(meta, dest, lengths, q, acc, stat, parts):
    return pl.pallas_call(
        self_kernel,
        out_shape=jax.ShapeDtypeStruct((GROUPS, 4, 64, HD), jnp.bfloat16),
        in_specs=[SMEM_SPEC] * 3 + [VMEM_SPEC] * 7,
        out_specs=VMEM_SPEC,
        compiler_params=params(),
        name="self_part",
    )(meta, dest, lengths, q, acc, stat, *parts)


def on_device(
    tokens, gain, w_query, b_query, w_key, b_key, w_value, b_value, rubric_cache, dest_of, lengths
):
    g = lax.axis_index("score")
    m = lax.axis_index("mp")
    z, c = g // 2, g % 2
    y, x = m // 4, m % 4
    meta = jnp.stack([y, c, x, g]).astype(jnp.int32)

    normed = norm_rows(tokens.reshape(CHUNK, D), gain.reshape(1, D))
    before = shift(normed, dy=1)
    after = shift(normed, dy=-1)
    far_a = shift(before[: CHUNK // 2], dy=1)
    far_b = shift(after[CHUNK // 2 :], dy=-1)
    chunks = (normed, before, after, far_a, far_b)

    first = lax.reduce_precision(b_query, 8, 7)
    second = lax.reduce_precision(b_query - first, 8, 7)
    third = b_query - first - second
    tail = jnp.stack([first, second, third]).astype(jnp.bfloat16)
    tail = jnp.pad(tail, ((0, BIAS_ROWS - 3), (0, 0)))
    half = jnp.concatenate([lax.dynamic_slice_in_dim(w_query, c * HALF_D, HALF_D, 0), tail], axis=0)
    w_mine = lax.all_gather(half, "mp", axis=0, axis_index_groups=X_GROUPS)
    w_other = shift(w_mine, flip=1)

    owner = dest_of[0]
    cache = rubric_cache[0]
    swapped = shift(cache, flip=1)
    cache = jnp.where(owner % 2 == c, cache, swapped)
    piece = lax.dynamic_slice_in_dim(cache, c * 64, 64, 1)
    z_before = shift(piece, dz=1)
    z_after = shift(piece, dz=-1)
    z_far = shift(piece, dz=2)
    turn = (owner // 2 - z) % 4
    piece = jnp.where(
        turn == 0, piece, jnp.where(turn == 3, z_before, jnp.where(turn == 1, z_after, z_far))
    )
    spread = jnp.broadcast_to(piece[:, None], (4, 4, 64, 2 * HD)).reshape(16, 64, 2 * HD)
    c_mine = lax.all_to_all(spread, "mp", 0, 0, tiled=True).reshape(1024, 2 * HD)
    c_other = shift(c_mine, flip=1)

    frequency = jnp.exp(jnp.arange(64, dtype=jnp.float32) * (-2.0 * math.log(THETA) / HD))
    slot = jnp.arange(64, dtype=jnp.int32)
    positions = PROMPT + (slot // 16) * 64 + x * 16 + slot % 16
    angles = positions.astype(jnp.float32)[:, None] * frequency[None, :]
    cos = jnp.cos(angles)
    sin = jnp.sin(angles)
    cos = jnp.concatenate([cos, cos], axis=1)
    sin = jnp.concatenate([-sin, sin], axis=1)

    kv = own_keys_values(
        meta, chunks, w_key, w_value, b_key.reshape(1, -1), b_value.reshape(1, -1), cos, sin
    )
    parts = (kv, shift(kv, dx=1), shift(kv, dx=-1), shift(kv, dx=2))
    q, acc, stat = rubric_part(meta, chunks, w_mine, w_other, cos, sin, c_mine, c_other)
    ready = self_part(meta, dest_of, lengths, q, acc, stat, parts)
    arrived = lax.all_to_all(
        ready.reshape(32, 64, HD), AXES, 0, 0, tiled=True, axis_index_groups=SCORE_X_GROUPS
    )
    result = arrived.reshape(GROUPS, 4, 4, 16, HD).transpose(0, 2, 1, 3, 4)
    return result.reshape(1, GROUPS, LEN_MAX, HD)


def solution(mesh):
    in_specs = (
        P("score", "mp", None),
        P(),
        P(None, "mp"),
        P("mp"),
        P(),
        P(),
        P(),
        P(),
        P("score", None, "mp", None),
        P(),
        P(),
    )
    out_specs = P("score", None, None, "mp")
    return jax.shard_map(
        on_device, mesh=mesh, in_specs=in_specs, out_specs=out_specs, check_vma=False
    )
```

time: 305 us -> 138 us (0.45)
  waiting for transfers between devices: 193 us -> 56.6 us
  other arithmetic: 38.6 us -> 2.89 us
  matrix products: 31.1 us -> 0 us
  starting transfers between devices: 0.08 us -> 21.1 us
  Pallas kernels: 0 us -> 18.5 us
  local copies, waits for them, and re-layouts: 7.57 us -> 4.07 us
    all_gather x2 -> x1, waiting for transfers between devices: 131 us -> 32.4 us  [on_device(): w_mine = lax.all_gather(half, 'mp', axis=0, axis_index_groups=X_GROUPS)]
    psum x1 -> x0, waiting for transfers between devices: 62.8 us -> none  [broadcast(): return lax.psum(block, axis)]
    dot_general x20 -> x0, matrix products: 31.1 us -> none  [the longest x1 8.96 us: on_device(): jnp.dot(normed, key_cols, preferred_element_type=jnp.float32) + key_bias]
    convert_element_type x3 -> x1, other arithmetic: 18.6 us -> 0.01 us  [on_device(): angles = positions.astype(jnp.float32)[:, None] * frequency[None, :]]
    pallas_call x0 -> x4, Pallas kernels: none -> 18.5 us  [the longest x1 10.9 us: rubric_part(): pl.pallas_call(query_kernel, out_shape=(jax.ShapeDtypeStruct((RESP, 4, 64...]
    reduce_sum x10 -> x0, other arithmetic: 17 us -> none  [the longest x1 13.2 us: on_device(): jnp.mean(wide * wide, axis=-1, keepdims=True) + EPSILON]
    ppermute x0 -> x13, starting transfers between devices: none -> 15.9 us  [shift(): return lax.ppermute(v, AXES, pairs)]
    all_to_all x0 -> x1, waiting for transfers between devices: none -> 13.8 us  [on_device(): lax.all_to_all(spread, 'mp', 0, 0, tiled=True).reshape(1024, 2 * HD)]
  transfers between devices with their start and end apart: 3 -> 15, of which waited for: 3 -> 5; matrix products, arithmetic and copies ran while one was open for 3% -> 2% of each run, Pallas kernels for 0% -> 10%
where the time goes in v1:
time: 138 us; the launch traced here: 137 us
  waiting for transfers between devices  56.6 us (41%)
  starting transfers between devices  21.1 us (15%)
  Pallas kernels  18.5 us (13%)
  blocking collectives  18.4 us (13%)
  between operations  15.6 us (11%)
  local copies, waits for them, and re-layouts  4.07 us (3%)
  other arithmetic  2.89 us (2%)
    all_gather x1, waiting for transfers between devices, on_device(): w_mine = lax.all_gather(half, 'mp', axis=0, axis_index_groups=X_GROUPS)  32.4 us
    all_to_all x1, blocking collectives, on_device(): lax.all_to_all(ready.reshape(32, 64, HD), AXES, 0, 0, tiled=True, axis_in...  18.4 us
    ppermute x13, starting transfers between devices, shift(): return lax.ppermute(v, AXES, pairs)  15.9 us
    all_to_all x1, waiting for transfers between devices, on_device(): lax.all_to_all(spread, 'mp', 0, 0, tiled=True).reshape(1024, 2 * HD)  13.8 us
    pallas_call x1, Pallas kernels, rubric_part(): pl.pallas_call(query_kernel, out_shape=(jax.ShapeDtypeStruct((RESP, 4, 64...  10.9 us
    ppermute x13, waiting for transfers between devices, shift(): return lax.ppermute(v, AXES, pairs)  10.4 us
    all_to_all x1, starting transfers between devices, on_device(): lax.all_to_all(spread, 'mp', 0, 0, tiled=True).reshape(1024, 2 * HD)  5.24 us
    pallas_call x1, Pallas kernels, self_part(): pl.pallas_call(self_kernel, out_shape=jax.ShapeDtypeStruct((GROUPS, 4, 64...  4.27 us
  transfers between devices with their start and end apart: 15, of which 5 were waited for; matrix products, arithmetic and copies ran while one was open for 2% of the time, Pallas kernels for 10%

profile of v1, /device:TPU:1, one launch (start us, length us, event | category | flops | bytes accessed | tf_op | source)
XLA Modules:
  0.0 137.2 jit_solution(11655074303356122051)
XLA Ops:
  6.5 0.7 fusion.8
  7.3 0.4 copy-done
  7.8 0.0 copy-start.2
  7.8 0.0 copy-start.3
  7.8 0.8 pad_maximum_fusion
  8.6 0.0 all-gather.3.cloned.1.call-update
  8.6 32.4 %all-gather.3.cloned.1.call-done = bf16[7232,128]{1,0:T(8,128)(2,1)} async-done(((bf16[1808,128]{1,0:T(8,128)(2,1)}), bf16[7232,128]{1,0:T(8,128)(2,1)}) %all-gather.3.cloned.1.call-update) | async-done | bytes 1851408 | tf_op jit(solution)/shard_map/all_gather | solution.py:255
  41.1 0.7 collective-permute-start.4
  41.7 0.0 collective-permute-start.5
  43.7 1.9 %collective-permute-done.5 = bf16[4,128,256]{2,1,0:T(8,128)(2,1)S(1)} collective-permute-done((bf16[4,128,256]{2,1,0:T(8,128)(2,1)}, bf16[4,128,256]{2,1,0:T(8,128)(2,1)S(1)}, u32[]{:S(2)}, u32[]{:S(2)}) %collective-permute-start.5) | collective-permute-done | bytes 262176 | tf_op jit(solution)/shard_map/ppermute | solution.py:40
  45.6 0.9 dynamic-slice_select_fusion
  46.6 1.3 collective-permute-start.6
  47.9 1.5 %collective-permute-start.7 = (bf16[4,64,256]{2,1,0:T(8,128)(2,1)S(1)}, bf16[4,64,256]{2,1,0:T(8,128)(2,1)S(1)}, u32[]{:S(2)}, u32[]{:S(2)}) collective-permute-start(bf16[4,64,256]{2,1,0:T(8,128)(2,1)S(1)} %dynamic-slice_select_fusion), channel_id=1, source_target_pairs={{0,96},{16,112},{32,0},{48,16},{64,32},{80,48},{96,64},{112,80},{4... | collective-permute-start | bytes 393224 | tf_op jit(solution)/shard_map/ppermute | solution.py:40
  49.4 1.6 %collective-permute-start.8 = (bf16[4,64,256]{2,1,0:T(8,128)(2,1)S(1)}, bf16[4,64,256]{2,1,0:T(8,128)(2,1)S(1)}, u32[]{:S(2)}, u32[]{:S(2)}) collective-permute-start(bf16[4,64,256]{2,1,0:T(8,128)(2,1)S(1)} %dynamic-slice_select_fusion), channel_id=1, source_target_pairs={{0,64},{16,80},{32,96},{48,112},{64,0},{80,16},{96,32},{112,48},{4... | collective-permute-start | bytes 393224 | tf_op jit(solution)/shard_map/ppermute | solution.py:40
  51.0 0.7 reshape.59.gain_ref
  51.7 0.0 copy-start.1
  51.7 1.1 copy-done.1
  52.8 0.4 norm_rows.1.own
  53.2 1.3 collective-permute-start
  54.5 0.0 collective-permute-done.6
  54.6 1.5 %collective-permute-start.1 = (bf16[96,3584]{1,0:T(8,128)(2,1)S(1)}, bf16[96,3584]{1,0:T(8,128)(2,1)S(1)}, u32[]{:S(2)}, u32[]{:S(2)}) collective-permute-start(bf16[96,3584]{1,0:T(8,128)(2,1)S(1)} %norm_rows.1.own), channel_id=1, source_target_pairs={{0,12},{16,28},{32,44},{48,60},{64,76},{80,92},{96,108},{112,124},... | collective-permute-start | bytes 2064392 | tf_op jit(solution)/shard_map/ppermute | solution.py:40
  56.1 0.0 collective-permute-done.7
  56.1 0.7 collective-permute-done.8
  56.8 0.8 broadcast_in_dim.2
  57.7 5.2 %all-to-all-start = ((bf16[16,64,256]{2,1,0:T(8,128)(2,1)}), bf16[16,64,256]{2,1,0:T(8,128)(2,1)S(1)}, u32[]{:S(2)}, u32[]{:S(2)}) async-start(bf16[16,64,256]{2,1,0:T(8,128)(2,1)} %bitcast.34), calls=%async_computation | async-start | bytes 1048576 | tf_op jit(solution)/shard_map/all_to_all | solution.py:271
  62.9 13.8 %all-to-all-done = bf16[16,64,256]{2,1,0:T(8,128)(2,1)S(1)} async-done(((bf16[16,64,256]{2,1,0:T(8,128)(2,1)}), bf16[16,64,256]{2,1,0:T(8,128)(2,1)S(1)}, u32[]{:S(2)}, u32[]{:S(2)}) %all-to-all-start) | async-done | bytes 524320 | tf_op jit(solution)/shard_map/all_to_all | solution.py:271
  76.7 2.2 %collective-permute-start.9 = (bf16[1024,256]{1,0:T(8,128)(2,1)S(1)}, bf16[1024,256]{1,0:T(8,128)(2,1)S(1)}, u32[]{:S(2)}, u32[]{:S(2)}) collective-permute-start(bf16[1024,256]{1,0:T(8,128)(2,1)S(1)} %bitcast.26), channel_id=1, source_target_pairs={{0,16},{16,0},{32,48},{48,32},{64,80},{80,64},{96,112},{112,96},{4... | collective-permute-start | bytes 1572872 | tf_op jit(solution)/shard_map/ppermute | solution.py:40
  78.9 0.0 collective-permute-done.before
  78.9 0.8 collective-permute-start.2
  79.7 0.0 collective-permute-done.1.after
  79.7 2.1 %collective-permute-start.3 = (bf16[48,3584]{1,0:T(8,128)(2,1)S(1)}, bf16[48,3584]{1,0:T(8,128)(2,1)S(1)}, u32[]{:S(2)}, u32[]{:S(2)}) collective-permute-start(bf16[48,3584]{1,0:T(8,128)(2,1)S(1)} %slice.13), channel_id=1, source_target_pairs={{0,12},{16,28},{32,44},{48,60},{64,76},{80,92},{96,108},{112,124},... | collective-permute-start | bytes 1032200 | tf_op jit(solution)/shard_map/ppermute | solution.py:40
  81.8 0.1 pad_add_fusion.meta
  81.9 0.2 fusion
  82.1 0.1 pad_maximum_fusion.1
  82.2 7.8 %collective-permute-done.2.far_a = bf16[48,3584]{1,0:T(8,128)(2,1)S(1)} collective-permute-done((bf16[48,3584]{1,0:T(8,128)(2,1)S(1)}, bf16[48,3584]{1,0:T(8,128)(2,1)S(1)}, u32[]{:S(2)}, u32[]{:S(2)}) %collective-permute-start.2) | collective-permute-done | bytes 344096 | tf_op jit(solution)/shard_map/ppermute | solution.py:40
  89.9 0.0 collective-permute-done.3.far_b
  89.9 3.0 %keys_values.1.kv0 = bf16[6,64,256]{2,1,0:T(8,128)(2,1)S(1)} custom-call(s32[4]{0:T(128)S(1)} %pad_add_fusion.meta, bf16[96,3584]{1,0:T(8,128)(2,1)S(1)} %norm_rows.1.own, bf16[96,3584]{1,0:T(8,128)(2,1)S(1)} %collective-permute-done.before, bf16[96,3584]{1,0:T(8,128)(2,1)S(1)} %collective-permute-done.1.after, ...), custom_call_target="tpu_custom_call" | custom-call | tf_op jit(solution)/shard_map/keys_values/pallas_call | solution.py:110
  92.9 0.0 copy-start.5
  92.9 0.3 collective-permute-start.10
  93.2 2.5 %collective-permute-start.11 = (bf16[6,64,256]{2,1,0:T(8,128)(2,1)S(1)}, bf16[6,64,256]{2,1,0:T(8,128)(2,1)S(1)}, u32[]{:S(2)}, u32[]{:S(2)}) collective-permute-start(bf16[6,64,256]{2,1,0:T(8,128)(2,1)S(1)} %keys_values.1.kv0), channel_id=1, source_target_pairs={{0,3},{16,19},{32,35},{48,51},{64,67},{80,83},{96,99},{112,115},{4... | collective-permute-start | bytes 589832 | tf_op jit(solution)/shard_map/ppermute | solution.py:40
  95.7 0.2 collective-permute-start.12
  95.9 0.0 collective-permute-done.4.w_other
  95.9 10.9 %rubric_part.1 = (bf16[6,4,64,128]{3,2,1,0:T(8,128)(2,1)S(1)}, f32[6,256,128]{2,1,0:T(8,128)S(1)}, f32[6,256,128]{2,1,0:T(8,128)S(1)}) custom-call(s32[4]{0:T(128)S(1)} %pad_add_fusion.meta, bf16[96,3584]{1,0:T(8,128)(2,1)S(1)} %norm_rows.1.own, bf16[96,3584]{1,0:T(8,128)(2,1)S(1)} %collective-permute-done.before, ...), custom_call_target="tpu_custom_call" | custom-call | flops 3000000000 | bytes 12000000 | tf_op jit(solution)/shard_map/rubric_part/pallas_call | solution.py:170
  106.7 0.0 collective-permute-done.10.kv1
  106.8 0.0 collective-permute-done.12.kv3
  106.8 4.3 %self_part.1 = bf16[8,4,64,128]{3,2,1,0:T(8,128)(2,1)S(1)} custom-call(s32[4]{0:T(128)S(1)} %pad_add_fusion.meta, s32[48]{0:T(128)S(1)} %copy-done.4, s32[48]{0:T(128)S(1)} %copy-done.5, bf16[6,4,64,128]{3,2,1,0:T(8,128)(2,1)S(1)} %get-tuple-element.8.q_ref, f32[6,256,128]{2,1,0:T(8,128)S(1)} %get-tuple-element.9.acc_ref, ...), custom_call_target="tpu_custom_call" | custom-call | tf_op jit(solution)/shard_map/self_part/pallas_call | solution.py:223
  111.1 18.4 %all_to_all.10 = bf16[32,64,128]{2,1,0:T(8,128)(2,1)S(1)} all-to-all(bf16[32,64,128]{2,1,0:T(8,128)(2,1)S(1)} %bitcast.24), channel_id=1, replica_groups={{0,1,2,3,16,17,18,19,32,33,34,35,48,49,50,51,64,65,66,67,80,81,82,83,96..., dimensions={0} | all-to-all | bytes 1048576 | tf_op jit(solution)/shard_map/all_to_all | solution.py:289
  129.5 0.9 copy.12
  (16 shorter events, 0.2 us)
Async XLA Ops:
  6.5 1.2 copy-start
  6.5 47.9 %copy-start.4 = (s32[48]{0:T(128)S(1)}, s32[48]{0:T(128)}, u32[]{:S(2)}) copy-start(s32[48]{0:T(128)} %dest.1) | copy-start | bytes 580
  6.5 34.5 %all-gather.3.cloned.1.call-start = ((), (), s32[]{:S(2)}) async-start(), calls=%async_computation.2 | async-start | bytes 2314240 | tf_op jit(solution)/shard_map/all_gather | solution.py:255
  7.8 82.1 %copy-start.2 = (f32[512]{0:T(512)S(1)}, f32[512]{0:T(512)}, u32[]{:S(2)}) copy-start(f32[512]{0:T(512)} %param.16) | copy-start | bytes 6148
  7.8 82.1 %copy-start.3 = (f32[512]{0:T(512)S(1)}, f32[512]{0:T(512)}, u32[]{:S(2)}) copy-start(f32[512]{0:T(512)} %param.18) | copy-start | bytes 6148
  41.1 54.8 %collective-permute-start.4 = (bf16[4,1808,128]{2,1,0:T(8,128)(2,1)}, bf16[4,1808,128]{2,1,0:T(8,128)(2,1)}, u32[]{:S(2)}, u32[]{:S(2)}) collective-permute-start(bf16[4,1808,128]{2,1,0:T(8,128)(2,1)} %bitcast.38), channel_id=1, source_target_pairs={{0,16},{16,0},{32,48},{48,32},{64,80},{80,64},{96,112},{112,96},{4... | collective-permute-start | bytes 5554184 | tf_op jit(solution)/shard_map/ppermute | solution.py:40
  41.7 3.9 %collective-permute-start.5 = (bf16[4,128,256]{2,1,0:T(8,128)(2,1)}, bf16[4,128,256]{2,1,0:T(8,128)(2,1)S(1)}, u32[]{:S(2)}, u32[]{:S(2)}) collective-permute-start(bf16[4,128,256]{2,1,0:T(8,128)(2,1)} %bitcast.36), channel_id=1, source_target_pairs={{0,16},{16,0},{32,48},{48,32},{64,80},{80,64},{96,112},{112,96},{4... | collective-permute-start | bytes 786440 | tf_op jit(solution)/shard_map/ppermute | solution.py:40
  46.6 8.0 %collective-permute-start.6 = (bf16[4,64,256]{2,1,0:T(8,128)(2,1)S(1)}, bf16[4,64,256]{2,1,0:T(8,128)(2,1)S(1)}, u32[]{:S(2)}, u32[]{:S(2)}) collective-permute-start(bf16[4,64,256]{2,1,0:T(8,128)(2,1)S(1)} %dynamic-slice_select_fusion), channel_id=1, source_target_pairs={{0,32},{16,48},{32,64},{48,80},{64,96},{80,112},{96,0},{112,16},{4... | collective-permute-start | bytes 393224 | tf_op jit(solution)/shard_map/ppermute | solution.py:40
  47.9 8.2 %collective-permute-start.7 = (bf16[4,64,256]{2,1,0:T(8,128)(2,1)S(1)}, bf16[4,64,256]{2,1,0:T(8,128)(2,1)S(1)}, u32[]{:S(2)}, u32[]{:S(2)}) collective-permute-start(bf16[4,64,256]{2,1,0:T(8,128)(2,1)S(1)} %dynamic-slice_select_fusion), channel_id=1, source_target_pairs={{0,96},{16,112},{32,0},{48,16},{64,32},{80,48},{96,64},{112,80},{4... | collective-permute-start | bytes 393224 | tf_op jit(solution)/shard_map/ppermute | solution.py:40
  49.4 7.4 %collective-permute-start.8 = (bf16[4,64,256]{2,1,0:T(8,128)(2,1)S(1)}, bf16[4,64,256]{2,1,0:T(8,128)(2,1)S(1)}, u32[]{:S(2)}, u32[]{:S(2)}) collective-permute-start(bf16[4,64,256]{2,1,0:T(8,128)(2,1)S(1)} %dynamic-slice_select_fusion), channel_id=1, source_target_pairs={{0,64},{16,80},{32,96},{48,112},{64,0},{80,16},{96,32},{112,48},{4... | collective-permute-start | bytes 393224 | tf_op jit(solution)/shard_map/ppermute | solution.py:40
  51.7 1.1 copy-start.1
  53.2 25.7 %collective-permute-start = (bf16[96,3584]{1,0:T(8,128)(2,1)S(1)}, bf16[96,3584]{1,0:T(8,128)(2,1)S(1)}, u32[]{:S(2)}, u32[]{:S(2)}) collective-permute-start(bf16[96,3584]{1,0:T(8,128)(2,1)S(1)} %norm_rows.1.own), channel_id=1, source_target_pairs={{0,4},{16,20},{32,36},{48,52},{64,68},{80,84},{96,100},{112,116},{... | collective-permute-start | bytes 2064392 | tf_op jit(solution)/shard_map/ppermute | solution.py:40
  54.6 25.1 %collective-permute-start.1 = (bf16[96,3584]{1,0:T(8,128)(2,1)S(1)}, bf16[96,3584]{1,0:T(8,128)(2,1)S(1)}, u32[]{:S(2)}, u32[]{:S(2)}) collective-permute-start(bf16[96,3584]{1,0:T(8,128)(2,1)S(1)} %norm_rows.1.own), channel_id=1, source_target_pairs={{0,12},{16,28},{32,44},{48,60},{64,76},{80,92},{96,108},{112,124},... | collective-permute-start | bytes 2064392 | tf_op jit(solution)/shard_map/ppermute | solution.py:40
  57.7 19.0 %all-to-all-start = ((bf16[16,64,256]{2,1,0:T(8,128)(2,1)}), bf16[16,64,256]{2,1,0:T(8,128)(2,1)S(1)}, u32[]{:S(2)}, u32[]{:S(2)}) async-start(bf16[16,64,256]{2,1,0:T(8,128)(2,1)} %bitcast.34), calls=%async_computation | async-start | bytes 1048576 | tf_op jit(solution)/shard_map/all_to_all | solution.py:271
  76.7 19.2 %collective-permute-start.9 = (bf16[1024,256]{1,0:T(8,128)(2,1)S(1)}, bf16[1024,256]{1,0:T(8,128)(2,1)S(1)}, u32[]{:S(2)}, u32[]{:S(2)}) collective-permute-start(bf16[1024,256]{1,0:T(8,128)(2,1)S(1)} %bitcast.26), channel_id=1, source_target_pairs={{0,16},{16,0},{32,48},{48,32},{64,80},{80,64},{96,112},{112,96},{4... | collective-permute-start | bytes 1572872 | tf_op jit(solution)/shard_map/ppermute | solution.py:40
  78.9 11.0 %collective-permute-start.2 = (bf16[48,3584]{1,0:T(8,128)(2,1)S(1)}, bf16[48,3584]{1,0:T(8,128)(2,1)S(1)}, u32[]{:S(2)}, u32[]{:S(2)}) collective-permute-start(bf16[48,3584]{1,0:T(8,128)(2,1)S(1)} %slice.12), channel_id=1, source_target_pairs={{0,4},{16,20},{32,36},{48,52},{64,68},{80,84},{96,100},{112,116},{... | collective-permute-start | bytes 1032200 | tf_op jit(solution)/shard_map/ppermute | solution.py:40
  79.7 10.2 %collective-permute-start.3 = (bf16[48,3584]{1,0:T(8,128)(2,1)S(1)}, bf16[48,3584]{1,0:T(8,128)(2,1)S(1)}, u32[]{:S(2)}, u32[]{:S(2)}) collective-permute-start(bf16[48,3584]{1,0:T(8,128)(2,1)S(1)} %slice.13), channel_id=1, source_target_pairs={{0,12},{16,28},{32,44},{48,60},{64,76},{80,92},{96,108},{112,124},... | collective-permute-start | bytes 1032200 | tf_op jit(solution)/shard_map/ppermute | solution.py:40
  92.9 13.9 %copy-start.5 = (s32[48]{0:T(128)S(1)}, s32[48]{0:T(128)}, u32[]{:S(2)}) copy-start(s32[48]{0:T(128)} %lengths.1) | copy-start | bytes 580
  92.9 13.8 %collective-permute-start.10 = (bf16[6,64,256]{2,1,0:T(8,128)(2,1)S(1)}, bf16[6,64,256]{2,1,0:T(8,128)(2,1)S(1)}, u32[]{:S(2)}, u32[]{:S(2)}) collective-permute-start(bf16[6,64,256]{2,1,0:T(8,128)(2,1)S(1)} %keys_values.1.kv0), channel_id=1, source_target_pairs={{0,1},{16,17},{32,33},{48,49},{64,65},{80,81},{96,97},{112,113},{4... | collective-permute-start | bytes 589832 | tf_op jit(solution)/shard_map/ppermute | solution.py:40
  93.2 13.6 %collective-permute-start.11 = (bf16[6,64,256]{2,1,0:T(8,128)(2,1)S(1)}, bf16[6,64,256]{2,1,0:T(8,128)(2,1)S(1)}, u32[]{:S(2)}, u32[]{:S(2)}) collective-permute-start(bf16[6,64,256]{2,1,0:T(8,128)(2,1)S(1)} %keys_values.1.kv0), channel_id=1, source_target_pairs={{0,3},{16,19},{32,35},{48,51},{64,67},{80,83},{96,99},{112,115},{4... | collective-permute-start | bytes 589832 | tf_op jit(solution)/shard_map/ppermute | solution.py:40
  95.7 11.1 %collective-permute-start.12 = (bf16[6,64,256]{2,1,0:T(8,128)(2,1)S(1)}, bf16[6,64,256]{2,1,0:T(8,128)(2,1)S(1)}, u32[]{:S(2)}, u32[]{:S(2)}) collective-permute-start(bf16[6,64,256]{2,1,0:T(8,128)(2,1)S(1)} %keys_values.1.kv0), channel_id=1, source_target_pairs={{0,2},{16,18},{32,34},{48,50},{64,66},{80,82},{96,98},{112,114},{4... | collective-permute-start | bytes 589832 | tf_op jit(solution)/shard_map/ppermute | solution.py:40
Sparse Core Ops, SparseCore 0:
  9.0 31.9 all-gather.2

commit v2 on v1

--- a/solution.py
+++ b/solution.py
@@ -242,9 +242,6 @@
     normed = norm_rows(tokens.reshape(CHUNK, D), gain.reshape(1, D))
     before = shift(normed, dy=1)
     after = shift(normed, dy=-1)
-    far_a = shift(before[: CHUNK // 2], dy=1)
-    far_b = shift(after[CHUNK // 2 :], dy=-1)
-    chunks = (normed, before, after, far_a, far_b)
 
     first = lax.reduce_precision(b_query, 8, 7)
     second = lax.reduce_precision(b_query - first, 8, 7)
@@ -253,13 +250,13 @@
     tail = jnp.pad(tail, ((0, BIAS_ROWS - 3), (0, 0)))
     half = jnp.concatenate([lax.dynamic_slice_in_dim(w_query, c * HALF_D, HALF_D, 0), tail], axis=0)
     w_mine = lax.all_gather(half, "mp", axis=0, axis_index_groups=X_GROUPS)
-    w_other = shift(w_mine, flip=1)
 
     owner = dest_of[0]
     cache = rubric_cache[0]
     swapped = shift(cache, flip=1)
     cache = jnp.where(owner % 2 == c, cache, swapped)
     piece = lax.dynamic_slice_in_dim(cache, c * 64, 64, 1)
+    piece, _ = lax.optimization_barrier((piece, normed))
     z_before = shift(piece, dz=1)
     z_after = shift(piece, dz=-1)
     z_far = shift(piece, dz=2)
@@ -268,8 +265,14 @@
         turn == 0, piece, jnp.where(turn == 3, z_before, jnp.where(turn == 1, z_after, z_far))
     )
     spread = jnp.broadcast_to(piece[:, None], (4, 4, 64, 2 * HD)).reshape(16, 64, 2 * HD)
+    before_then, after_then, _ = lax.optimization_barrier((before, after, spread))
+    far_a = shift(before_then[: CHUNK // 2], dy=1)
+    far_b = shift(after_then[CHUNK // 2 :], dy=-1)
+    chunks = (normed, before, after, far_a, far_b)
     c_mine = lax.all_to_all(spread, "mp", 0, 0, tiled=True).reshape(1024, 2 * HD)
     c_other = shift(c_mine, flip=1)
+    w_mine, _, _, _ = lax.optimization_barrier((w_mine, far_a, far_b, c_mine))
+    w_other = shift(w_mine, flip=1)
 
     frequency = jnp.exp(jnp.arange(64, dtype=jnp.float32) * (-2.0 * math.log(THETA) / HD))
     slot = jnp.arange(64, dtype=jnp.int32)

time: 138 us -> 99.4 us (0.72)
  waiting for transfers between devices: 56.6 us -> 17.5 us
  starting transfers between devices: 21.1 us -> 23.8 us
  blocking collectives: 18.4 us -> 16.5 us
  between operations: 15.6 us -> 13.8 us
  local copies, waits for them, and re-layouts: 4.07 us -> 5.53 us
    all_gather x1, waiting for transfers between devices: 32.4 us -> 0.01 us  [on_device(): w_mine = lax.all_gather(half, 'mp', axis=0, axis_index_groups=X_GROUPS)]
    all_to_all x1, waiting for transfers between devices: 13.8 us -> 10.2 us  [on_device(): lax.all_to_all(spread, 'mp', 0, 0, tiled=True).reshape(1024, 2 * HD)]
    ppermute x13, waiting for transfers between devices: 10.4 us -> 7.3 us  [shift(): return lax.ppermute(v, AXES, pairs)]
    ppermute x13, starting transfers between devices: 15.9 us -> 18.5 us  [shift(): return lax.ppermute(v, AXES, pairs)]
    all_to_all x1, blocking collectives: 18.4 us -> 16.5 us  [on_device(): lax.all_to_all(ready.reshape(32, 64, HD), AXES, 0, 0, tiled=True, axis_in...]
    slice x2, local copies, waits for them, and re-layouts: 0.05 us -> 1.51 us  [the longest x1 0.76 us: on_device(): far_a = shift(before_then[:CHUNK // 2], dy=1)]
  transfers between devices with their start and end apart: 15 -> 15, of which waited for: 5 -> 4; matrix products, arithmetic and copies ran while one was open for 2% -> 4% of each run, Pallas kernels for 10% -> 15%
where the time goes in v2:
time: 99.4 us; the launch traced here: 99 us
  starting transfers between devices  23.8 us (24%)
  Pallas kernels  18.9 us (19%)
  waiting for transfers between devices  17.5 us (18%)
  blocking collectives  16.5 us (17%)
  between operations  13.8 us (14%)
  local copies, waits for them, and re-layouts  5.53 us (6%)
  other arithmetic  2.92 us (3%)
    ppermute x13, starting transfers between devices, shift(): return lax.ppermute(v, AXES, pairs)  18.5 us
    all_to_all x1, blocking collectives, on_device(): lax.all_to_all(ready.reshape(32, 64, HD), AXES, 0, 0, tiled=True, axis_in...  16.5 us
    pallas_call x1, Pallas kernels, rubric_part(): pl.pallas_call(query_kernel, out_shape=(jax.ShapeDtypeStruct((RESP, 4, 64...  11 us
    all_to_all x1, waiting for transfers between devices, on_device(): lax.all_to_all(spread, 'mp', 0, 0, tiled=True).reshape(1024, 2 * HD)  10.2 us
    ppermute x13, waiting for transfers between devices, shift(): return lax.ppermute(v, AXES, pairs)  7.3 us
    all_to_all x1, starting transfers between devices, on_device(): lax.all_to_all(spread, 'mp', 0, 0, tiled=True).reshape(1024, 2 * HD)  5.32 us
    pallas_call x1, Pallas kernels, self_part(): pl.pallas_call(self_kernel, out_shape=jax.ShapeDtypeStruct((GROUPS, 4, 64...  4.27 us
    pallas_call x1, Pallas kernels, own_keys_values(): pl.pallas_call(kv_kernel, out_shape=jax.ShapeDtypeStruct((RESP, 64, 2 * H...  3.19 us
  transfers between devices with their start and end apart: 15, of which 4 were waited for; matrix products, arithmetic and copies ran while one was open for 4% of the time, Pallas kernels for 15%

profile of v2, /device:TPU:1, one launch (start us, length us, event | category | flops | bytes accessed | tf_op | source)
XLA Modules:
  0.0 99.0 jit_solution(10608107297713272355)
XLA Ops:
  6.6 0.8 fusion.8
  7.3 0.4 copy-done
  7.8 0.0 copy-start.2
  7.8 0.0 copy-start.3
  7.8 0.8 pad_maximum_fusion
  8.6 0.0 all-gather.3.cloned.1.call-update
  8.6 1.5 %collective-permute-start.2 = (bf16[4,128,256]{2,1,0:T(8,128)(2,1)}, bf16[4,128,256]{2,1,0:T(8,128)(2,1)}, u32[]{:S(2)}, u32[]{:S(2)}) collective-permute-start(bf16[4,128,256]{2,1,0:T(8,128)(2,1)} %bitcast.36), channel_id=1, source_target_pairs={{0,16},{16,0},{32,48},{48,32},{64,80},{80,64},{96,112},{112,96},{4... | collective-permute-start | bytes 786440 | tf_op jit(solution)/shard_map/ppermute | solution.py:40
  10.1 0.7 reshape.59.gain_ref
  10.9 0.0 copy-start.1
  10.9 1.1 %copy-done.1 = bf16[6,16,3584]{2,1,0:T(8,128)(2,1)S(1)} copy-done((bf16[6,16,3584]{2,1,0:T(8,128)(2,1)S(1)}, bf16[6,16,3584]{2,1,0:T(8,128)(2,1)}, u32[]{:S(2)}) %copy-start.1) | copy-done | bytes 688152
  12.0 0.4 norm_rows.1.own
  12.4 1.4 %collective-permute-start = (bf16[96,3584]{1,0:T(8,128)(2,1)S(1)}, bf16[96,3584]{1,0:T(8,128)(2,1)S(1)}, u32[]{:S(2)}, u32[]{:S(2)}) collective-permute-start(bf16[96,3584]{1,0:T(8,128)(2,1)S(1)} %norm_rows.1.own), channel_id=1, source_target_pairs={{0,4},{16,20},{32,36},{48,52},{64,68},{80,84},{96,100},{112,116},{... | collective-permute-start | bytes 2064392 | tf_op jit(solution)/shard_map/ppermute | solution.py:40
  13.8 1.5 %collective-permute-start.1 = (bf16[96,3584]{1,0:T(8,128)(2,1)S(1)}, bf16[96,3584]{1,0:T(8,128)(2,1)S(1)}, u32[]{:S(2)}, u32[]{:S(2)}) collective-permute-start(bf16[96,3584]{1,0:T(8,128)(2,1)S(1)} %norm_rows.1.own), channel_id=1, source_target_pairs={{0,12},{16,28},{32,44},{48,60},{64,76},{80,92},{96,108},{112,124},... | collective-permute-start | bytes 2064392 | tf_op jit(solution)/shard_map/ppermute | solution.py:40
  15.5 0.0 collective-permute-done.2
  15.5 1.0 dynamic-slice_select_fusion
  16.5 1.7 %collective-permute-start.3 = (bf16[4,64,256]{2,1,0:T(8,128)(2,1)S(1)}, bf16[4,64,256]{2,1,0:T(8,128)(2,1)S(1)}, u32[]{:S(2)}, u32[]{:S(2)}) collective-permute-start(bf16[4,64,256]{2,1,0:T(8,128)(2,1)S(1)} %dynamic-slice_select_fusion), channel_id=1, source_target_pairs={{0,32},{16,48},{32,64},{48,80},{64,96},{80,112},{96,0},{112,16},{4... | collective-permute-start | bytes 393224 | tf_op jit(solution)/shard_map/ppermute | solution.py:40
  18.1 2.2 %collective-permute-start.4 = (bf16[4,64,256]{2,1,0:T(8,128)(2,1)S(1)}, bf16[4,64,256]{2,1,0:T(8,128)(2,1)S(1)}, u32[]{:S(2)}, u32[]{:S(2)}) collective-permute-start(bf16[4,64,256]{2,1,0:T(8,128)(2,1)S(1)} %dynamic-slice_select_fusion), channel_id=1, source_target_pairs={{0,96},{16,112},{32,0},{48,16},{64,32},{80,48},{96,64},{112,80},{4... | collective-permute-start | bytes 393224 | tf_op jit(solution)/shard_map/ppermute | solution.py:40
  20.3 1.2 %collective-permute-start.5 = (bf16[4,64,256]{2,1,0:T(8,128)(2,1)S(1)}, bf16[4,64,256]{2,1,0:T(8,128)(2,1)S(1)}, u32[]{:S(2)}, u32[]{:S(2)}) collective-permute-start(bf16[4,64,256]{2,1,0:T(8,128)(2,1)S(1)} %dynamic-slice_select_fusion), channel_id=1, source_target_pairs={{0,64},{16,80},{32,96},{48,112},{64,0},{80,16},{96,32},{112,48},{4... | collective-permute-start | bytes 393224 | tf_op jit(solution)/shard_map/ppermute | solution.py:40
  21.7 2.1 %collective-permute-done.3 = bf16[4,64,256]{2,1,0:T(8,128)(2,1)S(1)} collective-permute-done((bf16[4,64,256]{2,1,0:T(8,128)(2,1)S(1)}, bf16[4,64,256]{2,1,0:T(8,128)(2,1)S(1)}, u32[]{:S(2)}, u32[]{:S(2)}) %collective-permute-start.3) | collective-permute-done | bytes 131104 | tf_op jit(solution)/shard_map/ppermute | solution.py:40
  23.8 0.0 collective-permute-done.4
  23.8 3.7 %collective-permute-done.5 = bf16[4,64,256]{2,1,0:T(8,128)(2,1)S(1)} collective-permute-done((bf16[4,64,256]{2,1,0:T(8,128)(2,1)S(1)}, bf16[4,64,256]{2,1,0:T(8,128)(2,1)S(1)}, u32[]{:S(2)}, u32[]{:S(2)}) %collective-permute-start.5) | collective-permute-done | bytes 131104 | tf_op jit(solution)/shard_map/ppermute | solution.py:40
  27.5 0.8 broadcast_in_dim.2
  28.3 5.3 %all-to-all-start = ((bf16[16,64,256]{2,1,0:T(8,128)(2,1)}), bf16[16,64,256]{2,1,0:T(8,128)(2,1)S(1)}, u32[]{:S(2)}, u32[]{:S(2)}) async-start(bf16[16,64,256]{2,1,0:T(8,128)(2,1)} %bitcast.34), calls=%async_computation | async-start | bytes 1048576 | tf_op jit(solution)/shard_map/all_to_all | solution.py:272
  33.6 0.0 collective-permute-done.before
  33.6 0.8 slice.10
  34.4 1.4 %collective-permute-start.6 = (bf16[48,3584]{1,0:T(8,128)(2,1)}, bf16[48,3584]{1,0:T(8,128)(2,1)}, u32[]{:S(2)}, u32[]{:S(2)}) collective-permute-start(bf16[48,3584]{1,0:T(8,128)(2,1)} %slice.10), channel_id=1, source_target_pairs={{0,4},{16,20},{32,36},{48,52},{64,68},{80,84},{96,100},{112,116},{... | collective-permute-start | bytes 1032200 | tf_op jit(solution)/shard_map/ppermute | solution.py:40
  35.8 0.7 slice.11
  36.5 1.3 %collective-permute-start.7 = (bf16[48,3584]{1,0:T(8,128)(2,1)}, bf16[48,3584]{1,0:T(8,128)(2,1)}, u32[]{:S(2)}, u32[]{:S(2)}) collective-permute-start(bf16[48,3584]{1,0:T(8,128)(2,1)} %slice.11), channel_id=1, source_target_pairs={{0,12},{16,28},{32,44},{48,60},{64,76},{80,92},{96,108},{112,124},... | collective-permute-start | bytes 1032200 | tf_op jit(solution)/shard_map/ppermute | solution.py:40
  37.8 10.2 %all-to-all-done = bf16[16,64,256]{2,1,0:T(8,128)(2,1)S(1)} async-done(((bf16[16,64,256]{2,1,0:T(8,128)(2,1)}), bf16[16,64,256]{2,1,0:T(8,128)(2,1)S(1)}, u32[]{:S(2)}, u32[]{:S(2)}) %all-to-all-start) | async-done | bytes 524320 | tf_op jit(solution)/shard_map/all_to_all | solution.py:272
  48.0 1.5 %collective-permute-done.6.far_a = bf16[48,3584]{1,0:T(8,128)(2,1)} collective-permute-done((bf16[48,3584]{1,0:T(8,128)(2,1)}, bf16[48,3584]{1,0:T(8,128)(2,1)}, u32[]{:S(2)}, u32[]{:S(2)}) %collective-permute-start.6) | collective-permute-done | bytes 344096 | tf_op jit(solution)/shard_map/ppermute | solution.py:40
  49.6 0.0 collective-permute-done.7.far_b
  49.6 1.9 %collective-permute-start.8 = (bf16[4,1808,128]{2,1,0:T(8,128)(2,1)}, bf16[4,1808,128]{2,1,0:T(8,128)(2,1)}, u32[]{:S(2)}, u32[]{:S(2)}) collective-permute-start(bf16[4,1808,128]{2,1,0:T(8,128)(2,1)} %bitcast.38), channel_id=1, source_target_pairs={{0,16},{16,0},{32,48},{48,32},{64,80},{80,64},{96,112},{112,96},{4... | collective-permute-start | bytes 5554184 | tf_op jit(solution)/shard_map/ppermute | solution.py:40
  51.5 0.1 collective-permute-start.9
  51.6 0.1 pad_add_fusion.meta
  51.6 0.2 fusion
  51.9 0.1 pad_maximum_fusion.1
  52.0 3.2 %keys_values.1.kv0 = bf16[6,64,256]{2,1,0:T(8,128)(2,1)S(1)} custom-call(s32[4]{0:T(128)S(1)} %pad_add_fusion.meta, bf16[96,3584]{1,0:T(8,128)(2,1)S(1)} %norm_rows.1.own, bf16[96,3584]{1,0:T(8,128)(2,1)S(1)} %collective-permute-done.before, bf16[96,3584]{1,0:T(8,128)(2,1)S(1)} %collective-permute-done.1.after, ...), custom_call_target="tpu_custom_call" | custom-call | tf_op jit(solution)/shard_map/keys_values/pallas_call | solution.py:110
  55.2 0.0 copy-start.5
  55.2 1.3 %collective-permute-start.10 = (bf16[6,64,256]{2,1,0:T(8,128)(2,1)S(1)}, bf16[6,64,256]{2,1,0:T(8,128)(2,1)S(1)}, u32[]{:S(2)}, u32[]{:S(2)}) collective-permute-start(bf16[6,64,256]{2,1,0:T(8,128)(2,1)S(1)} %keys_values.1.kv0), channel_id=1, source_target_pairs={{0,1},{16,17},{32,33},{48,49},{64,65},{80,81},{96,97},{112,113},{4... | collective-permute-start | bytes 589832 | tf_op jit(solution)/shard_map/ppermute | solution.py:40
  56.4 1.5 %collective-permute-start.11 = (bf16[6,64,256]{2,1,0:T(8,128)(2,1)S(1)}, bf16[6,64,256]{2,1,0:T(8,128)(2,1)S(1)}, u32[]{:S(2)}, u32[]{:S(2)}) collective-permute-start(bf16[6,64,256]{2,1,0:T(8,128)(2,1)S(1)} %keys_values.1.kv0), channel_id=1, source_target_pairs={{0,3},{16,19},{32,35},{48,51},{64,67},{80,83},{96,99},{112,115},{4... | collective-permute-start | bytes 589832 | tf_op jit(solution)/shard_map/ppermute | solution.py:40
  57.9 1.5 %collective-permute-start.12 = (bf16[6,64,256]{2,1,0:T(8,128)(2,1)S(1)}, bf16[6,64,256]{2,1,0:T(8,128)(2,1)S(1)}, u32[]{:S(2)}, u32[]{:S(2)}) collective-permute-start(bf16[6,64,256]{2,1,0:T(8,128)(2,1)S(1)} %keys_values.1.kv0), channel_id=1, source_target_pairs={{0,2},{16,18},{32,34},{48,50},{64,66},{80,82},{96,98},{112,114},{4... | collective-permute-start | bytes 589832 | tf_op jit(solution)/shard_map/ppermute | solution.py:40
  59.4 0.0 collective-permute-done.9.c_other
  59.4 0.0 collective-permute-done.8.w_other
  59.4 11.0 %rubric_part.1 = (bf16[6,4,64,128]{3,2,1,0:T(8,128)(2,1)S(1)}, f32[6,256,128]{2,1,0:T(8,128)S(1)}, f32[6,256,128]{2,1,0:T(8,128)S(1)}) custom-call(s32[4]{0:T(128)S(1)} %pad_add_fusion.meta, bf16[96,3584]{1,0:T(8,128)(2,1)S(1)} %norm_rows.1.own, bf16[96,3584]{1,0:T(8,128)(2,1)S(1)} %collective-permute-done.before, ...), custom_call_target="tpu_custom_call" | custom-call | flops 3000000000 | bytes 12000000 | tf_op jit(solution)/shard_map/rubric_part/pallas_call | solution.py:170
  70.4 0.0 collective-permute-done.10.kv1
  70.5 4.3 %self_part.1 = bf16[8,4,64,128]{3,2,1,0:T(8,128)(2,1)S(1)} custom-call(s32[4]{0:T(128)S(1)} %pad_add_fusion.meta, s32[48]{0:T(128)S(1)} %copy-done.4, s32[48]{0:T(128)S(1)} %copy-done.5, bf16[6,4,64,128]{3,2,1,0:T(8,128)(2,1)S(1)} %get-tuple-element.16.q_ref, f32[6,256,128]{2,1,0:T(8,128)S(1)} %get-tuple-element.17.acc_ref, ...), custom_call_target="tpu_custom_call" | custom-call | tf_op jit(solution)/shard_map/self_part/pallas_call | solution.py:223
  74.8 16.5 %all_to_all.10 = bf16[32,64,128]{2,1,0:T(8,128)(2,1)S(1)} all-to-all(bf16[32,64,128]{2,1,0:T(8,128)(2,1)S(1)} %bitcast.24), channel_id=1, replica_groups={{0,1,2,3,16,17,18,19,32,33,34,35,48,49,50,51,64,65,66,67,80,81,82,83,96..., dimensions={0} | all-to-all | bytes 1048576 | tf_op jit(solution)/shard_map/all_to_all | solution.py:292
  91.3 0.9 copy.12
  (18 shorter events, 0.1 us)
Async XLA Ops:
  6.5 1.2 %copy-start = (bf16[3584,128]{1,0:T(8,128)(2,1)S(1)}, bf16[3584,128]{1,0:T(8,128)(2,1)}, u32[]{:S(2)}) copy-start(bf16[3584,128]{1,0:T(8,128)(2,1)} %param.13) | copy-start | bytes 2752516
  6.5 9.0 %copy-start.6 = (bf16[1,4,128,256]{3,2,1,0:T(8,128)(2,1)S(1)}, bf16[1,4,128,256]{3,2,1,0:T(8,128)(2,1)}, u32[]{:S(2)}) copy-start(bf16[1,4,128,256]{3,2,1,0:T(8,128)(2,1)} %param.19) | copy-start | bytes 786436
  6.5 8.8 %copy-start.4 = (s32[48]{0:T(128)S(1)}, s32[48]{0:T(128)}, u32[]{:S(2)}) copy-start(s32[48]{0:T(128)} %dest.1) | copy-start | bytes 580
  6.5 43.0 %all-gather.3.cloned.1.call-start = ((), (), s32[]{:S(2)}) async-start(), calls=%async_computation.2 | async-start | bytes 2314240 | tf_op jit(solution)/shard_map/all_gather | solution.py:252
  7.8 44.1 %copy-start.2 = (f32[512]{0:T(512)S(1)}, f32[512]{0:T(512)}, u32[]{:S(2)}) copy-start(f32[512]{0:T(512)} %param.16) | copy-start | bytes 6148
  7.8 44.1 %copy-start.3 = (f32[512]{0:T(512)S(1)}, f32[512]{0:T(512)}, u32[]{:S(2)}) copy-start(f32[512]{0:T(512)} %param.18) | copy-start | bytes 6148
  8.6 6.8 %collective-permute-start.2 = (bf16[4,128,256]{2,1,0:T(8,128)(2,1)}, bf16[4,128,256]{2,1,0:T(8,128)(2,1)}, u32[]{:S(2)}, u32[]{:S(2)}) collective-permute-start(bf16[4,128,256]{2,1,0:T(8,128)(2,1)} %bitcast.36), channel_id=1, source_target_pairs={{0,16},{16,0},{32,48},{48,32},{64,80},{80,64},{96,112},{112,96},{4... | collective-permute-start | bytes 786440 | tf_op jit(solution)/shard_map/ppermute | solution.py:40
  10.9 1.1 %copy-start.1 = (bf16[6,16,3584]{2,1,0:T(8,128)(2,1)S(1)}, bf16[6,16,3584]{2,1,0:T(8,128)(2,1)}, u32[]{:S(2)}) copy-start(bf16[6,16,3584]{2,1,0:T(8,128)(2,1)} %param.11) | copy-start | bytes 2064388
  12.4 21.3 %collective-permute-start = (bf16[96,3584]{1,0:T(8,128)(2,1)S(1)}, bf16[96,3584]{1,0:T(8,128)(2,1)S(1)}, u32[]{:S(2)}, u32[]{:S(2)}) collective-permute-start(bf16[96,3584]{1,0:T(8,128)(2,1)S(1)} %norm_rows.1.own), channel_id=1, source_target_pairs={{0,4},{16,20},{32,36},{48,52},{64,68},{80,84},{96,100},{112,116},{... | collective-permute-start | bytes 2064392 | tf_op jit(solution)/shard_map/ppermute | solution.py:40
  13.8 19.8 %collective-permute-start.1 = (bf16[96,3584]{1,0:T(8,128)(2,1)S(1)}, bf16[96,3584]{1,0:T(8,128)(2,1)S(1)}, u32[]{:S(2)}, u32[]{:S(2)}) collective-permute-start(bf16[96,3584]{1,0:T(8,128)(2,1)S(1)} %norm_rows.1.own), channel_id=1, source_target_pairs={{0,12},{16,28},{32,44},{48,60},{64,76},{80,92},{96,108},{112,124},... | collective-permute-start | bytes 2064392 | tf_op jit(solution)/shard_map/ppermute | solution.py:40
  16.5 7.3 %collective-permute-start.3 = (bf16[4,64,256]{2,1,0:T(8,128)(2,1)S(1)}, bf16[4,64,256]{2,1,0:T(8,128)(2,1)S(1)}, u32[]{:S(2)}, u32[]{:S(2)}) collective-permute-start(bf16[4,64,256]{2,1,0:T(8,128)(2,1)S(1)} %dynamic-slice_select_fusion), channel_id=1, source_target_pairs={{0,32},{16,48},{32,64},{48,80},{64,96},{80,112},{96,0},{112,16},{4... | collective-permute-start | bytes 393224 | tf_op jit(solution)/shard_map/ppermute | solution.py:40
  18.1 5.6 %collective-permute-start.4 = (bf16[4,64,256]{2,1,0:T(8,128)(2,1)S(1)}, bf16[4,64,256]{2,1,0:T(8,128)(2,1)S(1)}, u32[]{:S(2)}, u32[]{:S(2)}) collective-permute-start(bf16[4,64,256]{2,1,0:T(8,128)(2,1)S(1)} %dynamic-slice_select_fusion), channel_id=1, source_target_pairs={{0,96},{16,112},{32,0},{48,16},{64,32},{80,48},{96,64},{112,80},{4... | collective-permute-start | bytes 393224 | tf_op jit(solution)/shard_map/ppermute | solution.py:40
  20.3 7.1 %collective-permute-start.5 = (bf16[4,64,256]{2,1,0:T(8,128)(2,1)S(1)}, bf16[4,64,256]{2,1,0:T(8,128)(2,1)S(1)}, u32[]{:S(2)}, u32[]{:S(2)}) collective-permute-start(bf16[4,64,256]{2,1,0:T(8,128)(2,1)S(1)} %dynamic-slice_select_fusion), channel_id=1, source_target_pairs={{0,64},{16,80},{32,96},{48,112},{64,0},{80,16},{96,32},{112,48},{4... | collective-permute-start | bytes 393224 | tf_op jit(solution)/shard_map/ppermute | solution.py:40
  28.3 19.7 %all-to-all-start = ((bf16[16,64,256]{2,1,0:T(8,128)(2,1)}), bf16[16,64,256]{2,1,0:T(8,128)(2,1)S(1)}, u32[]{:S(2)}, u32[]{:S(2)}) async-start(bf16[16,64,256]{2,1,0:T(8,128)(2,1)} %bitcast.34), calls=%async_computation | async-start | bytes 1048576 | tf_op jit(solution)/shard_map/all_to_all | solution.py:272
  34.4 15.1 %collective-permute-start.6 = (bf16[48,3584]{1,0:T(8,128)(2,1)}, bf16[48,3584]{1,0:T(8,128)(2,1)}, u32[]{:S(2)}, u32[]{:S(2)}) collective-permute-start(bf16[48,3584]{1,0:T(8,128)(2,1)} %slice.10), channel_id=1, source_target_pairs={{0,4},{16,20},{32,36},{48,52},{64,68},{80,84},{96,100},{112,116},{... | collective-permute-start | bytes 1032200 | tf_op jit(solution)/shard_map/ppermute | solution.py:40
  36.5 13.0 %collective-permute-start.7 = (bf16[48,3584]{1,0:T(8,128)(2,1)}, bf16[48,3584]{1,0:T(8,128)(2,1)}, u32[]{:S(2)}, u32[]{:S(2)}) collective-permute-start(bf16[48,3584]{1,0:T(8,128)(2,1)} %slice.11), channel_id=1, source_target_pairs={{0,12},{16,28},{32,44},{48,60},{64,76},{80,92},{96,108},{112,124},... | collective-permute-start | bytes 1032200 | tf_op jit(solution)/shard_map/ppermute | solution.py:40
  49.6 9.8 %collective-permute-start.8 = (bf16[4,1808,128]{2,1,0:T(8,128)(2,1)}, bf16[4,1808,128]{2,1,0:T(8,128)(2,1)}, u32[]{:S(2)}, u32[]{:S(2)}) collective-permute-start(bf16[4,1808,128]{2,1,0:T(8,128)(2,1)} %bitcast.38), channel_id=1, source_target_pairs={{0,16},{16,0},{32,48},{48,32},{64,80},{80,64},{96,112},{112,96},{4... | collective-permute-start | bytes 5554184 | tf_op jit(solution)/shard_map/ppermute | solution.py:40
  51.5 7.9 %collective-permute-start.9 = (bf16[1024,256]{1,0:T(8,128)(2,1)S(1)}, bf16[1024,256]{1,0:T(8,128)(2,1)S(1)}, u32[]{:S(2)}, u32[]{:S(2)}) collective-permute-start(bf16[1024,256]{1,0:T(8,128)(2,1)S(1)} %bitcast.26), channel_id=1, source_target_pairs={{0,16},{16,0},{32,48},{48,32},{64,80},{80,64},{96,112},{112,96},{4... | collective-permute-start | bytes 1572872 | tf_op jit(solution)/shard_map/ppermute | solution.py:40
  55.2 15.3 %copy-start.5 = (s32[48]{0:T(128)S(1)}, s32[48]{0:T(128)}, u32[]{:S(2)}) copy-start(s32[48]{0:T(128)} %lengths.1) | copy-start | bytes 580
  55.2 15.3 %collective-permute-start.10 = (bf16[6,64,256]{2,1,0:T(8,128)(2,1)S(1)}, bf16[6,64,256]{2,1,0:T(8,128)(2,1)S(1)}, u32[]{:S(2)}, u32[]{:S(2)}) collective-permute-start(bf16[6,64,256]{2,1,0:T(8,128)(2,1)S(1)} %keys_values.1.kv0), channel_id=1, source_target_pairs={{0,1},{16,17},{32,33},{48,49},{64,65},{80,81},{96,97},{112,113},{4... | collective-permute-start | bytes 589832 | tf_op jit(solution)/shard_map/ppermute | solution.py:40
  56.4 14.0 %collective-permute-start.11 = (bf16[6,64,256]{2,1,0:T(8,128)(2,1)S(1)}, bf16[6,64,256]{2,1,0:T(8,128)(2,1)S(1)}, u32[]{:S(2)}, u32[]{:S(2)}) collective-permute-start(bf16[6,64,256]{2,1,0:T(8,128)(2,1)S(1)} %keys_values.1.kv0), channel_id=1, source_target_pairs={{0,3},{16,19},{32,35},{48,51},{64,67},{80,83},{96,99},{112,115},{4... | collective-permute-start | bytes 589832 | tf_op jit(solution)/shard_map/ppermute | solution.py:40
  57.9 12.5 %collective-permute-start.12 = (bf16[6,64,256]{2,1,0:T(8,128)(2,1)S(1)}, bf16[6,64,256]{2,1,0:T(8,128)(2,1)S(1)}, u32[]{:S(2)}, u32[]{:S(2)}) collective-permute-start(bf16[6,64,256]{2,1,0:T(8,128)(2,1)S(1)} %keys_values.1.kv0), channel_id=1, source_target_pairs={{0,2},{16,18},{32,34},{48,50},{64,66},{80,82},{96,98},{112,114},{4... | collective-permute-start | bytes 589832 | tf_op jit(solution)/shard_map/ppermute | solution.py:40
Sparse Core Ops, SparseCore 0:
  9.0 36.5 all-gather.2

commit v3 on v1

v3 whole, which is shorter than its diff:
```python
import math

import jax
import jax.numpy as jnp
from jax import lax
from jax.experimental import pallas as pl
from jax.experimental.pallas import tpu as pltpu
from jax.sharding import PartitionSpec as P

D = 3584
KV_HEADS = 4
HD = 128
LEN_MAX = 256
PROMPT = 2048
RESP = 6
GROUPS = 8
HALF_D = D // 2
BIAS_ROWS = 16
CHUNK = RESP * 16
THETA = 1000000.0
EPSILON = 1e-06
SCALE = 1.0 / math.sqrt(HD)
LIMIT = 36
LOG2E = math.log2(math.e)
AXES = ("score", "mp")


def device_number(x, y, z, c):
    return (z * 2 + c) * 16 + y * 4 + x


def shift(v, dx=0, dy=0, dz=0, flip=0):
    pairs = []
    for x in range(4):
        for y in range(4):
            for z in range(4):
                for c in range(2):
                    target = device_number((x + dx) % 4, (y + dy) % 4, (z + dz) % 4, c ^ flip)
                    pairs.append((device_number(x, y, z, c), target))
    return lax.ppermute(v, AXES, pairs)


def exchange_z(v, bit):
    pairs = []
    for x in range(4):
        for y in range(4):
            for z in range(4):
                for c in range(2):
                    pairs.append((device_number(x, y, z, c), device_number(x, y, z ^ bit, c)))
    return lax.ppermute(v, AXES, pairs)


SCORE_X_GROUPS = [[s * 16 + y * 4 + x for s in range(8) for x in range(4)] for y in range(4)]


def params(mib):
    return pltpu.CompilerParams(vmem_limit_bytes=mib * 1024 * 1024)


VMEM_SPEC = pl.BlockSpec(memory_space=pltpu.VMEM)
SMEM_SPEC = pl.BlockSpec(memory_space=pltpu.SMEM)


def rope(v, cos, sin):
    return v * cos + pltpu.roll(v, 64, axis=1) * sin


TURNS = (0, 3, 1, 2)


def chunk_y(y, j):
    return lax.rem(y + TURNS[j], 4)


def norm(tokens, gain):
    wide = tokens.astype(jnp.float32)
    mean = jnp.mean(wide * wide, axis=-1, keepdims=True)
    return (wide * lax.rsqrt(mean + EPSILON) * gain).astype(jnp.bfloat16)


def table(ref, y):
    base = pl.multiple_of(y * 16, 16)
    return base, ref[pl.ds(base, 16), :]


def project(y, rows, chunk_ids, wk, wv, bk, bv, cos_ref, sin_ref, out):
    w = jnp.concatenate([wk[...], wv[...]], axis=1)
    both = jnp.dot(rows, w, preferred_element_type=jnp.float32)
    at = pl.multiple_of(y * HD, HD)
    key = both[:, :HD] + bk[:, pl.ds(at, HD)]
    value = (both[:, HD:] + bv[:, pl.ds(at, HD)]).astype(jnp.bfloat16)
    for n, j in enumerate(chunk_ids):
        base, cos = table(cos_ref, chunk_y(y, j))
        ignored, sin = table(sin_ref, chunk_y(y, j))
        for i in range(RESP):
            part = slice(n * CHUNK + i * 16, n * CHUNK + i * 16 + 16)
            out[i, pl.ds(base, 16), 0:HD] = rope(key[part], cos, sin).astype(jnp.bfloat16)
            out[i, pl.ds(base, 16), HD : 2 * HD] = value[part]


def own_kernel(own, gain, rows):
    rows[...] = norm(own[...], gain[...])


def near_kernel(meta, own, before, after, gain, wk, wv, bk, bv, cos_ref, sin_ref, out, rows):
    out[...] = jnp.zeros_like(out)
    rows[0:CHUNK, :] = own[...]
    rows[CHUNK : 2 * CHUNK, :] = norm(before[...], gain[...])
    rows[2 * CHUNK : 3 * CHUNK, :] = norm(after[...], gain[...])
    project(meta[0], rows[...], (0, 1, 2), wk, wv, bk, bv, cos_ref, sin_ref, out)


def far_kernel(meta, near, far_a, far_b, gain, wk, wv, bk, bv, cos_ref, sin_ref, out, rows):
    out[...] = near[...]
    rows[0 : CHUNK // 2, :] = norm(far_a[...], gain[...])
    rows[CHUNK // 2 : CHUNK, :] = norm(far_b[...], gain[...])
    project(meta[0], rows[...], (3,), wk, wv, bk, bv, cos_ref, sin_ref, out)


def norm_own(own, gain):
    return pl.pallas_call(
        own_kernel,
        out_shape=jax.ShapeDtypeStruct((CHUNK, D), jnp.bfloat16),
        in_specs=[VMEM_SPEC] * 2,
        out_specs=VMEM_SPEC,
        compiler_params=params(LIMIT),
        name="own_rows",
    )(own, gain)


def keys_values(kernel, name, count, meta, chunks, small):
    return pl.pallas_call(
        kernel,
        out_shape=(
            jax.ShapeDtypeStruct((RESP, 64, 2 * HD), jnp.bfloat16),
            jax.ShapeDtypeStruct((count, D), jnp.bfloat16),
        ),
        in_specs=[SMEM_SPEC] + [VMEM_SPEC] * (len(chunks) + len(small)),
        out_specs=(VMEM_SPEC, VMEM_SPEC),
        compiler_params=params(LIMIT),
        name=name,
    )(meta, *chunks, *small)


def query_kernel(
    meta, near, far, w_own, b_own, m1, m2, m3, o1, o2, o3, cos_ref, sin_ref, q_out, rows
):
    y, c, x = meta[0], meta[1], meta[2]
    rows[0 : 3 * CHUNK, :] = near[...]
    rows[3 * CHUNK : 4 * CHUNK, :] = far[...]
    mine_at = pl.multiple_of(c * HALF_D, 128)
    other_at = pl.multiple_of((1 - c) * HALF_D, 128)

    def bias(ref):
        tail = ref[HALF_D : HALF_D + BIAS_ROWS, :].astype(jnp.float32)
        return tail[0:1, :] + tail[1:2, :] + tail[2:3, :]

    mine = [w_own[pl.ds(mine_at, HALF_D), :]] + [ref[:HALF_D, :] for ref in (m1, m2, m3)]
    other = [w_own[pl.ds(other_at, HALF_D), :]] + [ref[:HALF_D, :] for ref in (o1, o2, o3)]
    biases = [b_own[...], bias(m1), bias(m2), bias(m3)]
    for lo in (0, 2):
        first = jnp.concatenate(mine[lo : lo + 2], axis=1)
        second = jnp.concatenate(other[lo : lo + 2], axis=1)
        both = jnp.dot(rows[:, pl.ds(mine_at, HALF_D)], first, preferred_element_type=jnp.float32)
        both = both + jnp.dot(
            rows[:, pl.ds(other_at, HALF_D)], second, preferred_element_type=jnp.float32
        )
        for n in (lo, lo + 1):
            head = lax.rem(x + TURNS[n], 4)
            raw = both[:, (n - lo) * HD : (n - lo + 1) * HD] + biases[n]
            for j in range(4):
                base, cos = table(cos_ref, chunk_y(y, j))
                ignored, sin = table(sin_ref, chunk_y(y, j))
                for i in range(RESP):
                    part = raw[j * CHUNK + i * 16 : j * CHUNK + i * 16 + 16, :]
                    q_out[i, head, pl.ds(base, 16), :] = rope(part, cos, sin).astype(jnp.bfloat16)


def make_queries(meta, near, far, w_own, b_own, mine, other, cos, sin):
    return pl.pallas_call(
        query_kernel,
        out_shape=jax.ShapeDtypeStruct((RESP, 4, 64, HD), jnp.bfloat16),
        in_specs=[SMEM_SPEC] + [VMEM_SPEC] * 12,
        out_specs=VMEM_SPEC,
        scratch_shapes=[pltpu.VMEM((4 * CHUNK, D), jnp.bfloat16)],
        compiler_params=params(LIMIT),
        name="queries",
    )(meta, near, far, w_own, b_own, *mine, *other, cos, sin)


def rubric_kernel(q_ref, c_mine, c_other, acc_out, stat_out):
    def step(i, carry):
        q = q_ref[i].reshape(4 * 64, HD)
        keys = jnp.concatenate([c_mine[:, :HD], c_other[:, :HD]], axis=0)
        scores = lax.dot_general(q, keys, (((1,), (1,)), ((), ())), preferred_element_type=jnp.float32)
        top = jnp.max(scores, axis=-1, keepdims=True)
        weights = jnp.exp2(scores * (SCALE * LOG2E) - top * (SCALE * LOG2E))
        total = jnp.sum(weights, axis=-1, keepdims=True)
        values = jnp.concatenate([c_mine[:, HD:], c_other[:, HD:]], axis=0)
        acc_out[i] = jnp.dot(weights.astype(jnp.bfloat16), values, preferred_element_type=jnp.float32)
        lane = lax.broadcasted_iota(jnp.int32, (4 * 64, HD), 1)
        stat_out[i] = jnp.where(lane < 64, top, total)
        return carry

    lax.fori_loop(0, RESP, step, 0)


def rubric_part(q, c_mine, c_other):
    return pl.pallas_call(
        rubric_kernel,
        out_shape=(
            jax.ShapeDtypeStruct((RESP, 256, HD), jnp.float32),
            jax.ShapeDtypeStruct((RESP, 256, HD), jnp.float32),
        ),
        in_specs=[VMEM_SPEC] * 3,
        out_specs=(VMEM_SPEC, VMEM_SPEC),
        compiler_params=params(LIMIT),
        name="rubric_part",
    )(q, c_mine, c_other)


def self_kernel(meta, dest, lengths, q_ref, acc_ref, stat_ref, kv0, kv1, kv2, kv3, out):
    x = meta[2]
    g = meta[3]
    out[...] = jnp.zeros_like(out)
    row = lax.broadcasted_iota(jnp.int32, (256, 256), 0)
    col = lax.broadcasted_iota(jnp.int32, (256, 256), 1)
    slot_row = lax.rem(row, 64)
    row_pos = (slot_row // 16) * 64 + x * 16 + lax.rem(slot_row, 16)
    slot_col = lax.rem(col, 64)
    which = col // 64
    offset = jnp.where(which == 0, 0, jnp.where(which == 1, 3, jnp.where(which == 2, 1, 2)))
    col_x = lax.rem(x + offset, 4)
    col_pos = (slot_col // 16) * 64 + col_x * 16 + lax.rem(slot_col, 16)
    causal = col_pos <= row_pos
    one_pos = row_pos[:, 0:HD]
    for i in range(RESP):
        length = lengths[g * RESP + i]
        q = q_ref[i].reshape(256, HD)
        keys = jnp.concatenate([kv0[i, :, :HD], kv1[i, :, :HD], kv2[i, :, :HD], kv3[i, :, :HD]], axis=0)
        values = jnp.concatenate([kv0[i, :, HD:], kv1[i, :, HD:], kv2[i, :, HD:], kv3[i, :, HD:]], axis=0)
        scores = lax.dot_general(q, keys, (((1,), (1,)), ((), ())), preferred_element_type=jnp.float32)
        scores = jnp.where(causal & (col_pos < length), scores, -jnp.inf)
        far_top = stat_ref[i, :, 0:1]
        far_total = stat_ref[i, :, 64:65]
        top = jnp.maximum(jnp.max(scores, axis=-1, keepdims=True), far_top)
        weights = jnp.exp2((scores - top) * (SCALE * LOG2E))
        factor = jnp.exp2((far_top - top) * (SCALE * LOG2E))
        total = jnp.sum(weights, axis=-1, keepdims=True) + far_total * factor
        near = jnp.dot(weights.astype(jnp.bfloat16), values, preferred_element_type=jnp.float32)
        mixed = (acc_ref[i] * factor + near) / total
        mixed = jnp.where(one_pos < length, mixed, 0.0).astype(jnp.bfloat16)
        out[dest[g * RESP + i]] = mixed.reshape(4, 64, HD)


def self_part(meta, dest, lengths, q, acc, stat, parts):
    return pl.pallas_call(
        self_kernel,
        out_shape=jax.ShapeDtypeStruct((GROUPS, 4, 64, HD), jnp.bfloat16),
        in_specs=[SMEM_SPEC] * 3 + [VMEM_SPEC] * 7,
        out_specs=VMEM_SPEC,
        compiler_params=params(LIMIT),
        name="self_part",
    )(meta, dest, lengths, q, acc, stat, *parts)


def on_device(
    tokens, gain, w_query, b_query, w_key, b_key, w_value, b_value, rubric_cache, dest_of, lengths
):
    g = lax.axis_index("score")
    m = lax.axis_index("mp")
    z, c = g // 2, g % 2
    y, x = m // 4, m % 4
    meta = jnp.stack([y, c, x, g]).astype(jnp.int32)

    own = tokens.reshape(CHUNK, D)
    gain = gain.reshape(1, D)
    before = shift(own, dy=1)
    after = shift(own, dy=-1)
    far_a = shift(before[: CHUNK // 2], dy=1)
    far_b = shift(after[CHUNK // 2 :], dy=-1)

    frequency = jnp.exp(jnp.arange(64, dtype=jnp.float32) * (-2.0 * math.log(THETA) / HD))
    slot = jnp.arange(64, dtype=jnp.int32)
    positions = PROMPT + (slot // 16) * 64 + x * 16 + slot % 16
    angles = positions.astype(jnp.float32)[:, None] * frequency[None, :]
    cos = jnp.cos(angles)
    sin = jnp.sin(angles)
    cos = jnp.concatenate([cos, cos], axis=1)
    sin = jnp.concatenate([-sin, sin], axis=1)

    wk = lax.dynamic_slice_in_dim(w_key, y * HD, HD, 1)
    wv = lax.dynamic_slice_in_dim(w_value, y * HD, HD, 1)
    small = (gain, wk, wv, b_key.reshape(1, -1), b_value.reshape(1, -1), cos, sin)
    own_rows = norm_own(own, gain)

    first = lax.reduce_precision(b_query, 8, 7)
    second = lax.reduce_precision(b_query - first, 8, 7)
    third = b_query - first - second
    tail = jnp.stack([first, second, third]).astype(jnp.bfloat16)
    tail = jnp.pad(tail, ((0, BIAS_ROWS - 3), (0, 0)))
    half = jnp.concatenate([lax.dynamic_slice_in_dim(w_query, c * HALF_D, HALF_D, 0), tail], axis=0)
    mine = (shift(half, dx=1), shift(half, dx=-1), shift(half, dx=2))
    other = tuple(shift(v, flip=1) for v in mine)

    owner = dest_of[0]
    cache = rubric_cache[0]
    swapped = shift(cache, flip=1)
    cache = jnp.where(owner % 2 == c, cache, swapped)
    piece = lax.dynamic_slice_in_dim(cache, c * 64, 64, 1)
    for bit in (1, 2):
        across = exchange_z(piece, bit)
        same = (owner // 2 & bit) == (z & bit)
        piece = jnp.where(same, piece, across)
    spread = jnp.broadcast_to(piece[:, None], (4, 4, 64, 2 * HD)).reshape(16, 64, 2 * HD)
    c_mine = lax.all_to_all(spread, "mp", 0, 0, tiled=True).reshape(1024, 2 * HD)

    kv, near_rows = keys_values(
        near_kernel, "near_rows", 3 * CHUNK, meta, (own_rows, before, after), small
    )
    c_mine, _ = lax.optimization_barrier((c_mine, near_rows))
    c_other = shift(c_mine, flip=1)
    kv, far_rows = keys_values(far_kernel, "far_rows", CHUNK, meta, (kv, far_a, far_b), small)
    parts = (kv, shift(kv, dx=1), shift(kv, dx=-1), shift(kv, dx=2))
    q = make_queries(
        meta, near_rows, far_rows, w_query, b_query.reshape(1, HD), mine, other, cos, sin
    )
    acc, stat = rubric_part(q, c_mine, c_other)
    ready = self_part(meta, dest_of, lengths, q, acc, stat, parts)
    arrived = lax.all_to_all(
        ready.reshape(32, 64, HD), AXES, 0, 0, tiled=True, axis_index_groups=SCORE_X_GROUPS
    )
    result = arrived.reshape(GROUPS, 4, 4, 16, HD).transpose(0, 2, 1, 3, 4)
    return result.reshape(1, GROUPS, LEN_MAX, HD)


def solution(mesh):
    in_specs = (
        P("score", "mp", None),
        P(),
        P(None, "mp"),
        P("mp"),
        P(),
        P(),
        P(),
        P(),
        P("score", None, "mp", None),
        P(),
        P(),
    )
    out_specs = P("score", None, None, "mp")
    return jax.shard_map(
        on_device, mesh=mesh, in_specs=in_specs, out_specs=out_specs, check_vma=False
    )
```

time: 138 us -> 93.2 us (0.68)
  waiting for transfers between devices: 56.6 us -> 3 us
  between operations: 15.6 us -> 2.98 us
  local copies, waits for them, and re-layouts: 4.07 us -> 14.6 us
  starting transfers between devices: 21.1 us -> 30.3 us
    all_gather x1 -> x0, waiting for transfers between devices: 32.4 us -> none  [on_device(): w_mine = lax.all_gather(half, 'mp', axis=0, axis_index_groups=X_GROUPS)]
    all_to_all x1, waiting for transfers between devices: 13.8 us -> 0.01 us  [on_device(): lax.all_to_all(spread, 'mp', 0, 0, tiled=True).reshape(1024, 2 * HD)]
    ppermute x13 -> x15, waiting for transfers between devices: 10.4 us -> 1.59 us  [shift(): return lax.ppermute(v, AXES, pairs)]
    unnamed x12 -> x32, local copies, waits for them, and re-layouts: 1.56 us -> 7.63 us
    ppermute x13 -> x15, starting transfers between devices: 15.9 us -> 21.4 us  [shift(): return lax.ppermute(v, AXES, pairs)]
    ppermute x0 -> x2, starting transfers between devices: none -> 5.18 us  [exchange_z(): return lax.ppermute(v, AXES, pairs)]
    slice x1, local copies, waits for them, and re-layouts: 0.02 us -> 1.76 us  [on_device(): far_b = shift(after[CHUNK // 2:], dy=-1)]
    dynamic_slice x0 -> x1, local copies, waits for them, and re-layouts: none -> 1.59 us  [on_device(): wv = lax.dynamic_slice_in_dim(w_value, y * HD, HD, 1)]
  transfers between devices with their start and end apart: 15 -> 18, of which waited for: 5 -> 2; matrix products, arithmetic and copies ran while one was open for 2% -> 10% of each run, Pallas kernels for 10% -> 16%
where the time goes in v3:
time: 93.2 us; the launch traced here: 92.5 us
  starting transfers between devices  30.3 us (33%)
  blocking collectives  19.7 us (21%)
  Pallas kernels  19.1 us (20%)
  local copies, waits for them, and re-layouts  14.6 us (16%)
  waiting for transfers between devices  3 us (3%)
  between operations  2.98 us (3%)
  other arithmetic  2.82 us (3%)
    ppermute x15, starting transfers between devices, shift(): return lax.ppermute(v, AXES, pairs)  21.4 us
    all_to_all x1, blocking collectives, on_device(): lax.all_to_all(ready.reshape(32, 64, HD), AXES, 0, 0, tiled=True, axis_in...  19.7 us
    unnamed x32, local copies, waits for them, and re-layouts  7.63 us
    pallas_call x1, Pallas kernels, rubric_part(): pl.pallas_call(rubric_kernel, out_shape=(jax.ShapeDtypeStruct((RESP, 256,...  6.83 us
    ppermute x2, starting transfers between devices, exchange_z(): return lax.ppermute(v, AXES, pairs)  5.18 us
    pallas_call x1, Pallas kernels, self_part(): pl.pallas_call(self_kernel, out_shape=jax.ShapeDtypeStruct((GROUPS, 4, 64...  4.34 us
    pallas_call x2, Pallas kernels, keys_values(): pl.pallas_call(kernel, out_shape=(jax.ShapeDtypeStruct((RESP, 64, 2 * HD)...  4.05 us
    all_to_all x1, starting transfers between devices, on_device(): lax.all_to_all(spread, 'mp', 0, 0, tiled=True).reshape(1024, 2 * HD)  3.66 us
  transfers between devices with their start and end apart: 18, of which 2 were waited for; matrix products, arithmetic and copies ran while one was open for 10% of the time, Pallas kernels for 16%

profile of v3, /device:TPU:1, one launch (start us, length us, event | category | flops | bytes accessed | tf_op | source)
XLA Modules:
  0.0 92.5 jit_solution(7061626232371546629)
XLA Ops:
  0.0 2.1 %collective-permute-start = (bf16[96,3584]{1,0:T(8,128)(2,1)}, bf16[96,3584]{1,0:T(8,128)(2,1)S(1)}, u32[]{:S(2)}, u32[]{:S(2)}) collective-permute-start(bf16[96,3584]{1,0:T(8,128)(2,1)} %bitcast.27), channel_id=1, source_target_pairs={{0,4},{16,20},{32,36},{48,52},{64,68},{80,84},{96,100},{112,116},{... | collective-permute-start | bytes 2064392 | tf_op jit(solution)/shard_map/ppermute | solution.py:40
  2.1 1.4 %collective-permute-start.1 = (bf16[96,3584]{1,0:T(8,128)(2,1)}, bf16[96,3584]{1,0:T(8,128)(2,1)}, u32[]{:S(2)}, u32[]{:S(2)}) collective-permute-start(bf16[96,3584]{1,0:T(8,128)(2,1)} %bitcast.28), channel_id=1, source_target_pairs={{0,12},{16,28},{32,44},{48,60},{64,76},{80,92},{96,108},{112,124},... | collective-permute-start | bytes 2064392 | tf_op jit(solution)/shard_map/ppermute | solution.py:40
  3.6 1.1 %collective-permute-start.10 = (bf16[4,128,256]{2,1,0:T(8,128)(2,1)}, bf16[4,128,256]{2,1,0:T(8,128)(2,1)S(1)}, u32[]{:S(2)}, u32[]{:S(2)}) collective-permute-start(bf16[4,128,256]{2,1,0:T(8,128)(2,1)} %bitcast.41), channel_id=1, source_target_pairs={{0,16},{16,0},{32,48},{48,32},{64,80},{80,64},{96,112},{112,96},{4... | collective-permute-start | bytes 786440 | tf_op jit(solution)/shard_map/ppermute | solution.py:40
  4.7 0.7 fusion.8
  7.3 1.1 %constant_dynamic-slice_fusion = bf16[1792,128]{1,0:T(8,128)(2,1)S(1)} fusion(bf16[3584,128]{1,0:T(8,128)(2,1)} %w_own.1, s32[]{:T(128)S(6)} %select_n.83), kind=kLoop, calls=%fused_computation.17 | loop fusion | bytes 917508 | tf_op jit(solution)/shard_map/dynamic_slice | solution.py:302
  8.4 0.9 %dynamic-slice_select_fusion = bf16[4,64,256]{2,1,0:T(8,128)(2,1)S(1)} fusion(bf16[4,128,256]{2,1,0:T(8,128)(2,1)S(1)} %collective-permute-done.10, s32[]{:T(128)S(6)} %select_n.91, bf16[4,128,256]{2,1,0:T(8,128)(2,1)} %bitcast.42, pred[]{:T(512)S(6)} %eq.17), kind=kLoop, calls=%fused_computation.1 | loop fusion | flops 65536 | bytes 393221 | tf_op jit(solution)/shard_map/jit(_where)/select_n | solution.py:309
  9.3 1.8 %collective-permute-start.11 = (bf16[4,64,256]{2,1,0:T(8,128)(2,1)S(1)}, bf16[4,64,256]{2,1,0:T(8,128)(2,1)S(1)}, u32[]{:S(2)}, u32[]{:S(2)}) collective-permute-start(bf16[4,64,256]{2,1,0:T(8,128)(2,1)S(1)} %dynamic-slice_select_fusion), channel_id=1, source_target_pairs={{0,32},{16,48},{32,0},{48,16},{64,96},{80,112},{96,64},{112,80},{4... | collective-permute-start | bytes 393224 | tf_op jit(solution)/shard_map/ppermute | solution.py:50
  11.1 0.8 pad_maximum_fusion
  11.9 1.2 %collective-permute-start.4 = (bf16[1808,128]{1,0:T(8,128)(2,1)}, bf16[1808,128]{1,0:T(8,128)(2,1)}, u32[]{:S(2)}, u32[]{:S(2)}) collective-permute-start(bf16[1808,128]{1,0:T(8,128)(2,1)} %pad_maximum_fusion), channel_id=1, source_target_pairs={{0,1},{16,17},{32,33},{48,49},{64,65},{80,81},{96,97},{112,113},{4... | collective-permute-start | bytes 1388552 | tf_op jit(solution)/shard_map/ppermute | solution.py:40
  13.1 1.5 %collective-permute-start.5 = (bf16[1808,128]{1,0:T(8,128)(2,1)}, bf16[1808,128]{1,0:T(8,128)(2,1)}, u32[]{:S(2)}, u32[]{:S(2)}) collective-permute-start(bf16[1808,128]{1,0:T(8,128)(2,1)} %pad_maximum_fusion), channel_id=1, source_target_pairs={{0,3},{16,19},{32,35},{48,51},{64,67},{80,83},{96,99},{112,115},{4... | collective-permute-start | bytes 1388552 | tf_op jit(solution)/shard_map/ppermute | solution.py:40
  15.4 3.4 %collective-permute-start.12 = (bf16[4,64,256]{2,1,0:T(8,128)(2,1)S(1)}, bf16[4,64,256]{2,1,0:T(8,128)(2,1)S(1)}, u32[]{:S(2)}, u32[]{:S(2)}) collective-permute-start(bf16[4,64,256]{2,1,0:T(8,128)(2,1)S(1)} %broadcast_select_fusion), channel_id=1, source_target_pairs={{0,64},{16,80},{32,96},{48,112},{64,0},{80,16},{96,32},{112,48},{4... | collective-permute-start | bytes 393224 | tf_op jit(solution)/shard_map/ppermute | solution.py:50
  18.7 1.6 %constant_dynamic-slice_fusion.1 = (bf16[3584,128]{1,0:T(8,128)(2,1)S(1)}, bf16[3584,128]{1,0:T(8,128)(2,1)S(1)}) fusion(bf16[3584,512]{1,0:T(8,128)(2,1)} %param.17, s32[]{:T(128)S(6)} %select_n.80, bf16[3584,512]{1,0:T(8,128)(2,1)} %param.15), kind=kLoop, calls=%fused_computation.18 | loop fusion | bytes 3670020 | tf_op jit(solution)/shard_map/dynamic_slice | solution.py:293
  20.4 1.4 %collective-permute-done.12 = bf16[4,64,256]{2,1,0:T(8,128)(2,1)S(1)} collective-permute-done((bf16[4,64,256]{2,1,0:T(8,128)(2,1)S(1)}, bf16[4,64,256]{2,1,0:T(8,128)(2,1)S(1)}, u32[]{:S(2)}, u32[]{:S(2)}) %collective-permute-start.12) | collective-permute-done | bytes 131104 | tf_op jit(solution)/shard_map/ppermute | solution.py:50
  21.8 2.6 %collective-permute-start.6 = (bf16[1808,128]{1,0:T(8,128)(2,1)}, bf16[1808,128]{1,0:T(8,128)(2,1)}, u32[]{:S(2)}, u32[]{:S(2)}) collective-permute-start(bf16[1808,128]{1,0:T(8,128)(2,1)} %pad_maximum_fusion), channel_id=1, source_target_pairs={{0,2},{16,18},{32,34},{48,50},{64,66},{80,82},{96,98},{112,114},{4... | collective-permute-start | bytes 1388552 | tf_op jit(solution)/shard_map/ppermute | solution.py:40
  24.4 0.8 broadcast_in_dim.2
  25.3 3.7 %all-to-all-start = ((bf16[16,64,256]{2,1,0:T(8,128)(2,1)}), bf16[16,64,256]{2,1,0:T(8,128)(2,1)S(1)}, u32[]{:S(2)}, u32[]{:S(2)}) async-start(bf16[16,64,256]{2,1,0:T(8,128)(2,1)} %bitcast.39), calls=%async_computation | async-start | bytes 1048576 | tf_op jit(solution)/shard_map/all_to_all | solution.py:316
  29.0 0.8 slice.12
  29.8 1.4 %collective-permute-start.2 = (bf16[48,3584]{1,0:T(8,128)(2,1)}, bf16[48,3584]{1,0:T(8,128)(2,1)}, u32[]{:S(2)}, u32[]{:S(2)}) collective-permute-start(bf16[48,3584]{1,0:T(8,128)(2,1)} %slice.12), channel_id=1, source_target_pairs={{0,4},{16,20},{32,36},{48,52},{64,68},{80,84},{96,100},{112,116},{... | collective-permute-start | bytes 1032200 | tf_op jit(solution)/shard_map/ppermute | solution.py:40
  31.1 0.2 fusion
  31.3 2.4 %collective-permute-start.7 = (bf16[1808,128]{1,0:T(8,128)(2,1)}, bf16[1808,128]{1,0:T(8,128)(2,1)}, u32[]{:S(2)}, u32[]{:S(2)}) collective-permute-start(bf16[1808,128]{1,0:T(8,128)(2,1)} %collective-permute-done.4.m1), channel_id=1, source_target_pairs={{0,16},{16,0},{32,48},{48,32},{64,80},{80,64},{96,112},{112,96},{4... | collective-permute-start | bytes 1388552 | tf_op jit(solution)/shard_map/ppermute | solution.py:40
  33.8 0.1 collective-permute-start.8
  33.9 0.1 pad_maximum_fusion.1
  34.0 1.8 %slice.13 = bf16[48,3584]{1,0:T(8,128)(2,1)} slice(bf16[96,3584]{1,0:T(8,128)(2,1)} %collective-permute-done.1.after), slice={[48:96], [0:3584]} | slice | bytes 688128 | tf_op jit(solution)/shard_map/slice | solution.py:281
  35.7 1.0 %collective-permute-start.3 = (bf16[48,3584]{1,0:T(8,128)(2,1)}, bf16[48,3584]{1,0:T(8,128)(2,1)}, u32[]{:S(2)}, u32[]{:S(2)}) collective-permute-start(bf16[48,3584]{1,0:T(8,128)(2,1)} %slice.13), channel_id=1, source_target_pairs={{0,12},{16,28},{32,44},{48,60},{64,76},{80,92},{96,108},{112,124},... | collective-permute-start | bytes 1032200 | tf_op jit(solution)/shard_map/ppermute | solution.py:40
  36.8 0.1 pad_add_fusion.meta
  36.9 1.1 %copy-done.5 = bf16[6,16,3584]{2,1,0:T(8,128)(2,1)S(1)} copy-done((bf16[6,16,3584]{2,1,0:T(8,128)(2,1)S(1)}, bf16[6,16,3584]{2,1,0:T(8,128)(2,1)}, u32[]{:S(2)}) %copy-start.5) | copy-done | bytes 688152
  38.0 0.4 own_rows.1.own
  38.4 1.2 %copy-done.4 = bf16[96,3584]{1,0:T(8,128)(2,1)S(1)} copy-done((bf16[96,3584]{1,0:T(8,128)(2,1)S(1)}, bf16[96,3584]{1,0:T(8,128)(2,1)}, u32[]{:S(2)}) %copy-start.4) | copy-done | bytes 688152
  39.6 0.7 copy-done.8
  40.3 0.7 copy-done.10
  40.9 2.3 %near_rows.1 = (bf16[6,64,256]{2,1,0:T(8,128)(2,1)S(1)}, bf16[288,3584]{1,0:T(8,128)(2,1)S(1)}) custom-call(s32[4]{0:T(128)S(1)} %pad_add_fusion.meta, bf16[96,3584]{1,0:T(8,128)(2,1)S(1)} %own_rows.1.own, bf16[96,3584]{1,0:T(8,128)(2,1)S(1)} %copy-done.4, bf16[96,3584]{1,0:T(8,128)(2,1)} %collective-permute-done.1.after, f32[1,3584]{1,0:T(1,128)S(1)} %reshape.62.gain, ...), custom_call_target="tpu_custom_call" | custom-call | tf_op jit(solution)/shard_map/near_rows/pallas_call | solution.py:132
  43.2 1.3 %copy-done = bf16[288,3584]{1,0:T(8,128)(2,1)} copy-done((bf16[288,3584]{1,0:T(8,128)(2,1)}, bf16[288,3584]{1,0:T(8,128)(2,1)S(1)}, u32[]{:S(2)}) %copy-start) | copy-done | bytes 2064408
  44.6 0.8 collective-permute-start.13
  45.3 1.4 %collective-permute-start.9 = (bf16[1808,128]{1,0:T(8,128)(2,1)}, bf16[1808,128]{1,0:T(8,128)(2,1)S(1)}, u32[]{:S(2)}, u32[]{:S(2)}) collective-permute-start(bf16[1808,128]{1,0:T(8,128)(2,1)} %collective-permute-done.6.m3), channel_id=1, source_target_pairs={{0,16},{16,0},{32,48},{48,32},{64,80},{80,64},{96,112},{112,96},{4... | collective-permute-start | bytes 1388552 | tf_op jit(solution)/shard_map/ppermute | solution.py:40
  46.7 1.6 %collective-permute-done.3.far_b = bf16[48,3584]{1,0:T(8,128)(2,1)} collective-permute-done((bf16[48,3584]{1,0:T(8,128)(2,1)}, bf16[48,3584]{1,0:T(8,128)(2,1)}, u32[]{:S(2)}, u32[]{:S(2)}) %collective-permute-start.3) | collective-permute-done | bytes 344096 | tf_op jit(solution)/shard_map/ppermute | solution.py:40
  48.3 0.6 copy-done.7
  48.9 0.7 copy-done.9
  49.6 0.7 copy-done.11
  50.3 1.8 %far_rows.1 = (bf16[6,64,256]{2,1,0:T(8,128)(2,1)S(1)}, bf16[96,3584]{1,0:T(8,128)(2,1)S(1)}) custom-call(s32[4]{0:T(128)S(1)} %copy-done.7, bf16[6,64,256]{2,1,0:T(8,128)(2,1)S(1)} %get-tuple-element.13.near, bf16[48,3584]{1,0:T(8,128)(2,1)} %collective-permute-done.2.far_a, bf16[48,3584]{1,0:T(8,128)(2,1)} %collective-permute-done.3.far_b, ...), custom_call_target="tpu_custom_call" | custom-call | tf_op jit(solution)/shard_map/far_rows/pallas_call | solution.py:132
  52.1 1.5 %collective-permute-start.14 = (bf16[6,64,256]{2,1,0:T(8,128)(2,1)S(1)}, bf16[6,64,256]{2,1,0:T(8,128)(2,1)S(1)}, u32[]{:S(2)}, u32[]{:S(2)}) collective-permute-start(bf16[6,64,256]{2,1,0:T(8,128)(2,1)S(1)} %get-tuple-element.18.kv0), channel_id=1, source_target_pairs={{0,1},{16,17},{32,33},{48,49},{64,65},{80,81},{96,97},{112,113},{4... | collective-permute-start | bytes 589832 | tf_op jit(solution)/shard_map/ppermute | solution.py:40
  53.6 1.2 %collective-permute-start.15 = (bf16[6,64,256]{2,1,0:T(8,128)(2,1)S(1)}, bf16[6,64,256]{2,1,0:T(8,128)(2,1)S(1)}, u32[]{:S(2)}, u32[]{:S(2)}) collective-permute-start(bf16[6,64,256]{2,1,0:T(8,128)(2,1)S(1)} %get-tuple-element.18.kv0), channel_id=1, source_target_pairs={{0,3},{16,19},{32,35},{48,51},{64,67},{80,83},{96,99},{112,115},{4... | collective-permute-start | bytes 589832 | tf_op jit(solution)/shard_map/ppermute | solution.py:40
  54.8 1.6 %collective-permute-start.16 = (bf16[6,64,256]{2,1,0:T(8,128)(2,1)S(1)}, bf16[6,64,256]{2,1,0:T(8,128)(2,1)S(1)}, u32[]{:S(2)}, u32[]{:S(2)}) collective-permute-start(bf16[6,64,256]{2,1,0:T(8,128)(2,1)S(1)} %get-tuple-element.18.kv0), channel_id=1, source_target_pairs={{0,2},{16,18},{32,34},{48,50},{64,66},{80,82},{96,98},{112,114},{4... | collective-permute-start | bytes 589832 | tf_op jit(solution)/shard_map/ppermute | solution.py:40
  56.5 0.6 copy-done.12
  57.1 3.6 %queries.1.q_ref = bf16[6,4,64,128]{3,2,1,0:T(8,128)(2,1)S(1)} custom-call(s32[4]{0:T(128)S(1)} %copy-done.7, bf16[288,3584]{1,0:T(8,128)(2,1)S(1)} %copy-done.1, bf16[96,3584]{1,0:T(8,128)(2,1)S(1)} %get-tuple-element.14.far, bf16[3584,128]{1,0:T(8,128)(2,1)S(1)} %copy-done.2, f32[1,128]{1,0:T(1,128)S(1)} %bitcast.34, ...), custom_call_target="tpu_custom_call" | custom-call | tf_op jit(solution)/shard_map/queries/pallas_call | solution.py:180
  60.7 6.8 %rubric_part.1 = (f32[6,256,128]{2,1,0:T(8,128)S(1)}, f32[6,256,128]{2,1,0:T(8,128)S(1)}) custom-call(bf16[6,4,64,128]{3,2,1,0:T(8,128)(2,1)S(1)} %queries.1.q_ref, bf16[1024,256]{1,0:T(8,128)(2,1)S(1)} %bitcast.26, bf16[1024,256]{1,0:T(8,128)(2,1)S(1)} %collective-permute-done.13.c_other), custom_call_target="tpu_custom_call" | custom-call | tf_op jit(solution)/shard_map/rubric_part/pallas_call | solution.py:209
  67.6 4.3 %self_part.1 = bf16[8,4,64,128]{3,2,1,0:T(8,128)(2,1)S(1)} custom-call(s32[4]{0:T(128)S(1)} %copy-done.7, s32[48]{0:T(128)S(1)} %copy-done.13, s32[48]{0:T(128)S(1)} %copy-done.14, bf16[6,4,64,128]{3,2,1,0:T(8,128)(2,1)S(1)} %queries.1.q_ref, f32[6,256,128]{2,1,0:T(8,128)S(1)} %get-tuple-element.16.acc_ref, f32[6,256,128]{2,1,0:T(8,128)S(1)} %get-tuple-element.17.stat_ref, ...), custom_call_target="tpu_custom_call" | custom-call | tf_op jit(solution)/shard_map/self_part/pallas_call | solution.py:257
  71.9 19.7 %all_to_all.10 = bf16[32,64,128]{2,1,0:T(8,128)(2,1)S(1)} all-to-all(bf16[32,64,128]{2,1,0:T(8,128)(2,1)S(1)} %bitcast.24), channel_id=1, replica_groups={{0,1,2,3,16,17,18,19,32,33,34,35,48,49,50,51,64,65,66,67,80,81,82,83,96..., dimensions={0} | all-to-all | bytes 1048576 | tf_op jit(solution)/shard_map/all_to_all | solution.py:330
  91.6 0.9 copy.12
  (45 shorter events, 0.2 us)
Async XLA Ops:
  0.0 29.0 %collective-permute-start = (bf16[96,3584]{1,0:T(8,128)(2,1)}, bf16[96,3584]{1,0:T(8,128)(2,1)S(1)}, u32[]{:S(2)}, u32[]{:S(2)}) collective-permute-start(bf16[96,3584]{1,0:T(8,128)(2,1)} %bitcast.27), channel_id=1, source_target_pairs={{0,4},{16,20},{32,36},{48,52},{64,68},{80,84},{96,100},{112,116},{... | collective-permute-start | bytes 2064392 | tf_op jit(solution)/shard_map/ppermute | solution.py:40
  2.1 31.8 %collective-permute-start.1 = (bf16[96,3584]{1,0:T(8,128)(2,1)}, bf16[96,3584]{1,0:T(8,128)(2,1)}, u32[]{:S(2)}, u32[]{:S(2)}) collective-permute-start(bf16[96,3584]{1,0:T(8,128)(2,1)} %bitcast.28), channel_id=1, source_target_pairs={{0,12},{16,28},{32,44},{48,60},{64,76},{80,92},{96,108},{112,124},... | collective-permute-start | bytes 2064392 | tf_op jit(solution)/shard_map/ppermute | solution.py:40
  3.6 4.8 %collective-permute-start.10 = (bf16[4,128,256]{2,1,0:T(8,128)(2,1)}, bf16[4,128,256]{2,1,0:T(8,128)(2,1)S(1)}, u32[]{:S(2)}, u32[]{:S(2)}) collective-permute-start(bf16[4,128,256]{2,1,0:T(8,128)(2,1)} %bitcast.41), channel_id=1, source_target_pairs={{0,16},{16,0},{32,48},{48,32},{64,80},{80,64},{96,112},{112,96},{4... | collective-permute-start | bytes 786440 | tf_op jit(solution)/shard_map/ppermute | solution.py:40
  9.3 6.0 %collective-permute-start.11 = (bf16[4,64,256]{2,1,0:T(8,128)(2,1)S(1)}, bf16[4,64,256]{2,1,0:T(8,128)(2,1)S(1)}, u32[]{:S(2)}, u32[]{:S(2)}) collective-permute-start(bf16[4,64,256]{2,1,0:T(8,128)(2,1)S(1)} %dynamic-slice_select_fusion), channel_id=1, source_target_pairs={{0,32},{16,48},{32,0},{48,16},{64,96},{80,112},{96,64},{112,80},{4... | collective-permute-start | bytes 393224 | tf_op jit(solution)/shard_map/ppermute | solution.py:50
  11.9 19.4 %collective-permute-start.4 = (bf16[1808,128]{1,0:T(8,128)(2,1)}, bf16[1808,128]{1,0:T(8,128)(2,1)}, u32[]{:S(2)}, u32[]{:S(2)}) collective-permute-start(bf16[1808,128]{1,0:T(8,128)(2,1)} %pad_maximum_fusion), channel_id=1, source_target_pairs={{0,1},{16,17},{32,33},{48,49},{64,65},{80,81},{96,97},{112,113},{4... | collective-permute-start | bytes 1388552 | tf_op jit(solution)/shard_map/ppermute | solution.py:40
  13.1 20.6 %collective-permute-start.5 = (bf16[1808,128]{1,0:T(8,128)(2,1)}, bf16[1808,128]{1,0:T(8,128)(2,1)}, u32[]{:S(2)}, u32[]{:S(2)}) collective-permute-start(bf16[1808,128]{1,0:T(8,128)(2,1)} %pad_maximum_fusion), channel_id=1, source_target_pairs={{0,3},{16,19},{32,35},{48,51},{64,67},{80,83},{96,99},{112,115},{4... | collective-permute-start | bytes 1388552 | tf_op jit(solution)/shard_map/ppermute | solution.py:40
  15.3 21.5 %copy-start.15 = (f32[3584]{0:T(1024)S(1)}, f32[3584]{0:T(1024)}, u32[]{:S(2)}) copy-start(f32[3584]{0:T(1024)} %param.12) | copy-start | bytes 43012
  15.4 6.4 %collective-permute-start.12 = (bf16[4,64,256]{2,1,0:T(8,128)(2,1)S(1)}, bf16[4,64,256]{2,1,0:T(8,128)(2,1)S(1)}, u32[]{:S(2)}, u32[]{:S(2)}) collective-permute-start(bf16[4,64,256]{2,1,0:T(8,128)(2,1)S(1)} %broadcast_select_fusion), channel_id=1, source_target_pairs={{0,64},{16,80},{32,96},{48,112},{64,0},{80,16},{96,32},{112,48},{4... | collective-permute-start | bytes 393224 | tf_op jit(solution)/shard_map/ppermute | solution.py:50
  21.8 22.8 %collective-permute-start.6 = (bf16[1808,128]{1,0:T(8,128)(2,1)}, bf16[1808,128]{1,0:T(8,128)(2,1)}, u32[]{:S(2)}, u32[]{:S(2)}) collective-permute-start(bf16[1808,128]{1,0:T(8,128)(2,1)} %pad_maximum_fusion), channel_id=1, source_target_pairs={{0,2},{16,18},{32,34},{48,50},{64,66},{80,82},{96,98},{112,114},{4... | collective-permute-start | bytes 1388552 | tf_op jit(solution)/shard_map/ppermute | solution.py:40
  25.3 19.3 %all-to-all-start = ((bf16[16,64,256]{2,1,0:T(8,128)(2,1)}), bf16[16,64,256]{2,1,0:T(8,128)(2,1)S(1)}, u32[]{:S(2)}, u32[]{:S(2)}) async-start(bf16[16,64,256]{2,1,0:T(8,128)(2,1)} %bitcast.39), calls=%async_computation | async-start | bytes 1048576 | tf_op jit(solution)/shard_map/all_to_all | solution.py:316
  29.0 7.9 %copy-start.3 = (bf16[96,3584]{1,0:T(8,128)(2,1)}, bf16[96,3584]{1,0:T(8,128)(2,1)S(1)}, u32[]{:S(2)}) copy-start(bf16[96,3584]{1,0:T(8,128)(2,1)S(1)} %collective-permute-done.before) | copy-start | bytes 2064388
  29.8 15.6 %collective-permute-start.2 = (bf16[48,3584]{1,0:T(8,128)(2,1)}, bf16[48,3584]{1,0:T(8,128)(2,1)}, u32[]{:S(2)}, u32[]{:S(2)}) collective-permute-start(bf16[48,3584]{1,0:T(8,128)(2,1)} %slice.12), channel_id=1, source_target_pairs={{0,4},{16,20},{32,36},{48,52},{64,68},{80,84},{96,100},{112,116},{... | collective-permute-start | bytes 1032200 | tf_op jit(solution)/shard_map/ppermute | solution.py:40
  31.3 22.2 %collective-permute-start.7 = (bf16[1808,128]{1,0:T(8,128)(2,1)}, bf16[1808,128]{1,0:T(8,128)(2,1)}, u32[]{:S(2)}, u32[]{:S(2)}) collective-permute-start(bf16[1808,128]{1,0:T(8,128)(2,1)} %collective-permute-done.4.m1), channel_id=1, source_target_pairs={{0,16},{16,0},{32,48},{48,32},{64,80},{80,64},{96,112},{112,96},{4... | collective-permute-start | bytes 1388552 | tf_op jit(solution)/shard_map/ppermute | solution.py:40
  33.8 21.0 %collective-permute-start.8 = (bf16[1808,128]{1,0:T(8,128)(2,1)}, bf16[1808,128]{1,0:T(8,128)(2,1)}, u32[]{:S(2)}, u32[]{:S(2)}) collective-permute-start(bf16[1808,128]{1,0:T(8,128)(2,1)} %collective-permute-done.5.m2), channel_id=1, source_target_pairs={{0,16},{16,0},{32,48},{48,32},{64,80},{80,64},{96,112},{112,96},{4... | collective-permute-start | bytes 1388552 | tf_op jit(solution)/shard_map/ppermute | solution.py:40
  35.7 12.6 %collective-permute-start.3 = (bf16[48,3584]{1,0:T(8,128)(2,1)}, bf16[48,3584]{1,0:T(8,128)(2,1)}, u32[]{:S(2)}, u32[]{:S(2)}) collective-permute-start(bf16[48,3584]{1,0:T(8,128)(2,1)} %slice.13), channel_id=1, source_target_pairs={{0,12},{16,28},{32,44},{48,60},{64,76},{80,92},{96,108},{112,124},... | collective-permute-start | bytes 1032200 | tf_op jit(solution)/shard_map/ppermute | solution.py:40
  36.9 1.5 %copy-start.6 = (s32[4]{0:T(128)}, s32[4]{0:T(128)S(1)}, u32[]{:S(2)}) copy-start(s32[4]{0:T(128)S(1)} %pad_add_fusion.meta) | copy-start | bytes 52
  36.9 1.1 %copy-start.5 = (bf16[6,16,3584]{2,1,0:T(8,128)(2,1)S(1)}, bf16[6,16,3584]{2,1,0:T(8,128)(2,1)}, u32[]{:S(2)}) copy-start(bf16[6,16,3584]{2,1,0:T(8,128)(2,1)} %param.11) | copy-start | bytes 2064388
  38.4 18.1 %copy-start.2 = (bf16[3584,128]{1,0:T(8,128)(2,1)S(1)}, bf16[3584,128]{1,0:T(8,128)(2,1)}, u32[]{:S(2)}) copy-start(bf16[3584,128]{1,0:T(8,128)(2,1)} %w_own.1) | copy-start | bytes 2752516
  38.4 1.2 %copy-start.4 = (bf16[96,3584]{1,0:T(8,128)(2,1)S(1)}, bf16[96,3584]{1,0:T(8,128)(2,1)}, u32[]{:S(2)}) copy-start(bf16[96,3584]{1,0:T(8,128)(2,1)} %copy-done.3) | copy-start | bytes 2064388
  39.6 0.7 copy-start.8
  40.2 0.7 copy-start.10
  43.2 1.4 %copy-start = (bf16[288,3584]{1,0:T(8,128)(2,1)}, bf16[288,3584]{1,0:T(8,128)(2,1)S(1)}, u32[]{:S(2)}) copy-start(bf16[288,3584]{1,0:T(8,128)(2,1)S(1)} %get-tuple-element.12.near) | copy-start | bytes 6193156
  44.6 11.9 %copy-start.1 = (bf16[288,3584]{1,0:T(8,128)(2,1)S(1)}, bf16[288,3584]{1,0:T(8,128)(2,1)}, u32[]{:S(2)}) copy-start(bf16[288,3584]{1,0:T(8,128)(2,1)} %copy-done) | copy-start | bytes 6193156
  44.6 16.1 %collective-permute-start.13 = (bf16[1024,256]{1,0:T(8,128)(2,1)S(1)}, bf16[1024,256]{1,0:T(8,128)(2,1)S(1)}, u32[]{:S(2)}, u32[]{:S(2)}) collective-permute-start(bf16[1024,256]{1,0:T(8,128)(2,1)S(1)} %bitcast.25), channel_id=1, source_target_pairs={{0,16},{16,0},{32,48},{48,32},{64,80},{80,64},{96,112},{112,96},{4... | collective-permute-start | bytes 1572872 | tf_op jit(solution)/shard_map/ppermute | solution.py:40
  45.3 11.1 %collective-permute-start.9 = (bf16[1808,128]{1,0:T(8,128)(2,1)}, bf16[1808,128]{1,0:T(8,128)(2,1)S(1)}, u32[]{:S(2)}, u32[]{:S(2)}) collective-permute-start(bf16[1808,128]{1,0:T(8,128)(2,1)} %collective-permute-done.6.m3), channel_id=1, source_target_pairs={{0,16},{16,0},{32,48},{48,32},{64,80},{80,64},{96,112},{112,96},{4... | collective-permute-start | bytes 1388552 | tf_op jit(solution)/shard_map/ppermute | solution.py:40
  48.3 0.6 copy-start.7
  48.9 0.7 copy-start.9
  49.6 0.7 copy-start.11
  52.1 15.5 %collective-permute-start.14 = (bf16[6,64,256]{2,1,0:T(8,128)(2,1)S(1)}, bf16[6,64,256]{2,1,0:T(8,128)(2,1)S(1)}, u32[]{:S(2)}, u32[]{:S(2)}) collective-permute-start(bf16[6,64,256]{2,1,0:T(8,128)(2,1)S(1)} %get-tuple-element.18.kv0), channel_id=1, source_target_pairs={{0,1},{16,17},{32,33},{48,49},{64,65},{80,81},{96,97},{112,113},{4... | collective-permute-start | bytes 589832 | tf_op jit(solution)/shard_map/ppermute | solution.py:40
  53.6 14.0 %collective-permute-start.15 = (bf16[6,64,256]{2,1,0:T(8,128)(2,1)S(1)}, bf16[6,64,256]{2,1,0:T(8,128)(2,1)S(1)}, u32[]{:S(2)}, u32[]{:S(2)}) collective-permute-start(bf16[6,64,256]{2,1,0:T(8,128)(2,1)S(1)} %get-tuple-element.18.kv0), channel_id=1, source_target_pairs={{0,3},{16,19},{32,35},{48,51},{64,67},{80,83},{96,99},{112,115},{4... | collective-permute-start | bytes 589832 | tf_op jit(solution)/shard_map/ppermute | solution.py:40
  54.8 12.7 %collective-permute-start.16 = (bf16[6,64,256]{2,1,0:T(8,128)(2,1)S(1)}, bf16[6,64,256]{2,1,0:T(8,128)(2,1)S(1)}, u32[]{:S(2)}, u32[]{:S(2)}) collective-permute-start(bf16[6,64,256]{2,1,0:T(8,128)(2,1)S(1)} %get-tuple-element.18.kv0), channel_id=1, source_target_pairs={{0,2},{16,18},{32,34},{48,50},{64,66},{80,82},{96,98},{112,114},{4... | collective-permute-start | bytes 589832 | tf_op jit(solution)/shard_map/ppermute | solution.py:40
  56.5 0.7 copy-start.12
  57.1 10.4 %copy-start.13 = (s32[48]{0:T(128)S(1)}, s32[48]{0:T(128)}, u32[]{:S(2)}) copy-start(s32[48]{0:T(128)} %dest.1) | copy-start | bytes 580
  57.1 10.5 %copy-start.14 = (s32[48]{0:T(128)S(1)}, s32[48]{0:T(128)}, u32[]{:S(2)}) copy-start(s32[48]{0:T(128)} %lengths.1) | copy-start | bytes 580

commit v4 on v3

--- a/solution.py
+++ b/solution.py
@@ -14,7 +14,6 @@
 PROMPT = 2048
 RESP = 6
 GROUPS = 8
-HALF_D = D // 2
 BIAS_ROWS = 16
 CHUNK = RESP * 16
 THETA = 1000000.0
@@ -40,13 +39,15 @@
     return lax.ppermute(v, AXES, pairs)
 
 
-def exchange_z(v, bit):
+def both_ways(v, axis):
     pairs = []
     for x in range(4):
         for y in range(4):
             for z in range(4):
                 for c in range(2):
-                    pairs.append((device_number(x, y, z, c), device_number(x, y, z ^ bit, c)))
+                    at = {"x": x, "y": y, "z": z}
+                    at[axis] = (at[axis] + 1 - 2 * c) % 4
+                    pairs.append((device_number(x, y, z, c), device_number(**at, c=c)))
     return lax.ppermute(v, AXES, pairs)
 
 
@@ -98,34 +99,18 @@
             out[i, pl.ds(base, 16), HD : 2 * HD] = value[part]
 
 
-def own_kernel(own, gain, rows):
-    rows[...] = norm(own[...], gain[...])
-
-
 def near_kernel(meta, own, before, after, gain, wk, wv, bk, bv, cos_ref, sin_ref, out, rows):
     out[...] = jnp.zeros_like(out)
-    rows[0:CHUNK, :] = own[...]
+    rows[0:CHUNK, :] = norm(own[...], gain[...])
     rows[CHUNK : 2 * CHUNK, :] = norm(before[...], gain[...])
     rows[2 * CHUNK : 3 * CHUNK, :] = norm(after[...], gain[...])
     project(meta[0], rows[...], (0, 1, 2), wk, wv, bk, bv, cos_ref, sin_ref, out)
 
 
-def far_kernel(meta, near, far_a, far_b, gain, wk, wv, bk, bv, cos_ref, sin_ref, out, rows):
+def far_kernel(meta, near, far, gain, wk, wv, bk, bv, cos_ref, sin_ref, out, rows):
     out[...] = near[...]
-    rows[0 : CHUNK // 2, :] = norm(far_a[...], gain[...])
-    rows[CHUNK // 2 : CHUNK, :] = norm(far_b[...], gain[...])
+    rows[...] = norm(far[...], gain[...])
     project(meta[0], rows[...], (3,), wk, wv, bk, bv, cos_ref, sin_ref, out)
-
-
-def norm_own(own, gain):
-    return pl.pallas_call(
-        own_kernel,
-        out_shape=jax.ShapeDtypeStruct((CHUNK, D), jnp.bfloat16),
-        in_specs=[VMEM_SPEC] * 2,
-        out_specs=VMEM_SPEC,
-        compiler_params=params(LIMIT),
-        name="own_rows",
-    )(own, gain)
 
 
 def keys_values(kernel, name, count, meta, chunks, small):
@@ -142,50 +127,38 @@
     )(meta, *chunks, *small)
 
 
-def query_kernel(
-    meta, near, far, w_own, b_own, m1, m2, m3, o1, o2, o3, cos_ref, sin_ref, q_out, rows
-):
+def query_kernel(meta, near, far, w0, w1, w2, w3, cos_ref, sin_ref, q_out, rows):
     y, c, x = meta[0], meta[1], meta[2]
     rows[0 : 3 * CHUNK, :] = near[...]
     rows[3 * CHUNK : 4 * CHUNK, :] = far[...]
-    mine_at = pl.multiple_of(c * HALF_D, 128)
-    other_at = pl.multiple_of((1 - c) * HALF_D, 128)
-
-    def bias(ref):
-        tail = ref[HALF_D : HALF_D + BIAS_ROWS, :].astype(jnp.float32)
-        return tail[0:1, :] + tail[1:2, :] + tail[2:3, :]
-
-    mine = [w_own[pl.ds(mine_at, HALF_D), :]] + [ref[:HALF_D, :] for ref in (m1, m2, m3)]
-    other = [w_own[pl.ds(other_at, HALF_D), :]] + [ref[:HALF_D, :] for ref in (o1, o2, o3)]
-    biases = [b_own[...], bias(m1), bias(m2), bias(m3)]
+    weights = (w0, w1, w2, w3)
+    heads = [lax.rem(x + turn, 4) for turn in (0, 3 - 2 * c, 1 + 2 * c, 2)]
     for lo in (0, 2):
-        first = jnp.concatenate(mine[lo : lo + 2], axis=1)
-        second = jnp.concatenate(other[lo : lo + 2], axis=1)
-        both = jnp.dot(rows[:, pl.ds(mine_at, HALF_D)], first, preferred_element_type=jnp.float32)
-        both = both + jnp.dot(
-            rows[:, pl.ds(other_at, HALF_D)], second, preferred_element_type=jnp.float32
-        )
+        w = jnp.concatenate([weights[lo][:D, :], weights[lo + 1][:D, :]], axis=1)
+        both = jnp.dot(rows[...], w, preferred_element_type=jnp.float32)
         for n in (lo, lo + 1):
-            head = lax.rem(x + TURNS[n], 4)
-            raw = both[:, (n - lo) * HD : (n - lo + 1) * HD] + biases[n]
+            tail = weights[n][D : D + BIAS_ROWS, :].astype(jnp.float32)
+            bias = tail[0:1, :] + tail[1:2, :] + tail[2:3, :]
+            raw = both[:, (n - lo) * HD : (n - lo + 1) * HD] + bias
             for j in range(4):
                 base, cos = table(cos_ref, chunk_y(y, j))
                 ignored, sin = table(sin_ref, chunk_y(y, j))
                 for i in range(RESP):
                     part = raw[j * CHUNK + i * 16 : j * CHUNK + i * 16 + 16, :]
-                    q_out[i, head, pl.ds(base, 16), :] = rope(part, cos, sin).astype(jnp.bfloat16)
-
-
-def make_queries(meta, near, far, w_own, b_own, mine, other, cos, sin):
+                    rotated = rope(part, cos, sin).astype(jnp.bfloat16)
+                    q_out[i, heads[n], pl.ds(base, 16), :] = rotated
+
+
+def make_queries(meta, near, far, weights, cos, sin):
     return pl.pallas_call(
         query_kernel,
         out_shape=jax.ShapeDtypeStruct((RESP, 4, 64, HD), jnp.bfloat16),
-        in_specs=[SMEM_SPEC] + [VMEM_SPEC] * 12,
+        in_specs=[SMEM_SPEC] + [VMEM_SPEC] * 8,
         out_specs=VMEM_SPEC,
         scratch_shapes=[pltpu.VMEM((4 * CHUNK, D), jnp.bfloat16)],
         compiler_params=params(LIMIT),
         name="queries",
-    )(meta, near, far, w_own, b_own, *mine, *other, cos, sin)
+    )(meta, near, far, *weights, cos, sin)
 
 
 def rubric_kernel(q_ref, c_mine, c_other, acc_out, stat_out):
@@ -202,7 +175,7 @@
         stat_out[i] = jnp.where(lane < 64, top, total)
         return carry
 
-    lax.fori_loop(0, RESP, step, 0)
+    lax.fori_loop(0, RESP, step, 0, unroll=True)
 
 
 def rubric_part(q, c_mine, c_other):
@@ -277,8 +250,7 @@
     gain = gain.reshape(1, D)
     before = shift(own, dy=1)
     after = shift(own, dy=-1)
-    far_a = shift(before[: CHUNK // 2], dy=1)
-    far_b = shift(after[CHUNK // 2 :], dy=-1)
+    far = shift(own, dy=2)
 
     frequency = jnp.exp(jnp.arange(64, dtype=jnp.float32) * (-2.0 * math.log(THETA) / HD))
     slot = jnp.arange(64, dtype=jnp.int32)
@@ -292,39 +264,41 @@
     wk = lax.dynamic_slice_in_dim(w_key, y * HD, HD, 1)
     wv = lax.dynamic_slice_in_dim(w_value, y * HD, HD, 1)
     small = (gain, wk, wv, b_key.reshape(1, -1), b_value.reshape(1, -1), cos, sin)
-    own_rows = norm_own(own, gain)
 
     first = lax.reduce_precision(b_query, 8, 7)
     second = lax.reduce_precision(b_query - first, 8, 7)
     third = b_query - first - second
     tail = jnp.stack([first, second, third]).astype(jnp.bfloat16)
     tail = jnp.pad(tail, ((0, BIAS_ROWS - 3), (0, 0)))
-    half = jnp.concatenate([lax.dynamic_slice_in_dim(w_query, c * HALF_D, HALF_D, 0), tail], axis=0)
-    mine = (shift(half, dx=1), shift(half, dx=-1), shift(half, dx=2))
-    other = tuple(shift(v, flip=1) for v in mine)
+    w_own = jnp.concatenate([w_query, tail], axis=0)
+    w_beside = both_ways(w_own, "x")
+    w_across = shift(w_beside, flip=1)
+    w_far = both_ways(w_beside, "x")
 
     owner = dest_of[0]
     cache = rubric_cache[0]
     swapped = shift(cache, flip=1)
     cache = jnp.where(owner % 2 == c, cache, swapped)
+    beside = both_ways(cache, "z")
+    across = shift(beside, flip=1)
+    turn = (owner // 2 - z) % 4
+    here = jnp.where(c == 0, 3, 1)
+    cache = jnp.where(turn == here, beside, jnp.where(turn == 4 - here, across, cache))
     piece = lax.dynamic_slice_in_dim(cache, c * 64, 64, 1)
-    for bit in (1, 2):
-        across = exchange_z(piece, bit)
-        same = (owner // 2 & bit) == (z & bit)
-        piece = jnp.where(same, piece, across)
+    piece = jnp.where(turn == 2, both_ways(piece, "z"), piece)
     spread = jnp.broadcast_to(piece[:, None], (4, 4, 64, 2 * HD)).reshape(16, 64, 2 * HD)
     c_mine = lax.all_to_all(spread, "mp", 0, 0, tiled=True).reshape(1024, 2 * HD)
 
     kv, near_rows = keys_values(
-        near_kernel, "near_rows", 3 * CHUNK, meta, (own_rows, before, after), small
+        near_kernel, "near_rows", 3 * CHUNK, meta, (own, before, after), small
     )
-    c_mine, _ = lax.optimization_barrier((c_mine, near_rows))
+    kv, far_rows = keys_values(far_kernel, "far_rows", CHUNK, meta, (kv, far), small)
+    c_mine, _ = lax.optimization_barrier((c_mine, kv))
     c_other = shift(c_mine, flip=1)
-    kv, far_rows = keys_values(far_kernel, "far_rows", CHUNK, meta, (kv, far_a, far_b), small)
     parts = (kv, shift(kv, dx=1), shift(kv, dx=-1), shift(kv, dx=2))
-    q = make_queries(
-        meta, near_rows, far_rows, w_query, b_query.reshape(1, HD), mine, other, cos, sin
-    )
+    far_rows, _ = lax.optimization_barrier((far_rows, c_other))
+    weights = (w_own, w_beside, w_across, w_far)
+    q = make_queries(meta, near_rows, far_rows, weights, cos, sin)
     acc, stat = rubric_part(q, c_mine, c_other)
     ready = self_part(meta, dest_of, lengths, q, acc, stat, parts)
     arrived = lax.all_to_all(

time: 93.2 us -> 87.7 us (0.941)
  local copies, waits for them, and re-layouts: 14.6 us -> 9.34 us
  starting transfers between devices: 30.3 us -> 28.4 us
  waiting for transfers between devices: 3 us -> 4.9 us
  Pallas kernels: 19.1 us -> 17.8 us
    ppermute x15 -> x10, starting transfers between devices: 21.4 us -> 13.1 us  [shift(): return lax.ppermute(v, AXES, pairs)]
    ppermute x2 -> x4, starting transfers between devices: 5.18 us -> 11.7 us  [both_ways(): return lax.ppermute(v, AXES, pairs)]
    ppermute x2 -> x4, waiting for transfers between devices: 1.4 us -> 4.87 us  [both_ways(): return lax.ppermute(v, AXES, pairs)]
    slice x2 -> x0, local copies, waits for them, and re-layouts: 2.56 us -> none  [the longest x1 1.76 us: on_device(): far_b = shift(after[CHUNK // 2:], dy=-1)]
    unnamed x32 -> x20, local copies, waits for them, and re-layouts: 7.63 us -> 6.03 us
    ppermute x15 -> x10, waiting for transfers between devices: 1.59 us -> 0.03 us  [shift(): return lax.ppermute(v, AXES, pairs)]
    pallas_call x1, Pallas kernels: 6.83 us -> 5.43 us  [rubric_part(): pl.pallas_call(rubric_kernel, out_shape=(jax.ShapeDtypeStruct((RESP, 256,...]
    dynamic_slice x1 -> x0, local copies, waits for them, and re-layouts: 1.05 us -> none  [on_device(): lax.dynamic_slice_in_dim(w_query, c * HALF_D, HALF_D, 0)]
  transfers between devices with their start and end apart: 18 -> 15, of which waited for: 2 -> 4; matrix products, arithmetic and copies ran while one was open for 10% -> 7% of each run, Pallas kernels for 16% -> 16%
where the time goes in v4:
time: 87.7 us; the launch traced here: 86.3 us
  starting transfers between devices  28.4 us (32%)
  blocking collectives  19.5 us (22%)
  Pallas kernels  17.8 us (20%)
  local copies, waits for them, and re-layouts  9.34 us (11%)
  waiting for transfers between devices  4.9 us (6%)
  other arithmetic  3.34 us (4%)
  between operations  2.97 us (3%)
    all_to_all x1, blocking collectives, on_device(): lax.all_to_all(ready.reshape(32, 64, HD), AXES, 0, 0, tiled=True, axis_in...  19.5 us
    ppermute x10, starting transfers between devices, shift(): return lax.ppermute(v, AXES, pairs)  13.1 us
    ppermute x4, starting transfers between devices, both_ways(): return lax.ppermute(v, AXES, pairs)  11.7 us
    unnamed x20, local copies, waits for them, and re-layouts  6.03 us
    pallas_call x1, Pallas kernels, rubric_part(): pl.pallas_call(rubric_kernel, out_shape=(jax.ShapeDtypeStruct((RESP, 256,...  5.43 us
    ppermute x4, waiting for transfers between devices, both_ways(): return lax.ppermute(v, AXES, pairs)  4.87 us
    pallas_call x2, Pallas kernels, keys_values(): pl.pallas_call(kernel, out_shape=(jax.ShapeDtypeStruct((RESP, 64, 2 * HD)...  4.53 us
    pallas_call x1, Pallas kernels, self_part(): pl.pallas_call(self_kernel, out_shape=jax.ShapeDtypeStruct((GROUPS, 4, 64...  4.31 us
  transfers between devices with their start and end apart: 15, of which 4 were waited for; matrix products, arithmetic and copies ran while one was open for 7% of the time, Pallas kernels for 16%

profile of v4, /device:TPU:1, one launch (start us, length us, event | category | flops | bytes accessed | tf_op | source)
XLA Modules:
  0.0 86.3 jit_solution(17656131719010874809)
XLA Ops:
  0.0 1.4 %collective-permute-start.3 = (bf16[4,128,256]{2,1,0:T(8,128)(2,1)}, bf16[4,128,256]{2,1,0:T(8,128)(2,1)S(1)}, u32[]{:S(2)}, u32[]{:S(2)}) collective-permute-start(bf16[4,128,256]{2,1,0:T(8,128)(2,1)} %bitcast.41), channel_id=1, source_target_pairs={{0,16},{16,0},{32,48},{48,32},{64,80},{80,64},{96,112},{112,96},{4... | collective-permute-start | bytes 786440 | tf_op jit(solution)/shard_map/ppermute | solution.py:39
  1.4 1.4 %collective-permute-start = (bf16[96,3584]{1,0:T(8,128)(2,1)}, bf16[96,3584]{1,0:T(8,128)(2,1)}, u32[]{:S(2)}, u32[]{:S(2)}) collective-permute-start(bf16[96,3584]{1,0:T(8,128)(2,1)} %bitcast.27), channel_id=1, source_target_pairs={{0,4},{16,20},{32,36},{48,52},{64,68},{80,84},{96,100},{112,116},{... | collective-permute-start | bytes 2064392 | tf_op jit(solution)/shard_map/ppermute | solution.py:39
  2.8 1.4 %collective-permute-start.1 = (bf16[96,3584]{1,0:T(8,128)(2,1)}, bf16[96,3584]{1,0:T(8,128)(2,1)}, u32[]{:S(2)}, u32[]{:S(2)}) collective-permute-start(bf16[96,3584]{1,0:T(8,128)(2,1)} %bitcast.28), channel_id=1, source_target_pairs={{0,12},{16,28},{32,44},{48,60},{64,76},{80,92},{96,108},{112,124},... | collective-permute-start | bytes 2064392 | tf_op jit(solution)/shard_map/ppermute | solution.py:39
  4.2 1.6 %collective-permute-start.2 = (bf16[96,3584]{1,0:T(8,128)(2,1)}, bf16[96,3584]{1,0:T(8,128)(2,1)}, u32[]{:S(2)}, u32[]{:S(2)}) collective-permute-start(bf16[96,3584]{1,0:T(8,128)(2,1)} %bitcast.29), channel_id=1, source_target_pairs={{0,8},{16,24},{32,40},{48,56},{64,72},{80,88},{96,104},{112,120},{... | collective-permute-start | bytes 2064392 | tf_op jit(solution)/shard_map/ppermute | solution.py:39
  7.9 0.0 collective-permute-done.3
  7.9 1.0 %broadcast_select_fusion = bf16[4,128,256]{2,1,0:T(8,128)(2,1)S(1)} fusion(bf16[4,128,256]{2,1,0:T(8,128)(2,1)S(1)} %collective-permute-done.3, pred[]{:T(512)S(6)} %eq.25, bf16[1,4,128,256]{3,2,1,0:T(8,128)(2,1)} %param.19), kind=kLoop, calls=%fused_computation.1 | loop fusion | flops 131072 | bytes 786433 | tf_op jit(solution)/shard_map/jit(_where)/select_n | solution.py:281
  8.8 3.8 %collective-permute-start.4 = (bf16[4,128,256]{2,1,0:T(8,128)(2,1)S(1)}, bf16[4,128,256]{2,1,0:T(8,128)(2,1)S(1)}, u32[]{:S(2)}, u32[]{:S(2)}) collective-permute-start(bf16[4,128,256]{2,1,0:T(8,128)(2,1)S(1)} %broadcast_select_fusion), channel_id=1, source_target_pairs={{0,32},{16,112},{32,64},{48,16},{64,96},{80,48},{96,0},{112,80},{4... | collective-permute-start | bytes 786440 | tf_op jit(solution)/shard_map/ppermute | solution.py:51
  12.7 0.7 fusion.8
  13.4 2.6 %collective-permute-done.4 = bf16[4,128,256]{2,1,0:T(8,128)(2,1)S(1)} collective-permute-done((bf16[4,128,256]{2,1,0:T(8,128)(2,1)S(1)}, bf16[4,128,256]{2,1,0:T(8,128)(2,1)S(1)}, u32[]{:S(2)}, u32[]{:S(2)}) %collective-permute-start.4) | collective-permute-done | bytes 262176 | tf_op jit(solution)/shard_map/ppermute | solution.py:51
  16.0 2.2 %collective-permute-start.5 = (bf16[4,128,256]{2,1,0:T(8,128)(2,1)S(1)}, bf16[4,128,256]{2,1,0:T(8,128)(2,1)S(1)}, u32[]{:S(2)}, u32[]{:S(2)}) collective-permute-start(bf16[4,128,256]{2,1,0:T(8,128)(2,1)S(1)} %collective-permute-done.4), channel_id=1, source_target_pairs={{0,16},{16,0},{32,48},{48,32},{64,80},{80,64},{96,112},{112,96},{4... | collective-permute-start | bytes 786440 | tf_op jit(solution)/shard_map/ppermute | solution.py:39
  18.2 1.2 %pad_maximum_fusion.w0 = bf16[3600,128]{1,0:T(8,128)(2,1)S(1)} fusion(bf16[16,128]{1,0:T(8,128)(2,1)S(1)} %fusion.5, bf16[3584,128]{1,0:T(8,128)(2,1)} %param.13), kind=kLoop, calls=%fused_computation | loop fusion | flops 1843200 | bytes 1843200 | tf_op jit(solution)/shard_map/concatenate | solution.py:273
  19.4 0.0 copy-start.9
  19.4 0.0 copy-start.5
  19.4 0.0 copy-start.6
  19.4 2.5 %collective-permute-start.8 = (bf16[3600,128]{1,0:T(8,128)(2,1)S(1)}, bf16[3600,128]{1,0:T(8,128)(2,1)}, u32[]{:S(2)}, u32[]{:S(2)}) collective-permute-start(bf16[3600,128]{1,0:T(8,128)(2,1)S(1)} %pad_maximum_fusion.w0), channel_id=1, source_target_pairs={{0,1},{16,19},{32,33},{48,51},{64,65},{80,83},{96,97},{112,115},{4... | collective-permute-start | bytes 2764808 | tf_op jit(solution)/shard_map/ppermute | solution.py:51
  22.7 0.1 dynamic-slice_select_fusion
  22.8 1.8 %collective-permute-start.6 = (bf16[4,64,256]{2,1,0:T(8,128)(2,1)S(1)}, bf16[4,64,256]{2,1,0:T(8,128)(2,1)S(1)}, u32[]{:S(2)}, u32[]{:S(2)}) collective-permute-start(bf16[4,64,256]{2,1,0:T(8,128)(2,1)S(1)} %dynamic-slice_select_fusion), channel_id=1, source_target_pairs={{0,32},{16,112},{32,64},{48,16},{64,96},{80,48},{96,0},{112,80},{4... | collective-permute-start | bytes 393224 | tf_op jit(solution)/shard_map/ppermute | solution.py:51
  24.6 1.6 %constant_dynamic-slice_fusion = (bf16[3584,128]{1,0:T(8,128)(2,1)S(1)}, bf16[3584,128]{1,0:T(8,128)(2,1)S(1)}) fusion(bf16[3584,512]{1,0:T(8,128)(2,1)} %param.17, s32[]{:T(128)S(6)} %select_n.90, bf16[3584,512]{1,0:T(8,128)(2,1)} %param.15), kind=kLoop, calls=%fused_computation.18 | loop fusion | bytes 3670020 | tf_op jit(solution)/shard_map/dynamic_slice | solution.py:265
  26.2 0.9 collective-permute-done.6
  27.1 0.8 broadcast_in_dim.2
  27.9 3.6 %all-to-all-start = ((bf16[16,64,256]{2,1,0:T(8,128)(2,1)}), bf16[16,64,256]{2,1,0:T(8,128)(2,1)S(1)}, u32[]{:S(2)}, u32[]{:S(2)}) async-start(bf16[16,64,256]{2,1,0:T(8,128)(2,1)} %bitcast.39), calls=%async_computation | async-start | bytes 1048576 | tf_op jit(solution)/shard_map/all_to_all | solution.py:290
  31.6 0.2 fusion
  31.8 0.6 collective-permute-done.8.w1
  32.4 3.5 %collective-permute-start.10 = (bf16[3600,128]{1,0:T(8,128)(2,1)}, bf16[3600,128]{1,0:T(8,128)(2,1)}, u32[]{:S(2)}, u32[]{:S(2)}) collective-permute-start(bf16[3600,128]{1,0:T(8,128)(2,1)} %collective-permute-done.8.w1), channel_id=1, source_target_pairs={{0,1},{16,19},{32,33},{48,51},{64,65},{80,83},{96,97},{112,115},{4... | collective-permute-start | bytes 2764808 | tf_op jit(solution)/shard_map/ppermute | solution.py:51
  35.9 0.4 collective-permute-start.9
  36.3 0.1 pad_add_fusion.meta
  36.3 0.1 pad_maximum_fusion.1
  36.4 0.0 collective-permute-done.1.after
  36.5 0.0 copy-start.2
  36.5 1.1 %copy-done.2 = bf16[6,16,3584]{2,1,0:T(8,128)(2,1)S(1)} copy-done((bf16[6,16,3584]{2,1,0:T(8,128)(2,1)S(1)}, bf16[6,16,3584]{2,1,0:T(8,128)(2,1)}, u32[]{:S(2)}) %copy-start.2) | copy-done | bytes 688152
  37.6 2.7 %near_rows.1 = (bf16[6,64,256]{2,1,0:T(8,128)(2,1)S(1)}, bf16[288,3584]{1,0:T(8,128)(2,1)S(1)}) custom-call(s32[4]{0:T(128)S(1)} %pad_add_fusion.meta, bf16[96,3584]{1,0:T(8,128)(2,1)S(1)} %bitcast.30, bf16[96,3584]{1,0:T(8,128)(2,1)} %collective-permute-done.before, bf16[96,3584]{1,0:T(8,128)(2,1)} %collective-permute-done.1.after, ...), custom_call_target="tpu_custom_call" | custom-call | tf_op jit(solution)/shard_map/near_rows/pallas_call | solution.py:117
  40.3 1.3 %copy-done = bf16[288,3584]{1,0:T(8,128)(2,1)} copy-done((bf16[288,3584]{1,0:T(8,128)(2,1)}, bf16[288,3584]{1,0:T(8,128)(2,1)S(1)}, u32[]{:S(2)}) %copy-start) | copy-done | bytes 2064408
  41.6 0.0 collective-permute-done.2.far
  41.6 1.8 %far_rows.1 = (bf16[6,64,256]{2,1,0:T(8,128)(2,1)S(1)}, bf16[96,3584]{1,0:T(8,128)(2,1)S(1)}) custom-call(s32[4]{0:T(128)S(1)} %pad_add_fusion.meta, bf16[6,64,256]{2,1,0:T(8,128)(2,1)S(1)} %get-tuple-element.14.near, bf16[96,3584]{1,0:T(8,128)(2,1)} %collective-permute-done.2.far, f32[1,3584]{1,0:T(1,128)S(1)} %reshape.59.gain, ...), custom_call_target="tpu_custom_call" | custom-call | tf_op jit(solution)/shard_map/far_rows/pallas_call | solution.py:117
  43.5 0.9 %copy-done.3 = bf16[96,3584]{1,0:T(8,128)(2,1)} copy-done((bf16[96,3584]{1,0:T(8,128)(2,1)}, bf16[96,3584]{1,0:T(8,128)(2,1)S(1)}, u32[]{:S(2)}) %copy-start.3) | copy-done | bytes 688152
  44.4 0.1 collective-permute-start.7
  44.5 2.8 %collective-permute-start.11 = (bf16[6,64,256]{2,1,0:T(8,128)(2,1)S(1)}, bf16[6,64,256]{2,1,0:T(8,128)(2,1)S(1)}, u32[]{:S(2)}, u32[]{:S(2)}) collective-permute-start(bf16[6,64,256]{2,1,0:T(8,128)(2,1)S(1)} %get-tuple-element.16.kv0), channel_id=1, source_target_pairs={{0,1},{16,17},{32,33},{48,49},{64,65},{80,81},{96,97},{112,113},{4... | collective-permute-start | bytes 589832 | tf_op jit(solution)/shard_map/ppermute | solution.py:39
  47.3 0.0 collective-permute-start.12
  47.3 0.0 collective-permute-done.7.c_other
  47.3 1.8 %collective-permute-start.13 = (bf16[6,64,256]{2,1,0:T(8,128)(2,1)S(1)}, bf16[6,64,256]{2,1,0:T(8,128)(2,1)S(1)}, u32[]{:S(2)}, u32[]{:S(2)}) collective-permute-start(bf16[6,64,256]{2,1,0:T(8,128)(2,1)S(1)} %get-tuple-element.16.kv0), channel_id=1, source_target_pairs={{0,2},{16,18},{32,34},{48,50},{64,66},{80,82},{96,98},{112,114},{4... | collective-permute-start | bytes 589832 | tf_op jit(solution)/shard_map/ppermute | solution.py:39
  49.1 0.8 collective-permute-done.10.w3
  49.9 1.6 %copy-done.1 = bf16[288,3584]{1,0:T(8,128)(2,1)S(1)} copy-done((bf16[288,3584]{1,0:T(8,128)(2,1)S(1)}, bf16[288,3584]{1,0:T(8,128)(2,1)}, u32[]{:S(2)}) %copy-start.1) | copy-done | bytes 2064408
  51.4 1.1 %copy-done.4 = bf16[96,3584]{1,0:T(8,128)(2,1)S(1)} copy-done((bf16[96,3584]{1,0:T(8,128)(2,1)S(1)}, bf16[96,3584]{1,0:T(8,128)(2,1)}, u32[]{:S(2)}) %copy-start.4) | copy-done | bytes 688152
  52.5 3.5 %queries.1.q_ref = bf16[6,4,64,128]{3,2,1,0:T(8,128)(2,1)S(1)} custom-call(s32[4]{0:T(128)S(1)} %pad_add_fusion.meta, bf16[288,3584]{1,0:T(8,128)(2,1)S(1)} %copy-done.1, bf16[96,3584]{1,0:T(8,128)(2,1)S(1)} %copy-done.4, bf16[3600,128]{1,0:T(8,128)(2,1)S(1)} %pad_maximum_fusion.w0, bf16[3600,128]{1,0:T(8,128)(2,1)} %collective-permute-done.8.w1, ...), custom_call_target="tpu_custom_call" | custom-call | tf_op jit(solution)/shard_map/queries/pallas_call | solution.py:153
  56.1 5.4 %rubric_part.1 = (f32[6,256,128]{2,1,0:T(8,128)S(1)}, f32[6,256,128]{2,1,0:T(8,128)S(1)}) custom-call(bf16[6,4,64,128]{3,2,1,0:T(8,128)(2,1)S(1)} %queries.1.q_ref, bf16[1024,256]{1,0:T(8,128)(2,1)S(1)} %bitcast.26, bf16[1024,256]{1,0:T(8,128)(2,1)S(1)} %collective-permute-done.7.c_other), custom_call_target="tpu_custom_call" | custom-call | tf_op jit(solution)/shard_map/rubric_part/pallas_call | solution.py:182
  61.6 4.3 %self_part.1 = bf16[8,4,64,128]{3,2,1,0:T(8,128)(2,1)S(1)} custom-call(s32[4]{0:T(128)S(1)} %pad_add_fusion.meta, s32[48]{0:T(128)S(1)} %copy-done.7, s32[48]{0:T(128)S(1)} %copy-done.8, bf16[6,4,64,128]{3,2,1,0:T(8,128)(2,1)S(1)} %queries.1.q_ref, f32[6,256,128]{2,1,0:T(8,128)S(1)} %get-tuple-element.19.acc_ref, ...), custom_call_target="tpu_custom_call" | custom-call | tf_op jit(solution)/shard_map/self_part/pallas_call | solution.py:230
  65.9 19.5 %all_to_all.10 = bf16[32,64,128]{2,1,0:T(8,128)(2,1)S(1)} all-to-all(bf16[32,64,128]{2,1,0:T(8,128)(2,1)S(1)} %bitcast.24), channel_id=1, replica_groups={{0,1,2,3,16,17,18,19,32,33,34,35,48,49,50,51,64,65,66,67,80,81,82,83,96..., dimensions={0} | all-to-all | bytes 1048576 | tf_op jit(solution)/shard_map/all_to_all | solution.py:304
  85.4 0.9 copy.12
  (23 shorter events, 0.1 us)
Async XLA Ops:
  0.0 7.9 %collective-permute-start.3 = (bf16[4,128,256]{2,1,0:T(8,128)(2,1)}, bf16[4,128,256]{2,1,0:T(8,128)(2,1)S(1)}, u32[]{:S(2)}, u32[]{:S(2)}) collective-permute-start(bf16[4,128,256]{2,1,0:T(8,128)(2,1)} %bitcast.41), channel_id=1, source_target_pairs={{0,16},{16,0},{32,48},{48,32},{64,80},{80,64},{96,112},{112,96},{4... | collective-permute-start | bytes 786440 | tf_op jit(solution)/shard_map/ppermute | solution.py:39
  1.4 35.0 %collective-permute-start = (bf16[96,3584]{1,0:T(8,128)(2,1)}, bf16[96,3584]{1,0:T(8,128)(2,1)}, u32[]{:S(2)}, u32[]{:S(2)}) collective-permute-start(bf16[96,3584]{1,0:T(8,128)(2,1)} %bitcast.27), channel_id=1, source_target_pairs={{0,4},{16,20},{32,36},{48,52},{64,68},{80,84},{96,100},{112,116},{... | collective-permute-start | bytes 2064392 | tf_op jit(solution)/shard_map/ppermute | solution.py:39
  2.8 33.6 %collective-permute-start.1 = (bf16[96,3584]{1,0:T(8,128)(2,1)}, bf16[96,3584]{1,0:T(8,128)(2,1)}, u32[]{:S(2)}, u32[]{:S(2)}) collective-permute-start(bf16[96,3584]{1,0:T(8,128)(2,1)} %bitcast.28), channel_id=1, source_target_pairs={{0,12},{16,28},{32,44},{48,60},{64,76},{80,92},{96,108},{112,124},... | collective-permute-start | bytes 2064392 | tf_op jit(solution)/shard_map/ppermute | solution.py:39
  4.2 37.4 %collective-permute-start.2 = (bf16[96,3584]{1,0:T(8,128)(2,1)}, bf16[96,3584]{1,0:T(8,128)(2,1)}, u32[]{:S(2)}, u32[]{:S(2)}) collective-permute-start(bf16[96,3584]{1,0:T(8,128)(2,1)} %bitcast.29), channel_id=1, source_target_pairs={{0,8},{16,24},{32,40},{48,56},{64,72},{80,88},{96,104},{112,120},{... | collective-permute-start | bytes 2064392 | tf_op jit(solution)/shard_map/ppermute | solution.py:39
  8.8 7.1 %collective-permute-start.4 = (bf16[4,128,256]{2,1,0:T(8,128)(2,1)S(1)}, bf16[4,128,256]{2,1,0:T(8,128)(2,1)S(1)}, u32[]{:S(2)}, u32[]{:S(2)}) collective-permute-start(bf16[4,128,256]{2,1,0:T(8,128)(2,1)S(1)} %broadcast_select_fusion), channel_id=1, source_target_pairs={{0,32},{16,112},{32,64},{48,16},{64,96},{80,48},{96,0},{112,80},{4... | collective-permute-start | bytes 786440 | tf_op jit(solution)/shard_map/ppermute | solution.py:51
  16.0 6.7 %collective-permute-start.5 = (bf16[4,128,256]{2,1,0:T(8,128)(2,1)S(1)}, bf16[4,128,256]{2,1,0:T(8,128)(2,1)S(1)}, u32[]{:S(2)}, u32[]{:S(2)}) collective-permute-start(bf16[4,128,256]{2,1,0:T(8,128)(2,1)S(1)} %collective-permute-done.4), channel_id=1, source_target_pairs={{0,16},{16,0},{32,48},{48,32},{64,80},{80,64},{96,112},{112,96},{4... | collective-permute-start | bytes 786440 | tf_op jit(solution)/shard_map/ppermute | solution.py:39
  19.4 12.1 %copy-start.9 = (f32[3584]{0:T(1024)S(1)}, f32[3584]{0:T(1024)}, u32[]{:S(2)}) copy-start(f32[3584]{0:T(1024)} %param.12) | copy-start | bytes 43012
  19.4 17.0 %copy-start.5 = (f32[512]{0:T(512)S(1)}, f32[512]{0:T(512)}, u32[]{:S(2)}) copy-start(f32[512]{0:T(512)} %param.16) | copy-start | bytes 6148
  19.4 17.0 %copy-start.6 = (f32[512]{0:T(512)S(1)}, f32[512]{0:T(512)}, u32[]{:S(2)}) copy-start(f32[512]{0:T(512)} %param.18) | copy-start | bytes 6148
  19.4 12.9 %collective-permute-start.8 = (bf16[3600,128]{1,0:T(8,128)(2,1)S(1)}, bf16[3600,128]{1,0:T(8,128)(2,1)}, u32[]{:S(2)}, u32[]{:S(2)}) collective-permute-start(bf16[3600,128]{1,0:T(8,128)(2,1)S(1)} %pad_maximum_fusion.w0), channel_id=1, source_target_pairs={{0,1},{16,19},{32,33},{48,51},{64,65},{80,83},{96,97},{112,115},{4... | collective-permute-start | bytes 2764808 | tf_op jit(solution)/shard_map/ppermute | solution.py:51
  22.8 4.3 %collective-permute-start.6 = (bf16[4,64,256]{2,1,0:T(8,128)(2,1)S(1)}, bf16[4,64,256]{2,1,0:T(8,128)(2,1)S(1)}, u32[]{:S(2)}, u32[]{:S(2)}) collective-permute-start(bf16[4,64,256]{2,1,0:T(8,128)(2,1)S(1)} %dynamic-slice_select_fusion), channel_id=1, source_target_pairs={{0,32},{16,112},{32,64},{48,16},{64,96},{80,48},{96,0},{112,80},{4... | collective-permute-start | bytes 393224 | tf_op jit(solution)/shard_map/ppermute | solution.py:51
  27.9 16.4 %all-to-all-start = ((bf16[16,64,256]{2,1,0:T(8,128)(2,1)}), bf16[16,64,256]{2,1,0:T(8,128)(2,1)S(1)}, u32[]{:S(2)}, u32[]{:S(2)}) async-start(bf16[16,64,256]{2,1,0:T(8,128)(2,1)} %bitcast.39), calls=%async_computation | async-start | bytes 1048576 | tf_op jit(solution)/shard_map/all_to_all | solution.py:290
  32.4 17.5 %collective-permute-start.10 = (bf16[3600,128]{1,0:T(8,128)(2,1)}, bf16[3600,128]{1,0:T(8,128)(2,1)}, u32[]{:S(2)}, u32[]{:S(2)}) collective-permute-start(bf16[3600,128]{1,0:T(8,128)(2,1)} %collective-permute-done.8.w1), channel_id=1, source_target_pairs={{0,1},{16,19},{32,33},{48,51},{64,65},{80,83},{96,97},{112,115},{4... | collective-permute-start | bytes 2764808 | tf_op jit(solution)/shard_map/ppermute | solution.py:51
  35.9 14.0 %collective-permute-start.9 = (bf16[3600,128]{1,0:T(8,128)(2,1)}, bf16[3600,128]{1,0:T(8,128)(2,1)}, u32[]{:S(2)}, u32[]{:S(2)}) collective-permute-start(bf16[3600,128]{1,0:T(8,128)(2,1)} %collective-permute-done.8.w1), channel_id=1, source_target_pairs={{0,16},{16,0},{32,48},{48,32},{64,80},{80,64},{96,112},{112,96},{4... | collective-permute-start | bytes 2764808 | tf_op jit(solution)/shard_map/ppermute | solution.py:39
  36.5 1.1 %copy-start.2 = (bf16[6,16,3584]{2,1,0:T(8,128)(2,1)S(1)}, bf16[6,16,3584]{2,1,0:T(8,128)(2,1)}, u32[]{:S(2)}) copy-start(bf16[6,16,3584]{2,1,0:T(8,128)(2,1)} %param.11) | copy-start | bytes 2064388
  40.3 1.3 %copy-start = (bf16[288,3584]{1,0:T(8,128)(2,1)}, bf16[288,3584]{1,0:T(8,128)(2,1)S(1)}, u32[]{:S(2)}) copy-start(bf16[288,3584]{1,0:T(8,128)(2,1)S(1)} %get-tuple-element.13.near) | copy-start | bytes 6193156
  43.5 0.9 %copy-start.3 = (bf16[96,3584]{1,0:T(8,128)(2,1)}, bf16[96,3584]{1,0:T(8,128)(2,1)S(1)}, u32[]{:S(2)}) copy-start(bf16[96,3584]{1,0:T(8,128)(2,1)S(1)} %get-tuple-element.18.far) | copy-start | bytes 2064388
  44.4 2.9 %collective-permute-start.7 = (bf16[1024,256]{1,0:T(8,128)(2,1)S(1)}, bf16[1024,256]{1,0:T(8,128)(2,1)S(1)}, u32[]{:S(2)}, u32[]{:S(2)}) collective-permute-start(bf16[1024,256]{1,0:T(8,128)(2,1)S(1)} %bitcast.25), channel_id=1, source_target_pairs={{0,16},{16,0},{32,48},{48,32},{64,80},{80,64},{96,112},{112,96},{4... | collective-permute-start | bytes 1572872 | tf_op jit(solution)/shard_map/ppermute | solution.py:39
  44.5 17.1 %collective-permute-start.11 = (bf16[6,64,256]{2,1,0:T(8,128)(2,1)S(1)}, bf16[6,64,256]{2,1,0:T(8,128)(2,1)S(1)}, u32[]{:S(2)}, u32[]{:S(2)}) collective-permute-start(bf16[6,64,256]{2,1,0:T(8,128)(2,1)S(1)} %get-tuple-element.16.kv0), channel_id=1, source_target_pairs={{0,1},{16,17},{32,33},{48,49},{64,65},{80,81},{96,97},{112,113},{4... | collective-permute-start | bytes 589832 | tf_op jit(solution)/shard_map/ppermute | solution.py:39
  47.3 14.3 %collective-permute-start.12 = (bf16[6,64,256]{2,1,0:T(8,128)(2,1)S(1)}, bf16[6,64,256]{2,1,0:T(8,128)(2,1)S(1)}, u32[]{:S(2)}, u32[]{:S(2)}) collective-permute-start(bf16[6,64,256]{2,1,0:T(8,128)(2,1)S(1)} %get-tuple-element.16.kv0), channel_id=1, source_target_pairs={{0,3},{16,19},{32,35},{48,51},{64,67},{80,83},{96,99},{112,115},{4... | collective-permute-start | bytes 589832 | tf_op jit(solution)/shard_map/ppermute | solution.py:39
  47.3 14.3 %collective-permute-start.13 = (bf16[6,64,256]{2,1,0:T(8,128)(2,1)S(1)}, bf16[6,64,256]{2,1,0:T(8,128)(2,1)S(1)}, u32[]{:S(2)}, u32[]{:S(2)}) collective-permute-start(bf16[6,64,256]{2,1,0:T(8,128)(2,1)S(1)} %get-tuple-element.16.kv0), channel_id=1, source_target_pairs={{0,2},{16,18},{32,34},{48,50},{64,66},{80,82},{96,98},{112,114},{4... | collective-permute-start | bytes 589832 | tf_op jit(solution)/shard_map/ppermute | solution.py:39
  49.9 1.6 %copy-start.1 = (bf16[288,3584]{1,0:T(8,128)(2,1)S(1)}, bf16[288,3584]{1,0:T(8,128)(2,1)}, u32[]{:S(2)}) copy-start(bf16[288,3584]{1,0:T(8,128)(2,1)} %copy-done) | copy-start | bytes 6193156
  51.4 1.1 %copy-start.4 = (bf16[96,3584]{1,0:T(8,128)(2,1)S(1)}, bf16[96,3584]{1,0:T(8,128)(2,1)}, u32[]{:S(2)}) copy-start(bf16[96,3584]{1,0:T(8,128)(2,1)} %copy-done.3) | copy-start | bytes 2064388
  52.5 9.0 %copy-start.7 = (s32[48]{0:T(128)S(1)}, s32[48]{0:T(128)}, u32[]{:S(2)}) copy-start(s32[48]{0:T(128)} %dest.1) | copy-start | bytes 580
  52.5 9.0 %copy-start.8 = (s32[48]{0:T(128)S(1)}, s32[48]{0:T(128)}, u32[]{:S(2)}) copy-start(s32[48]{0:T(128)} %lengths.1) | copy-start | bytes 580

commit v5 on v4

--- a/solution.py
+++ b/solution.py
@@ -39,14 +39,14 @@
     return lax.ppermute(v, AXES, pairs)
 
 
-def both_ways(v, axis):
+def both_ways(v, axis, step=1):
     pairs = []
     for x in range(4):
         for y in range(4):
             for z in range(4):
                 for c in range(2):
                     at = {"x": x, "y": y, "z": z}
-                    at[axis] = (at[axis] + 1 - 2 * c) % 4
+                    at[axis] = (at[axis] + step * (1 - 2 * c)) % 4
                     pairs.append((device_number(x, y, z, c), device_number(**at, c=c)))
     return lax.ppermute(v, AXES, pairs)
 
@@ -107,9 +107,10 @@
     project(meta[0], rows[...], (0, 1, 2), wk, wv, bk, bv, cos_ref, sin_ref, out)
 
 
-def far_kernel(meta, near, far, gain, wk, wv, bk, bv, cos_ref, sin_ref, out, rows):
+def far_kernel(meta, near, far_a, far_b, gain, wk, wv, bk, bv, cos_ref, sin_ref, out, rows):
     out[...] = near[...]
-    rows[...] = norm(far[...], gain[...])
+    rows[0 : CHUNK // 2, :] = norm(far_a[...], gain[...])
+    rows[CHUNK // 2 : CHUNK, :] = norm(far_b[...], gain[...])
     project(meta[0], rows[...], (3,), wk, wv, bk, bv, cos_ref, sin_ref, out)
 
 
@@ -161,80 +162,51 @@
     )(meta, near, far, *weights, cos, sin)
 
 
-def rubric_kernel(q_ref, c_mine, c_other, acc_out, stat_out):
-    def step(i, carry):
-        q = q_ref[i].reshape(4 * 64, HD)
-        keys = jnp.concatenate([c_mine[:, :HD], c_other[:, :HD]], axis=0)
-        scores = lax.dot_general(q, keys, (((1,), (1,)), ((), ())), preferred_element_type=jnp.float32)
-        top = jnp.max(scores, axis=-1, keepdims=True)
-        weights = jnp.exp2(scores * (SCALE * LOG2E) - top * (SCALE * LOG2E))
-        total = jnp.sum(weights, axis=-1, keepdims=True)
-        values = jnp.concatenate([c_mine[:, HD:], c_other[:, HD:]], axis=0)
-        acc_out[i] = jnp.dot(weights.astype(jnp.bfloat16), values, preferred_element_type=jnp.float32)
-        lane = lax.broadcasted_iota(jnp.int32, (4 * 64, HD), 1)
-        stat_out[i] = jnp.where(lane < 64, top, total)
-        return carry
-
-    lax.fori_loop(0, RESP, step, 0, unroll=True)
-
-
-def rubric_part(q, c_mine, c_other):
-    return pl.pallas_call(
-        rubric_kernel,
-        out_shape=(
-            jax.ShapeDtypeStruct((RESP, 256, HD), jnp.float32),
-            jax.ShapeDtypeStruct((RESP, 256, HD), jnp.float32),
-        ),
-        in_specs=[VMEM_SPEC] * 3,
-        out_specs=(VMEM_SPEC, VMEM_SPEC),
-        compiler_params=params(LIMIT),
-        name="rubric_part",
-    )(q, c_mine, c_other)
-
-
-def self_kernel(meta, dest, lengths, q_ref, acc_ref, stat_ref, kv0, kv1, kv2, kv3, out):
+def attend_kernel(meta, dest, lengths, q_ref, c_mine, c_other, kv0, kv1, kv2, kv3, out):
     x = meta[2]
     g = meta[3]
     out[...] = jnp.zeros_like(out)
-    row = lax.broadcasted_iota(jnp.int32, (256, 256), 0)
-    col = lax.broadcasted_iota(jnp.int32, (256, 256), 1)
-    slot_row = lax.rem(row, 64)
-    row_pos = (slot_row // 16) * 64 + x * 16 + lax.rem(slot_row, 16)
-    slot_col = lax.rem(col, 64)
-    which = col // 64
-    offset = jnp.where(which == 0, 0, jnp.where(which == 1, 3, jnp.where(which == 2, 1, 2)))
-    col_x = lax.rem(x + offset, 4)
-    col_pos = (slot_col // 16) * 64 + col_x * 16 + lax.rem(slot_col, 16)
+    row = lax.broadcasted_iota(jnp.int32, (256, 256), 0) & 63
+    col = lax.broadcasted_iota(jnp.int32, (1, 256), 1)
+    row_pos = (row >> 4) * 64 + x * 16 + (row & 15)
+    which = col >> 6
+    turn = jnp.where(which == 0, 0, jnp.where(which == 1, 3, jnp.where(which == 2, 1, 2)))
+    col_pos = ((col & 63) >> 4) * 64 + ((x + turn) & 3) * 16 + (col & 15)
     causal = col_pos <= row_pos
-    one_pos = row_pos[:, 0:HD]
+    keys = jnp.concatenate([c_mine[:, :HD], c_other[:, :HD]], axis=0)
+    values = jnp.concatenate([c_mine[:, HD:], c_other[:, HD:]], axis=0)
+    contract = (((1,), (1,)), ((), ()))
     for i in range(RESP):
         length = lengths[g * RESP + i]
         q = q_ref[i].reshape(256, HD)
-        keys = jnp.concatenate([kv0[i, :, :HD], kv1[i, :, :HD], kv2[i, :, :HD], kv3[i, :, :HD]], axis=0)
-        values = jnp.concatenate([kv0[i, :, HD:], kv1[i, :, HD:], kv2[i, :, HD:], kv3[i, :, HD:]], axis=0)
-        scores = lax.dot_general(q, keys, (((1,), (1,)), ((), ())), preferred_element_type=jnp.float32)
-        scores = jnp.where(causal & (col_pos < length), scores, -jnp.inf)
-        far_top = stat_ref[i, :, 0:1]
-        far_total = stat_ref[i, :, 64:65]
-        top = jnp.maximum(jnp.max(scores, axis=-1, keepdims=True), far_top)
-        weights = jnp.exp2((scores - top) * (SCALE * LOG2E))
-        factor = jnp.exp2((far_top - top) * (SCALE * LOG2E))
-        total = jnp.sum(weights, axis=-1, keepdims=True) + far_total * factor
-        near = jnp.dot(weights.astype(jnp.bfloat16), values, preferred_element_type=jnp.float32)
-        mixed = (acc_ref[i] * factor + near) / total
-        mixed = jnp.where(one_pos < length, mixed, 0.0).astype(jnp.bfloat16)
+        self_keys = jnp.concatenate([ref[i, :, :HD] for ref in (kv0, kv1, kv2, kv3)], axis=0)
+        self_values = jnp.concatenate([ref[i, :, HD:] for ref in (kv0, kv1, kv2, kv3)], axis=0)
+        far = lax.dot_general(q, keys, contract, preferred_element_type=jnp.float32)
+        near = lax.dot_general(q, self_keys, contract, preferred_element_type=jnp.float32)
+        near = jnp.where(causal & (col_pos < length), near, -jnp.inf)
+        top = jnp.maximum(
+            jnp.max(far, axis=-1, keepdims=True), jnp.max(near, axis=-1, keepdims=True)
+        ) * (SCALE * LOG2E)
+        far = jnp.exp2(far * (SCALE * LOG2E) - top)
+        near = jnp.exp2(near * (SCALE * LOG2E) - top)
+        total = jnp.sum(far, axis=-1, keepdims=True) + jnp.sum(near, axis=-1, keepdims=True)
+        mixed = jnp.dot(far.astype(jnp.bfloat16), values, preferred_element_type=jnp.float32)
+        mixed = mixed + jnp.dot(
+            near.astype(jnp.bfloat16), self_values, preferred_element_type=jnp.float32
+        )
+        mixed = jnp.where(row_pos[:, 0:HD] < length, mixed / total, 0.0).astype(jnp.bfloat16)
         out[dest[g * RESP + i]] = mixed.reshape(4, 64, HD)
 
 
-def self_part(meta, dest, lengths, q, acc, stat, parts):
+def attend(meta, dest, lengths, q, c_mine, c_other, parts):
     return pl.pallas_call(
-        self_kernel,
+        attend_kernel,
         out_shape=jax.ShapeDtypeStruct((GROUPS, 4, 64, HD), jnp.bfloat16),
         in_specs=[SMEM_SPEC] * 3 + [VMEM_SPEC] * 7,
         out_specs=VMEM_SPEC,
         compiler_params=params(LIMIT),
-        name="self_part",
-    )(meta, dest, lengths, q, acc, stat, *parts)
+        name="attend",
+    )(meta, dest, lengths, q, c_mine, c_other, *parts)
 
 
 def on_device(
@@ -250,7 +222,8 @@
     gain = gain.reshape(1, D)
     before = shift(own, dy=1)
     after = shift(own, dy=-1)
-    far = shift(own, dy=2)
+    far_a = shift(before[: CHUNK // 2], dy=1)
+    far_b = shift(after[CHUNK // 2 :], dy=-1)
 
     frequency = jnp.exp(jnp.arange(64, dtype=jnp.float32) * (-2.0 * math.log(THETA) / HD))
     slot = jnp.arange(64, dtype=jnp.int32)
@@ -279,28 +252,31 @@
     cache = rubric_cache[0]
     swapped = shift(cache, flip=1)
     cache = jnp.where(owner % 2 == c, cache, swapped)
+    piece = lax.dynamic_slice_in_dim(cache, c * 64, 64, 1)
     beside = both_ways(cache, "z")
-    across = shift(beside, flip=1)
+    z_far = shift(piece, dz=2)
+    for_other = lax.dynamic_slice_in_dim(beside, (1 - c) * 64, 64, 1)
+    beside = lax.dynamic_slice_in_dim(beside, c * 64, 64, 1)
+    from_other = shift(for_other, flip=1)
     turn = (owner // 2 - z) % 4
     here = jnp.where(c == 0, 3, 1)
-    cache = jnp.where(turn == here, beside, jnp.where(turn == 4 - here, across, cache))
-    piece = lax.dynamic_slice_in_dim(cache, c * 64, 64, 1)
-    piece = jnp.where(turn == 2, both_ways(piece, "z"), piece)
+    piece = jnp.where(
+        turn == 0, piece, jnp.where(turn == 2, z_far, jnp.where(turn == here, beside, from_other))
+    )
     spread = jnp.broadcast_to(piece[:, None], (4, 4, 64, 2 * HD)).reshape(16, 64, 2 * HD)
     c_mine = lax.all_to_all(spread, "mp", 0, 0, tiled=True).reshape(1024, 2 * HD)
 
     kv, near_rows = keys_values(
         near_kernel, "near_rows", 3 * CHUNK, meta, (own, before, after), small
     )
-    kv, far_rows = keys_values(far_kernel, "far_rows", CHUNK, meta, (kv, far), small)
+    kv, far_rows = keys_values(far_kernel, "far_rows", CHUNK, meta, (kv, far_a, far_b), small)
     c_mine, _ = lax.optimization_barrier((c_mine, kv))
     c_other = shift(c_mine, flip=1)
     parts = (kv, shift(kv, dx=1), shift(kv, dx=-1), shift(kv, dx=2))
     far_rows, _ = lax.optimization_barrier((far_rows, c_other))
     weights = (w_own, w_beside, w_across, w_far)
     q = make_queries(meta, near_rows, far_rows, weights, cos, sin)
-    acc, stat = rubric_part(q, c_mine, c_other)
-    ready = self_part(meta, dest_of, lengths, q, acc, stat, parts)
+    ready = attend(meta, dest_of, lengths, q, c_mine, c_other, parts)
     arrived = lax.all_to_all(
         ready.reshape(32, 64, HD), AXES, 0, 0, tiled=True, axis_index_groups=SCORE_X_GROUPS
     )

time: 87.7 us -> 84.4 us (0.962)
  Pallas kernels: 17.8 us -> 13.6 us
  local copies, waits for them, and re-layouts: 9.34 us -> 13.4 us
  blocking collectives: 19.5 us -> 16.6 us
  waiting for transfers between devices: 4.9 us -> 6.12 us
  other arithmetic: 3.34 us -> 4.52 us
  starting transfers between devices: 28.4 us -> 27.3 us
    ppermute x10 -> x12, waiting for transfers between devices: 0.03 us -> 6.11 us  [shift(): return lax.ppermute(v, AXES, pairs)]
    ppermute x4 -> x3, waiting for transfers between devices: 4.87 us -> 0.01 us  [both_ways(): return lax.ppermute(v, AXES, pairs)]
    pallas_call x2 -> x1, Pallas kernels: 9.73 us -> 6.23 us  [attend(): pl.pallas_call(attend_kernel, out_shape=jax.ShapeDtypeStruct((GROUPS, 4,...]
    all_to_all x1, blocking collectives: 19.5 us -> 16.6 us  [on_device(): lax.all_to_all(ready.reshape(32, 64, HD), AXES, 0, 0, tiled=True, axis_in...]
    ppermute x4 -> x3, starting transfers between devices: 11.7 us -> 9.31 us  [both_ways(): return lax.ppermute(v, AXES, pairs)]
    slice x0 -> x2, local copies, waits for them, and re-layouts: none -> 2 us  [the longest x1 1 us: on_device(): far_a = shift(before[:CHUNK // 2], dy=1)]
    dynamic_slice x0 -> x2, local copies, waits for them, and re-layouts: none -> 1.34 us  [the longest x1 0.68 us: on_device(): for_other = lax.dynamic_slice_in_dim(beside, (1 - c) * 64, 64, 1)]
    ppermute x10 -> x12, starting transfers between devices: 13.1 us -> 13.6 us  [shift(): return lax.ppermute(v, AXES, pairs)]
  transfers between devices with their start and end apart: 15 -> 16, of which waited for: 4 -> 3; matrix products, arithmetic and copies ran while one was open for 7% -> 13% of each run, Pallas kernels for 16% -> 9%
where the time goes in v5:
time: 84.4 us; the launch traced here: 83.7 us
  starting transfers between devices  27.3 us (32%)
  blocking collectives  16.6 us (20%)
  Pallas kernels  13.6 us (16%)
  local copies, waits for them, and re-layouts  13.4 us (16%)
  waiting for transfers between devices  6.12 us (7%)
  other arithmetic  4.52 us (5%)
  between operations  2.26 us (3%)
    all_to_all x1, blocking collectives, on_device(): lax.all_to_all(ready.reshape(32, 64, HD), AXES, 0, 0, tiled=True, axis_in...  16.6 us
    ppermute x12, starting transfers between devices, shift(): return lax.ppermute(v, AXES, pairs)  13.6 us
    ppermute x3, starting transfers between devices, both_ways(): return lax.ppermute(v, AXES, pairs)  9.31 us
    pallas_call x1, Pallas kernels, attend(): pl.pallas_call(attend_kernel, out_shape=jax.ShapeDtypeStruct((GROUPS, 4,...  6.23 us
    ppermute x12, waiting for transfers between devices, shift(): return lax.ppermute(v, AXES, pairs)  6.11 us
    unnamed x20, local copies, waits for them, and re-layouts  6.02 us
    all_to_all x1, starting transfers between devices, on_device(): lax.all_to_all(spread, 'mp', 0, 0, tiled=True).reshape(1024, 2 * HD)  4.35 us
    pallas_call x2, Pallas kernels, keys_values(): pl.pallas_call(kernel, out_shape=(jax.ShapeDtypeStruct((RESP, 64, 2 * HD)...  3.86 us
  transfers between devices with their start and end apart: 16, of which 3 were waited for; matrix products, arithmetic and copies ran while one was open for 13% of the time, Pallas kernels for 9%

profile of v5, /device:TPU:1, one launch (start us, length us, event | category | flops | bytes accessed | tf_op | source)
XLA Modules:
  0.0 83.7 jit_solution(13923326541617655279)
XLA Ops:
  0.0 2.1 %collective-permute-start = (bf16[96,3584]{1,0:T(8,128)(2,1)}, bf16[96,3584]{1,0:T(8,128)(2,1)}, u32[]{:S(2)}, u32[]{:S(2)}) collective-permute-start(bf16[96,3584]{1,0:T(8,128)(2,1)} %bitcast.27), channel_id=1, source_target_pairs={{0,4},{16,20},{32,36},{48,52},{64,68},{80,84},{96,100},{112,116},{... | collective-permute-start | bytes 2064392 | tf_op jit(solution)/shard_map/ppermute | solution.py:39
  2.1 1.5 %collective-permute-start.1 = (bf16[96,3584]{1,0:T(8,128)(2,1)}, bf16[96,3584]{1,0:T(8,128)(2,1)}, u32[]{:S(2)}, u32[]{:S(2)}) collective-permute-start(bf16[96,3584]{1,0:T(8,128)(2,1)} %bitcast.28), channel_id=1, source_target_pairs={{0,12},{16,28},{32,44},{48,60},{64,76},{80,92},{96,108},{112,124},... | collective-permute-start | bytes 2064392 | tf_op jit(solution)/shard_map/ppermute | solution.py:39
  3.6 1.0 %collective-permute-start.4 = (bf16[4,128,256]{2,1,0:T(8,128)(2,1)}, bf16[4,128,256]{2,1,0:T(8,128)(2,1)S(1)}, u32[]{:S(2)}, u32[]{:S(2)}) collective-permute-start(bf16[4,128,256]{2,1,0:T(8,128)(2,1)} %bitcast.40), channel_id=1, source_target_pairs={{0,16},{16,0},{32,48},{48,32},{64,80},{80,64},{96,112},{112,96},{4... | collective-permute-start | bytes 786440 | tf_op jit(solution)/shard_map/ppermute | solution.py:39
  6.6 0.7 fusion.8
  7.3 1.0 %broadcast_select_fusion = bf16[4,128,256]{2,1,0:T(8,128)(2,1)S(1)} fusion(bf16[4,128,256]{2,1,0:T(8,128)(2,1)S(1)} %collective-permute-done.4, pred[]{:T(512)S(6)} %eq.23, bf16[1,4,128,256]{3,2,1,0:T(8,128)(2,1)} %param.19), kind=kLoop, calls=%fused_computation.1 | loop fusion | flops 131072 | bytes 786433 | tf_op jit(solution)/shard_map/jit(_where)/select_n | solution.py:254
  8.3 3.9 %collective-permute-start.6 = (bf16[4,128,256]{2,1,0:T(8,128)(2,1)S(1)}, bf16[4,128,256]{2,1,0:T(8,128)(2,1)S(1)}, u32[]{:S(2)}, u32[]{:S(2)}) collective-permute-start(bf16[4,128,256]{2,1,0:T(8,128)(2,1)S(1)} %broadcast_select_fusion), channel_id=1, source_target_pairs={{0,32},{16,112},{32,64},{48,16},{64,96},{80,48},{96,0},{112,80},{4... | collective-permute-start | bytes 786440 | tf_op jit(solution)/shard_map/ppermute | solution.py:51
  12.2 1.2 %pad_maximum_fusion.w0 = bf16[3600,128]{1,0:T(8,128)(2,1)S(1)} fusion(bf16[16,128]{1,0:T(8,128)(2,1)S(1)} %fusion.5, bf16[3584,128]{1,0:T(8,128)(2,1)} %param.13), kind=kLoop, calls=%fused_computation | loop fusion | flops 1843200 | bytes 1843200 | tf_op jit(solution)/shard_map/concatenate | solution.py:246
  13.5 2.5 %collective-permute-start.9 = (bf16[3600,128]{1,0:T(8,128)(2,1)S(1)}, bf16[3600,128]{1,0:T(8,128)(2,1)}, u32[]{:S(2)}, u32[]{:S(2)}) collective-permute-start(bf16[3600,128]{1,0:T(8,128)(2,1)S(1)} %pad_maximum_fusion.w0), channel_id=1, source_target_pairs={{0,1},{16,19},{32,33},{48,51},{64,65},{80,83},{96,97},{112,115},{4... | collective-permute-start | bytes 2764808 | tf_op jit(solution)/shard_map/ppermute | solution.py:51
  16.0 0.7 constant_dynamic-slice_fusion.1
  16.7 0.7 constant_dynamic-slice_fusion
  17.3 0.8 collective-permute-start.7
  18.1 1.6 %constant_dynamic-slice_fusion.2 = (bf16[3584,128]{1,0:T(8,128)(2,1)S(1)}, bf16[3584,128]{1,0:T(8,128)(2,1)S(1)}) fusion(bf16[3584,512]{1,0:T(8,128)(2,1)} %param.17, s32[]{:T(128)S(6)} %select_n.94, bf16[3584,512]{1,0:T(8,128)(2,1)} %param.15), kind=kLoop, calls=%fused_computation.18 | loop fusion | bytes 3670020 | tf_op jit(solution)/shard_map/dynamic_slice | solution.py:238
  19.8 0.6 multiply_exponential_fusion
  20.4 1.8 %collective-permute-done.5 = bf16[4,64,256]{2,1,0:T(8,128)(2,1)S(1)} collective-permute-done((bf16[4,64,256]{2,1,0:T(8,128)(2,1)}, bf16[4,64,256]{2,1,0:T(8,128)(2,1)S(1)}, u32[]{:S(2)}, u32[]{:S(2)}) %collective-permute-start.5) | collective-permute-done | bytes 131104 | tf_op jit(solution)/shard_map/ppermute | solution.py:39
  22.2 0.0 collective-permute-done.7
  22.2 0.1 select_select_fusion
  22.3 0.8 %broadcast_in_dim.2 = bf16[4,4,64,256]{3,2,1,0:T(8,128)(2,1)} broadcast(bf16[4,64,256]{2,1,0:T(8,128)(2,1)S(1)} %select_select_fusion), dimensions={0,2,3} | broadcast | bytes 655360 | tf_op jit(solution)/shard_map/broadcast_in_dim | solution.py:266
  23.1 4.3 %all-to-all-start = ((bf16[16,64,256]{2,1,0:T(8,128)(2,1)}), bf16[16,64,256]{2,1,0:T(8,128)(2,1)S(1)}, u32[]{:S(2)}, u32[]{:S(2)}) async-start(bf16[16,64,256]{2,1,0:T(8,128)(2,1)} %bitcast.38), calls=%async_computation | async-start | bytes 1048576 | tf_op jit(solution)/shard_map/all_to_all | solution.py:267
  27.5 0.7 reshape.59.gain
  28.2 0.0 collective-permute-done.before
  28.2 1.0 %slice.12 = bf16[48,3584]{1,0:T(8,128)(2,1)S(1)} slice(bf16[96,3584]{1,0:T(8,128)(2,1)} %collective-permute-done.before), slice={[0:48], [0:3584]} | slice | bytes 688128 | tf_op jit(solution)/shard_map/slice | solution.py:225
  29.2 1.4 %collective-permute-start.2 = (bf16[48,3584]{1,0:T(8,128)(2,1)S(1)}, bf16[48,3584]{1,0:T(8,128)(2,1)S(1)}, u32[]{:S(2)}, u32[]{:S(2)}) collective-permute-start(bf16[48,3584]{1,0:T(8,128)(2,1)S(1)} %slice.12), channel_id=1, source_target_pairs={{0,4},{16,20},{32,36},{48,52},{64,68},{80,84},{96,100},{112,116},{... | collective-permute-start | bytes 1032200 | tf_op jit(solution)/shard_map/ppermute | solution.py:39
  30.7 0.0 collective-permute-done.1.after
  30.7 1.0 %slice.13 = bf16[48,3584]{1,0:T(8,128)(2,1)S(1)} slice(bf16[96,3584]{1,0:T(8,128)(2,1)} %collective-permute-done.1.after), slice={[48:96], [0:3584]} | slice | bytes 688128 | tf_op jit(solution)/shard_map/slice | solution.py:226
  31.7 1.4 %collective-permute-start.3 = (bf16[48,3584]{1,0:T(8,128)(2,1)S(1)}, bf16[48,3584]{1,0:T(8,128)(2,1)S(1)}, u32[]{:S(2)}, u32[]{:S(2)}) collective-permute-start(bf16[48,3584]{1,0:T(8,128)(2,1)S(1)} %slice.13), channel_id=1, source_target_pairs={{0,12},{16,28},{32,44},{48,60},{64,76},{80,92},{96,108},{112,124},... | collective-permute-start | bytes 1032200 | tf_op jit(solution)/shard_map/ppermute | solution.py:39
  33.1 0.8 fusion
  33.9 1.3 %collective-permute-start.10 = (bf16[3600,128]{1,0:T(8,128)(2,1)}, bf16[3600,128]{1,0:T(8,128)(2,1)}, u32[]{:S(2)}, u32[]{:S(2)}) collective-permute-start(bf16[3600,128]{1,0:T(8,128)(2,1)} %collective-permute-done.9.w1), channel_id=1, source_target_pairs={{0,16},{16,0},{32,48},{48,32},{64,80},{80,64},{96,112},{112,96},{4... | collective-permute-start | bytes 2764808 | tf_op jit(solution)/shard_map/ppermute | solution.py:39
  35.2 2.8 %collective-permute-start.11 = (bf16[3600,128]{1,0:T(8,128)(2,1)}, bf16[3600,128]{1,0:T(8,128)(2,1)}, u32[]{:S(2)}, u32[]{:S(2)}) collective-permute-start(bf16[3600,128]{1,0:T(8,128)(2,1)} %collective-permute-done.9.w1), channel_id=1, source_target_pairs={{0,1},{16,19},{32,33},{48,51},{64,65},{80,83},{96,97},{112,115},{4... | collective-permute-start | bytes 2764808 | tf_op jit(solution)/shard_map/ppermute | solution.py:51
  38.1 0.1 pad_add_fusion.meta
  38.1 0.1 pad_maximum_fusion.1
  38.3 0.0 copy-start.2
  38.3 1.1 %copy-done.2 = bf16[6,16,3584]{2,1,0:T(8,128)(2,1)S(1)} copy-done((bf16[6,16,3584]{2,1,0:T(8,128)(2,1)S(1)}, bf16[6,16,3584]{2,1,0:T(8,128)(2,1)}, u32[]{:S(2)}) %copy-start.2) | copy-done | bytes 688152
  39.4 2.6 %near_rows.1 = (bf16[6,64,256]{2,1,0:T(8,128)(2,1)S(1)}, bf16[288,3584]{1,0:T(8,128)(2,1)S(1)}) custom-call(s32[4]{0:T(128)S(1)} %pad_add_fusion.meta, bf16[96,3584]{1,0:T(8,128)(2,1)S(1)} %bitcast.29, bf16[96,3584]{1,0:T(8,128)(2,1)} %collective-permute-done.before, bf16[96,3584]{1,0:T(8,128)(2,1)} %collective-permute-done.1.after, ...), custom_call_target="tpu_custom_call" | custom-call | tf_op jit(solution)/shard_map/near_rows/pallas_call | solution.py:118
  42.0 1.3 %copy-done = bf16[288,3584]{1,0:T(8,128)(2,1)} copy-done((bf16[288,3584]{1,0:T(8,128)(2,1)}, bf16[288,3584]{1,0:T(8,128)(2,1)S(1)}, u32[]{:S(2)}) %copy-start) | copy-done | bytes 2064408
  43.3 1.8 %collective-permute-done.2.far_a = bf16[48,3584]{1,0:T(8,128)(2,1)S(1)} collective-permute-done((bf16[48,3584]{1,0:T(8,128)(2,1)S(1)}, bf16[48,3584]{1,0:T(8,128)(2,1)S(1)}, u32[]{:S(2)}, u32[]{:S(2)}) %collective-permute-start.2) | collective-permute-done | bytes 344096 | tf_op jit(solution)/shard_map/ppermute | solution.py:39
  45.1 1.2 %far_rows.1 = (bf16[6,64,256]{2,1,0:T(8,128)(2,1)S(1)}, bf16[96,3584]{1,0:T(8,128)(2,1)S(1)}) custom-call(s32[4]{0:T(128)S(1)} %pad_add_fusion.meta, bf16[6,64,256]{2,1,0:T(8,128)(2,1)S(1)} %get-tuple-element.12.near, bf16[48,3584]{1,0:T(8,128)(2,1)S(1)} %collective-permute-done.2.far_a, bf16[48,3584]{1,0:T(8,128)(2,1)S(1)} %collective-permute-done.3.far_b, ...), custom_call_target="tpu_custom_call" | custom-call | tf_op jit(solution)/shard_map/far_rows/pallas_call | solution.py:118
  46.4 0.9 %copy-done.3 = bf16[96,3584]{1,0:T(8,128)(2,1)} copy-done((bf16[96,3584]{1,0:T(8,128)(2,1)}, bf16[96,3584]{1,0:T(8,128)(2,1)S(1)}, u32[]{:S(2)}) %copy-start.3) | copy-done | bytes 688152
  47.3 0.4 collective-permute-start.8
  47.7 0.8 collective-permute-start.12
  48.5 1.9 %collective-permute-start.13 = (bf16[6,64,256]{2,1,0:T(8,128)(2,1)S(1)}, bf16[6,64,256]{2,1,0:T(8,128)(2,1)S(1)}, u32[]{:S(2)}, u32[]{:S(2)}) collective-permute-start(bf16[6,64,256]{2,1,0:T(8,128)(2,1)S(1)} %get-tuple-element.14.kv0), channel_id=1, source_target_pairs={{0,3},{16,19},{32,35},{48,51},{64,67},{80,83},{96,99},{112,115},{4... | collective-permute-start | bytes 589832 | tf_op jit(solution)/shard_map/ppermute | solution.py:39
  50.4 0.9 %collective-permute-start.14 = (bf16[6,64,256]{2,1,0:T(8,128)(2,1)S(1)}, bf16[6,64,256]{2,1,0:T(8,128)(2,1)S(1)}, u32[]{:S(2)}, u32[]{:S(2)}) collective-permute-start(bf16[6,64,256]{2,1,0:T(8,128)(2,1)S(1)} %get-tuple-element.14.kv0), channel_id=1, source_target_pairs={{0,2},{16,18},{32,34},{48,50},{64,66},{80,82},{96,98},{112,114},{4... | collective-permute-start | bytes 589832 | tf_op jit(solution)/shard_map/ppermute | solution.py:39
  51.4 1.6 %copy-done.1 = bf16[288,3584]{1,0:T(8,128)(2,1)S(1)} copy-done((bf16[288,3584]{1,0:T(8,128)(2,1)S(1)}, bf16[288,3584]{1,0:T(8,128)(2,1)}, u32[]{:S(2)}) %copy-start.1) | copy-done | bytes 2064408
  52.9 1.1 %copy-done.4 = bf16[96,3584]{1,0:T(8,128)(2,1)S(1)} copy-done((bf16[96,3584]{1,0:T(8,128)(2,1)S(1)}, bf16[96,3584]{1,0:T(8,128)(2,1)}, u32[]{:S(2)}) %copy-start.4) | copy-done | bytes 688152
  54.0 3.5 %queries.1.q_ref = bf16[6,4,64,128]{3,2,1,0:T(8,128)(2,1)S(1)} custom-call(s32[4]{0:T(128)S(1)} %pad_add_fusion.meta, bf16[288,3584]{1,0:T(8,128)(2,1)S(1)} %copy-done.1, bf16[96,3584]{1,0:T(8,128)(2,1)S(1)} %copy-done.4, bf16[3600,128]{1,0:T(8,128)(2,1)S(1)} %pad_maximum_fusion.w0, bf16[3600,128]{1,0:T(8,128)(2,1)} %collective-permute-done.9.w1, ...), custom_call_target="tpu_custom_call" | custom-call | tf_op jit(solution)/shard_map/queries/pallas_call | solution.py:154
  57.6 2.5 %collective-permute-done.14.kv3 = bf16[6,64,256]{2,1,0:T(8,128)(2,1)S(1)} collective-permute-done((bf16[6,64,256]{2,1,0:T(8,128)(2,1)S(1)}, bf16[6,64,256]{2,1,0:T(8,128)(2,1)S(1)}, u32[]{:S(2)}, u32[]{:S(2)}) %collective-permute-start.14) | collective-permute-done | bytes 196640 | tf_op jit(solution)/shard_map/ppermute | solution.py:39
  60.1 6.2 %attend.1 = bf16[8,4,64,128]{3,2,1,0:T(8,128)(2,1)S(1)} custom-call(s32[4]{0:T(128)S(1)} %pad_add_fusion.meta, s32[48]{0:T(128)S(1)} %copy-done.8, s32[48]{0:T(128)S(1)} %copy-done.9, bf16[6,4,64,128]{3,2,1,0:T(8,128)(2,1)S(1)} %queries.1.q_ref, bf16[1024,256]{1,0:T(8,128)(2,1)S(1)} %bitcast.25, bf16[1024,256]{1,0:T(8,128)(2,1)S(1)} %collective-permute-done.8.c_other, ...), custom_call_target="tpu_custom_call" | custom-call | tf_op jit(solution)/shard_map/attend/pallas_call | solution.py:202
  66.3 16.6 %all_to_all.10 = bf16[32,64,128]{2,1,0:T(8,128)(2,1)S(1)} all-to-all(bf16[32,64,128]{2,1,0:T(8,128)(2,1)S(1)} %bitcast.26), channel_id=1, replica_groups={{0,1,2,3,16,17,18,19,32,33,34,35,48,49,50,51,64,65,66,67,80,81,82,83,96..., dimensions={0} | all-to-all | bytes 1048576 | tf_op jit(solution)/shard_map/all_to_all | solution.py:280
  82.9 0.9 %copy.12 = bf16[8,4,4,16,128]{4,3,1,2,0:T(8,128)(2,1)} copy(bf16[8,4,4,16,128]{4,3,2,1,0:T(8,128)(2,1)S(1)} %bitcast.39) | data formatting | bytes 1048576 | tf_op jit(solution)/shard_map/reshape | solution.py:283
  (27 shorter events, 0.1 us)
Async XLA Ops:
  0.0 19.7 %copy-start.7 = (s32[48]{0:T(128)S(1)}, s32[48]{0:T(128)}, u32[]{:S(2)}) copy-start(s32[48]{0:T(128)} %dest.1) | copy-start | bytes 580
  0.0 28.2 %collective-permute-start = (bf16[96,3584]{1,0:T(8,128)(2,1)}, bf16[96,3584]{1,0:T(8,128)(2,1)}, u32[]{:S(2)}, u32[]{:S(2)}) collective-permute-start(bf16[96,3584]{1,0:T(8,128)(2,1)} %bitcast.27), channel_id=1, source_target_pairs={{0,4},{16,20},{32,36},{48,52},{64,68},{80,84},{96,100},{112,116},{... | collective-permute-start | bytes 2064392 | tf_op jit(solution)/shard_map/ppermute | solution.py:39
  2.1 28.5 %collective-permute-start.1 = (bf16[96,3584]{1,0:T(8,128)(2,1)}, bf16[96,3584]{1,0:T(8,128)(2,1)}, u32[]{:S(2)}, u32[]{:S(2)}) collective-permute-start(bf16[96,3584]{1,0:T(8,128)(2,1)} %bitcast.28), channel_id=1, source_target_pairs={{0,12},{16,28},{32,44},{48,60},{64,76},{80,92},{96,108},{112,124},... | collective-permute-start | bytes 2064392 | tf_op jit(solution)/shard_map/ppermute | solution.py:39
  3.6 3.7 %collective-permute-start.4 = (bf16[4,128,256]{2,1,0:T(8,128)(2,1)}, bf16[4,128,256]{2,1,0:T(8,128)(2,1)S(1)}, u32[]{:S(2)}, u32[]{:S(2)}) collective-permute-start(bf16[4,128,256]{2,1,0:T(8,128)(2,1)} %bitcast.40), channel_id=1, source_target_pairs={{0,16},{16,0},{32,48},{48,32},{64,80},{80,64},{96,112},{112,96},{4... | collective-permute-start | bytes 786440 | tf_op jit(solution)/shard_map/ppermute | solution.py:39
  8.3 8.4 %collective-permute-start.6 = (bf16[4,128,256]{2,1,0:T(8,128)(2,1)S(1)}, bf16[4,128,256]{2,1,0:T(8,128)(2,1)S(1)}, u32[]{:S(2)}, u32[]{:S(2)}) collective-permute-start(bf16[4,128,256]{2,1,0:T(8,128)(2,1)S(1)} %broadcast_select_fusion), channel_id=1, source_target_pairs={{0,32},{16,112},{32,64},{48,16},{64,96},{80,48},{96,0},{112,80},{4... | collective-permute-start | bytes 786440 | tf_op jit(solution)/shard_map/ppermute | solution.py:51
  13.5 20.4 %collective-permute-start.9 = (bf16[3600,128]{1,0:T(8,128)(2,1)S(1)}, bf16[3600,128]{1,0:T(8,128)(2,1)}, u32[]{:S(2)}, u32[]{:S(2)}) collective-permute-start(bf16[3600,128]{1,0:T(8,128)(2,1)S(1)} %pad_maximum_fusion.w0), channel_id=1, source_target_pairs={{0,1},{16,19},{32,33},{48,51},{64,65},{80,83},{96,97},{112,115},{4... | collective-permute-start | bytes 2764808 | tf_op jit(solution)/shard_map/ppermute | solution.py:51
  16.7 5.5 %collective-permute-start.5 = (bf16[4,64,256]{2,1,0:T(8,128)(2,1)}, bf16[4,64,256]{2,1,0:T(8,128)(2,1)S(1)}, u32[]{:S(2)}, u32[]{:S(2)}) collective-permute-start(bf16[4,64,256]{2,1,0:T(8,128)(2,1)} %constant_dynamic-slice_fusion.1), channel_id=1, source_target_pairs={{0,64},{16,80},{32,96},{48,112},{64,0},{80,16},{96,32},{112,48},{4... | collective-permute-start | bytes 393224 | tf_op jit(solution)/shard_map/ppermute | solution.py:39
  17.3 20.9 %copy-start.5 = (f32[512]{0:T(512)S(1)}, f32[512]{0:T(512)}, u32[]{:S(2)}) copy-start(f32[512]{0:T(512)} %param.16) | copy-start | bytes 6148
  17.3 20.9 %copy-start.6 = (f32[512]{0:T(512)S(1)}, f32[512]{0:T(512)}, u32[]{:S(2)}) copy-start(f32[512]{0:T(512)} %param.18) | copy-start | bytes 6148
  17.3 4.8 %collective-permute-start.7 = (bf16[4,64,256]{2,1,0:T(8,128)(2,1)}, bf16[4,64,256]{2,1,0:T(8,128)(2,1)S(1)}, u32[]{:S(2)}, u32[]{:S(2)}) collective-permute-start(bf16[4,64,256]{2,1,0:T(8,128)(2,1)} %constant_dynamic-slice_fusion), channel_id=1, source_target_pairs={{0,16},{16,0},{32,48},{48,32},{64,80},{80,64},{96,112},{112,96},{4... | collective-permute-start | bytes 393224 | tf_op jit(solution)/shard_map/ppermute | solution.py:39
  23.1 24.2 %all-to-all-start = ((bf16[16,64,256]{2,1,0:T(8,128)(2,1)}), bf16[16,64,256]{2,1,0:T(8,128)(2,1)S(1)}, u32[]{:S(2)}, u32[]{:S(2)}) async-start(bf16[16,64,256]{2,1,0:T(8,128)(2,1)} %bitcast.38), calls=%async_computation | async-start | bytes 1048576 | tf_op jit(solution)/shard_map/all_to_all | solution.py:267
  29.2 15.9 %collective-permute-start.2 = (bf16[48,3584]{1,0:T(8,128)(2,1)S(1)}, bf16[48,3584]{1,0:T(8,128)(2,1)S(1)}, u32[]{:S(2)}, u32[]{:S(2)}) collective-permute-start(bf16[48,3584]{1,0:T(8,128)(2,1)S(1)} %slice.12), channel_id=1, source_target_pairs={{0,4},{16,20},{32,36},{48,52},{64,68},{80,84},{96,100},{112,116},{... | collective-permute-start | bytes 1032200 | tf_op jit(solution)/shard_map/ppermute | solution.py:39
  31.7 13.4 %collective-permute-start.3 = (bf16[48,3584]{1,0:T(8,128)(2,1)S(1)}, bf16[48,3584]{1,0:T(8,128)(2,1)S(1)}, u32[]{:S(2)}, u32[]{:S(2)}) collective-permute-start(bf16[48,3584]{1,0:T(8,128)(2,1)S(1)} %slice.13), channel_id=1, source_target_pairs={{0,12},{16,28},{32,44},{48,60},{64,76},{80,92},{96,108},{112,124},... | collective-permute-start | bytes 1032200 | tf_op jit(solution)/shard_map/ppermute | solution.py:39
  33.9 17.5 %collective-permute-start.10 = (bf16[3600,128]{1,0:T(8,128)(2,1)}, bf16[3600,128]{1,0:T(8,128)(2,1)}, u32[]{:S(2)}, u32[]{:S(2)}) collective-permute-start(bf16[3600,128]{1,0:T(8,128)(2,1)} %collective-permute-done.9.w1), channel_id=1, source_target_pairs={{0,16},{16,0},{32,48},{48,32},{64,80},{80,64},{96,112},{112,96},{4... | collective-permute-start | bytes 2764808 | tf_op jit(solution)/shard_map/ppermute | solution.py:39
  35.2 16.1 %collective-permute-start.11 = (bf16[3600,128]{1,0:T(8,128)(2,1)}, bf16[3600,128]{1,0:T(8,128)(2,1)}, u32[]{:S(2)}, u32[]{:S(2)}) collective-permute-start(bf16[3600,128]{1,0:T(8,128)(2,1)} %collective-permute-done.9.w1), channel_id=1, source_target_pairs={{0,1},{16,19},{32,33},{48,51},{64,65},{80,83},{96,97},{112,115},{4... | collective-permute-start | bytes 2764808 | tf_op jit(solution)/shard_map/ppermute | solution.py:51
  38.3 1.1 %copy-start.2 = (bf16[6,16,3584]{2,1,0:T(8,128)(2,1)S(1)}, bf16[6,16,3584]{2,1,0:T(8,128)(2,1)}, u32[]{:S(2)}) copy-start(bf16[6,16,3584]{2,1,0:T(8,128)(2,1)} %param.11) | copy-start | bytes 2064388
  42.0 1.3 %copy-start = (bf16[288,3584]{1,0:T(8,128)(2,1)}, bf16[288,3584]{1,0:T(8,128)(2,1)S(1)}, u32[]{:S(2)}) copy-start(bf16[288,3584]{1,0:T(8,128)(2,1)S(1)} %get-tuple-element.11.near) | copy-start | bytes 6193156
  46.4 0.9 %copy-start.3 = (bf16[96,3584]{1,0:T(8,128)(2,1)}, bf16[96,3584]{1,0:T(8,128)(2,1)S(1)}, u32[]{:S(2)}) copy-start(bf16[96,3584]{1,0:T(8,128)(2,1)S(1)} %get-tuple-element.16.far) | copy-start | bytes 2064388
  47.3 12.8 %copy-start.8 = (s32[48]{0:T(128)S(1)}, s32[48]{0:T(128)}, u32[]{:S(2)}) copy-start(s32[48]{0:T(128)} %dest.1) | copy-start | bytes 580
  47.3 12.8 %copy-start.9 = (s32[48]{0:T(128)S(1)}, s32[48]{0:T(128)}, u32[]{:S(2)}) copy-start(s32[48]{0:T(128)} %lengths.1) | copy-start | bytes 580
  47.3 3.1 %collective-permute-start.8 = (bf16[1024,256]{1,0:T(8,128)(2,1)S(1)}, bf16[1024,256]{1,0:T(8,128)(2,1)S(1)}, u32[]{:S(2)}, u32[]{:S(2)}) collective-permute-start(bf16[1024,256]{1,0:T(8,128)(2,1)S(1)} %bitcast.24), channel_id=1, source_target_pairs={{0,16},{16,0},{32,48},{48,32},{64,80},{80,64},{96,112},{112,96},{4... | collective-permute-start | bytes 1572872 | tf_op jit(solution)/shard_map/ppermute | solution.py:39
  47.7 9.8 %collective-permute-start.12 = (bf16[6,64,256]{2,1,0:T(8,128)(2,1)S(1)}, bf16[6,64,256]{2,1,0:T(8,128)(2,1)S(1)}, u32[]{:S(2)}, u32[]{:S(2)}) collective-permute-start(bf16[6,64,256]{2,1,0:T(8,128)(2,1)S(1)} %get-tuple-element.14.kv0), channel_id=1, source_target_pairs={{0,1},{16,17},{32,33},{48,49},{64,65},{80,81},{96,97},{112,113},{4... | collective-permute-start | bytes 589832 | tf_op jit(solution)/shard_map/ppermute | solution.py:39
  48.5 9.0 %collective-permute-start.13 = (bf16[6,64,256]{2,1,0:T(8,128)(2,1)S(1)}, bf16[6,64,256]{2,1,0:T(8,128)(2,1)S(1)}, u32[]{:S(2)}, u32[]{:S(2)}) collective-permute-start(bf16[6,64,256]{2,1,0:T(8,128)(2,1)S(1)} %get-tuple-element.14.kv0), channel_id=1, source_target_pairs={{0,3},{16,19},{32,35},{48,51},{64,67},{80,83},{96,99},{112,115},{4... | collective-permute-start | bytes 589832 | tf_op jit(solution)/shard_map/ppermute | solution.py:39
  50.4 9.6 %collective-permute-start.14 = (bf16[6,64,256]{2,1,0:T(8,128)(2,1)S(1)}, bf16[6,64,256]{2,1,0:T(8,128)(2,1)S(1)}, u32[]{:S(2)}, u32[]{:S(2)}) collective-permute-start(bf16[6,64,256]{2,1,0:T(8,128)(2,1)S(1)} %get-tuple-element.14.kv0), channel_id=1, source_target_pairs={{0,2},{16,18},{32,34},{48,50},{64,66},{80,82},{96,98},{112,114},{4... | collective-permute-start | bytes 589832 | tf_op jit(solution)/shard_map/ppermute | solution.py:39
  51.4 1.6 %copy-start.1 = (bf16[288,3584]{1,0:T(8,128)(2,1)S(1)}, bf16[288,3584]{1,0:T(8,128)(2,1)}, u32[]{:S(2)}) copy-start(bf16[288,3584]{1,0:T(8,128)(2,1)} %copy-done) | copy-start | bytes 6193156
  52.9 1.1 %copy-start.4 = (bf16[96,3584]{1,0:T(8,128)(2,1)S(1)}, bf16[96,3584]{1,0:T(8,128)(2,1)}, u32[]{:S(2)}) copy-start(bf16[96,3584]{1,0:T(8,128)(2,1)} %copy-done.3) | copy-start | bytes 2064388

commit v6 on v5

--- a/solution.py
+++ b/solution.py
@@ -194,7 +194,8 @@
         mixed = mixed + jnp.dot(
             near.astype(jnp.bfloat16), self_values, preferred_element_type=jnp.float32
         )
-        mixed = jnp.where(row_pos[:, 0:HD] < length, mixed / total, 0.0).astype(jnp.bfloat16)
+        mixed = mixed * (1.0 / total)
+        mixed = jnp.where(row_pos[:, 0:HD] < length, mixed, 0.0).astype(jnp.bfloat16)
         out[dest[g * RESP + i]] = mixed.reshape(4, 64, HD)
 
 
@@ -272,7 +273,8 @@
     kv, far_rows = keys_values(far_kernel, "far_rows", CHUNK, meta, (kv, far_a, far_b), small)
     c_mine, _ = lax.optimization_barrier((c_mine, kv))
     c_other = shift(c_mine, flip=1)
-    parts = (kv, shift(kv, dx=1), shift(kv, dx=-1), shift(kv, dx=2))
+    two_away = shift(kv, dx=2)
+    parts = (kv, shift(kv, dx=1), shift(kv, dx=-1), two_away)
     far_rows, _ = lax.optimization_barrier((far_rows, c_other))
     weights = (w_own, w_beside, w_across, w_far)
     q = make_queries(meta, near_rows, far_rows, weights, cos, sin)

time: 84.4 us -> 84.4 us (level)
  no operation moved by 1% of the time
where the time goes in v6:
time: 84.4 us; the launch traced here: 83.7 us
  starting transfers between devices  27.3 us (32%)
  blocking collectives  16.6 us (20%)
  Pallas kernels  13.6 us (16%)
  local copies, waits for them, and re-layouts  13.4 us (16%)
  waiting for transfers between devices  6.12 us (7%)
  other arithmetic  4.52 us (5%)
  between operations  2.26 us (3%)
    all_to_all x1, blocking collectives, on_device(): lax.all_to_all(ready.reshape(32, 64, HD), AXES, 0, 0, tiled=True, axis_in...  16.6 us
    ppermute x12, starting transfers between devices, shift(): return lax.ppermute(v, AXES, pairs)  13.6 us
    ppermute x3, starting transfers between devices, both_ways(): return lax.ppermute(v, AXES, pairs)  9.31 us
    pallas_call x1, Pallas kernels, attend(): pl.pallas_call(attend_kernel, out_shape=jax.ShapeDtypeStruct((GROUPS, 4,...  6.23 us
    ppermute x12, waiting for transfers between devices, shift(): return lax.ppermute(v, AXES, pairs)  6.11 us
    unnamed x20, local copies, waits for them, and re-layouts  6.02 us
    all_to_all x1, starting transfers between devices, on_device(): lax.all_to_all(spread, 'mp', 0, 0, tiled=True).reshape(1024, 2 * HD)  4.35 us
    pallas_call x2, Pallas kernels, keys_values(): pl.pallas_call(kernel, out_shape=(jax.ShapeDtypeStruct((RESP, 64, 2 * HD)...  3.86 us
  transfers between devices with their start and end apart: 16, of which 3 were waited for; matrix products, arithmetic and copies ran while one was open for 13% of the time, Pallas kernels for 9%

profile of v6, /device:TPU:1, one launch (start us, length us, event | category | flops | bytes accessed | tf_op | source)
XLA Modules:
  0.0 83.7 jit_solution(13923326541617655279)
XLA Ops:
  0.0 2.1 %collective-permute-start = (bf16[96,3584]{1,0:T(8,128)(2,1)}, bf16[96,3584]{1,0:T(8,128)(2,1)}, u32[]{:S(2)}, u32[]{:S(2)}) collective-permute-start(bf16[96,3584]{1,0:T(8,128)(2,1)} %bitcast.27), channel_id=1, source_target_pairs={{0,4},{16,20},{32,36},{48,52},{64,68},{80,84},{96,100},{112,116},{... | collective-permute-start | bytes 2064392 | tf_op jit(solution)/shard_map/ppermute | solution.py:39
  2.1 1.5 %collective-permute-start.1 = (bf16[96,3584]{1,0:T(8,128)(2,1)}, bf16[96,3584]{1,0:T(8,128)(2,1)}, u32[]{:S(2)}, u32[]{:S(2)}) collective-permute-start(bf16[96,3584]{1,0:T(8,128)(2,1)} %bitcast.28), channel_id=1, source_target_pairs={{0,12},{16,28},{32,44},{48,60},{64,76},{80,92},{96,108},{112,124},... | collective-permute-start | bytes 2064392 | tf_op jit(solution)/shard_map/ppermute | solution.py:39
  3.6 1.0 %collective-permute-start.4 = (bf16[4,128,256]{2,1,0:T(8,128)(2,1)}, bf16[4,128,256]{2,1,0:T(8,128)(2,1)S(1)}, u32[]{:S(2)}, u32[]{:S(2)}) collective-permute-start(bf16[4,128,256]{2,1,0:T(8,128)(2,1)} %bitcast.40), channel_id=1, source_target_pairs={{0,16},{16,0},{32,48},{48,32},{64,80},{80,64},{96,112},{112,96},{4... | collective-permute-start | bytes 786440 | tf_op jit(solution)/shard_map/ppermute | solution.py:39
  6.6 0.7 fusion.8
  7.3 1.0 %broadcast_select_fusion = bf16[4,128,256]{2,1,0:T(8,128)(2,1)S(1)} fusion(bf16[4,128,256]{2,1,0:T(8,128)(2,1)S(1)} %collective-permute-done.4, pred[]{:T(512)S(6)} %eq.23, bf16[1,4,128,256]{3,2,1,0:T(8,128)(2,1)} %param.19), kind=kLoop, calls=%fused_computation.1 | loop fusion | flops 131072 | bytes 786433 | tf_op jit(solution)/shard_map/jit(_where)/select_n | solution.py:255
  8.3 3.9 %collective-permute-start.6 = (bf16[4,128,256]{2,1,0:T(8,128)(2,1)S(1)}, bf16[4,128,256]{2,1,0:T(8,128)(2,1)S(1)}, u32[]{:S(2)}, u32[]{:S(2)}) collective-permute-start(bf16[4,128,256]{2,1,0:T(8,128)(2,1)S(1)} %broadcast_select_fusion), channel_id=1, source_target_pairs={{0,32},{16,112},{32,64},{48,16},{64,96},{80,48},{96,0},{112,80},{4... | collective-permute-start | bytes 786440 | tf_op jit(solution)/shard_map/ppermute | solution.py:51
  12.2 1.2 %pad_maximum_fusion.w0 = bf16[3600,128]{1,0:T(8,128)(2,1)S(1)} fusion(bf16[16,128]{1,0:T(8,128)(2,1)S(1)} %fusion.5, bf16[3584,128]{1,0:T(8,128)(2,1)} %param.13), kind=kLoop, calls=%fused_computation | loop fusion | flops 1843200 | bytes 1843200 | tf_op jit(solution)/shard_map/concatenate | solution.py:247
  13.5 2.5 %collective-permute-start.9 = (bf16[3600,128]{1,0:T(8,128)(2,1)S(1)}, bf16[3600,128]{1,0:T(8,128)(2,1)}, u32[]{:S(2)}, u32[]{:S(2)}) collective-permute-start(bf16[3600,128]{1,0:T(8,128)(2,1)S(1)} %pad_maximum_fusion.w0), channel_id=1, source_target_pairs={{0,1},{16,19},{32,33},{48,51},{64,65},{80,83},{96,97},{112,115},{4... | collective-permute-start | bytes 2764808 | tf_op jit(solution)/shard_map/ppermute | solution.py:51
  16.0 0.7 constant_dynamic-slice_fusion.1
  16.7 0.7 constant_dynamic-slice_fusion
  17.3 0.8 collective-permute-start.7
  18.1 1.6 %constant_dynamic-slice_fusion.2 = (bf16[3584,128]{1,0:T(8,128)(2,1)S(1)}, bf16[3584,128]{1,0:T(8,128)(2,1)S(1)}) fusion(bf16[3584,512]{1,0:T(8,128)(2,1)} %param.17, s32[]{:T(128)S(6)} %select_n.94, bf16[3584,512]{1,0:T(8,128)(2,1)} %param.15), kind=kLoop, calls=%fused_computation.18 | loop fusion | bytes 3670020 | tf_op jit(solution)/shard_map/dynamic_slice | solution.py:239
  19.8 0.6 multiply_exponential_fusion
  20.4 1.8 %collective-permute-done.5 = bf16[4,64,256]{2,1,0:T(8,128)(2,1)S(1)} collective-permute-done((bf16[4,64,256]{2,1,0:T(8,128)(2,1)}, bf16[4,64,256]{2,1,0:T(8,128)(2,1)S(1)}, u32[]{:S(2)}, u32[]{:S(2)}) %collective-permute-start.5) | collective-permute-done | bytes 131104 | tf_op jit(solution)/shard_map/ppermute | solution.py:39
  22.2 0.0 collective-permute-done.7
  22.2 0.1 select_select_fusion
  22.3 0.8 %broadcast_in_dim.2 = bf16[4,4,64,256]{3,2,1,0:T(8,128)(2,1)} broadcast(bf16[4,64,256]{2,1,0:T(8,128)(2,1)S(1)} %select_select_fusion), dimensions={0,2,3} | broadcast | bytes 655360 | tf_op jit(solution)/shard_map/broadcast_in_dim | solution.py:267
  23.1 4.3 %all-to-all-start = ((bf16[16,64,256]{2,1,0:T(8,128)(2,1)}), bf16[16,64,256]{2,1,0:T(8,128)(2,1)S(1)}, u32[]{:S(2)}, u32[]{:S(2)}) async-start(bf16[16,64,256]{2,1,0:T(8,128)(2,1)} %bitcast.38), calls=%async_computation | async-start | bytes 1048576 | tf_op jit(solution)/shard_map/all_to_all | solution.py:268
  27.5 0.7 reshape.59.gain
  28.2 0.0 collective-permute-done.before
  28.2 1.0 %slice.12 = bf16[48,3584]{1,0:T(8,128)(2,1)S(1)} slice(bf16[96,3584]{1,0:T(8,128)(2,1)} %collective-permute-done.before), slice={[0:48], [0:3584]} | slice | bytes 688128 | tf_op jit(solution)/shard_map/slice | solution.py:226
  29.2 1.4 %collective-permute-start.2 = (bf16[48,3584]{1,0:T(8,128)(2,1)S(1)}, bf16[48,3584]{1,0:T(8,128)(2,1)S(1)}, u32[]{:S(2)}, u32[]{:S(2)}) collective-permute-start(bf16[48,3584]{1,0:T(8,128)(2,1)S(1)} %slice.12), channel_id=1, source_target_pairs={{0,4},{16,20},{32,36},{48,52},{64,68},{80,84},{96,100},{112,116},{... | collective-permute-start | bytes 1032200 | tf_op jit(solution)/shard_map/ppermute | solution.py:39
  30.7 0.0 collective-permute-done.1.after
  30.7 1.0 %slice.13 = bf16[48,3584]{1,0:T(8,128)(2,1)S(1)} slice(bf16[96,3584]{1,0:T(8,128)(2,1)} %collective-permute-done.1.after), slice={[48:96], [0:3584]} | slice | bytes 688128 | tf_op jit(solution)/shard_map/slice | solution.py:227
  31.7 1.4 %collective-permute-start.3 = (bf16[48,3584]{1,0:T(8,128)(2,1)S(1)}, bf16[48,3584]{1,0:T(8,128)(2,1)S(1)}, u32[]{:S(2)}, u32[]{:S(2)}) collective-permute-start(bf16[48,3584]{1,0:T(8,128)(2,1)S(1)} %slice.13), channel_id=1, source_target_pairs={{0,12},{16,28},{32,44},{48,60},{64,76},{80,92},{96,108},{112,124},... | collective-permute-start | bytes 1032200 | tf_op jit(solution)/shard_map/ppermute | solution.py:39
  33.1 0.8 fusion
  33.9 1.3 %collective-permute-start.10 = (bf16[3600,128]{1,0:T(8,128)(2,1)}, bf16[3600,128]{1,0:T(8,128)(2,1)}, u32[]{:S(2)}, u32[]{:S(2)}) collective-permute-start(bf16[3600,128]{1,0:T(8,128)(2,1)} %collective-permute-done.9.w1), channel_id=1, source_target_pairs={{0,16},{16,0},{32,48},{48,32},{64,80},{80,64},{96,112},{112,96},{4... | collective-permute-start | bytes 2764808 | tf_op jit(solution)/shard_map/ppermute | solution.py:39
  35.2 2.8 %collective-permute-start.11 = (bf16[3600,128]{1,0:T(8,128)(2,1)}, bf16[3600,128]{1,0:T(8,128)(2,1)}, u32[]{:S(2)}, u32[]{:S(2)}) collective-permute-start(bf16[3600,128]{1,0:T(8,128)(2,1)} %collective-permute-done.9.w1), channel_id=1, source_target_pairs={{0,1},{16,19},{32,33},{48,51},{64,65},{80,83},{96,97},{112,115},{4... | collective-permute-start | bytes 2764808 | tf_op jit(solution)/shard_map/ppermute | solution.py:51
  38.1 0.1 pad_add_fusion.meta
  38.1 0.1 pad_maximum_fusion.1
  38.3 0.0 copy-start.2
  38.3 1.1 %copy-done.2 = bf16[6,16,3584]{2,1,0:T(8,128)(2,1)S(1)} copy-done((bf16[6,16,3584]{2,1,0:T(8,128)(2,1)S(1)}, bf16[6,16,3584]{2,1,0:T(8,128)(2,1)}, u32[]{:S(2)}) %copy-start.2) | copy-done | bytes 688152
  39.4 2.6 %near_rows.1 = (bf16[6,64,256]{2,1,0:T(8,128)(2,1)S(1)}, bf16[288,3584]{1,0:T(8,128)(2,1)S(1)}) custom-call(s32[4]{0:T(128)S(1)} %pad_add_fusion.meta, bf16[96,3584]{1,0:T(8,128)(2,1)S(1)} %bitcast.29, bf16[96,3584]{1,0:T(8,128)(2,1)} %collective-permute-done.before, bf16[96,3584]{1,0:T(8,128)(2,1)} %collective-permute-done.1.after, ...), custom_call_target="tpu_custom_call" | custom-call | tf_op jit(solution)/shard_map/near_rows/pallas_call | solution.py:118
  42.0 1.3 %copy-done = bf16[288,3584]{1,0:T(8,128)(2,1)} copy-done((bf16[288,3584]{1,0:T(8,128)(2,1)}, bf16[288,3584]{1,0:T(8,128)(2,1)S(1)}, u32[]{:S(2)}) %copy-start) | copy-done | bytes 2064408
  43.3 1.8 %collective-permute-done.2.far_a = bf16[48,3584]{1,0:T(8,128)(2,1)S(1)} collective-permute-done((bf16[48,3584]{1,0:T(8,128)(2,1)S(1)}, bf16[48,3584]{1,0:T(8,128)(2,1)S(1)}, u32[]{:S(2)}, u32[]{:S(2)}) %collective-permute-start.2) | collective-permute-done | bytes 344096 | tf_op jit(solution)/shard_map/ppermute | solution.py:39
  45.1 1.2 %far_rows.1 = (bf16[6,64,256]{2,1,0:T(8,128)(2,1)S(1)}, bf16[96,3584]{1,0:T(8,128)(2,1)S(1)}) custom-call(s32[4]{0:T(128)S(1)} %pad_add_fusion.meta, bf16[6,64,256]{2,1,0:T(8,128)(2,1)S(1)} %get-tuple-element.12.near, bf16[48,3584]{1,0:T(8,128)(2,1)S(1)} %collective-permute-done.2.far_a, bf16[48,3584]{1,0:T(8,128)(2,1)S(1)} %collective-permute-done.3.far_b, ...), custom_call_target="tpu_custom_call" | custom-call | tf_op jit(solution)/shard_map/far_rows/pallas_call | solution.py:118
  46.4 0.9 %copy-done.3 = bf16[96,3584]{1,0:T(8,128)(2,1)} copy-done((bf16[96,3584]{1,0:T(8,128)(2,1)}, bf16[96,3584]{1,0:T(8,128)(2,1)S(1)}, u32[]{:S(2)}) %copy-start.3) | copy-done | bytes 688152
  47.3 0.4 collective-permute-start.8
  47.7 0.8 collective-permute-start.12
  48.5 1.9 %collective-permute-start.13 = (bf16[6,64,256]{2,1,0:T(8,128)(2,1)S(1)}, bf16[6,64,256]{2,1,0:T(8,128)(2,1)S(1)}, u32[]{:S(2)}, u32[]{:S(2)}) collective-permute-start(bf16[6,64,256]{2,1,0:T(8,128)(2,1)S(1)} %get-tuple-element.14.kv0), channel_id=1, source_target_pairs={{0,3},{16,19},{32,35},{48,51},{64,67},{80,83},{96,99},{112,115},{4... | collective-permute-start | bytes 589832 | tf_op jit(solution)/shard_map/ppermute | solution.py:39
  50.4 0.9 %collective-permute-start.14 = (bf16[6,64,256]{2,1,0:T(8,128)(2,1)S(1)}, bf16[6,64,256]{2,1,0:T(8,128)(2,1)S(1)}, u32[]{:S(2)}, u32[]{:S(2)}) collective-permute-start(bf16[6,64,256]{2,1,0:T(8,128)(2,1)S(1)} %get-tuple-element.14.kv0), channel_id=1, source_target_pairs={{0,2},{16,18},{32,34},{48,50},{64,66},{80,82},{96,98},{112,114},{4... | collective-permute-start | bytes 589832 | tf_op jit(solution)/shard_map/ppermute | solution.py:39
  51.4 1.6 %copy-done.1 = bf16[288,3584]{1,0:T(8,128)(2,1)S(1)} copy-done((bf16[288,3584]{1,0:T(8,128)(2,1)S(1)}, bf16[288,3584]{1,0:T(8,128)(2,1)}, u32[]{:S(2)}) %copy-start.1) | copy-done | bytes 2064408
  52.9 1.1 %copy-done.4 = bf16[96,3584]{1,0:T(8,128)(2,1)S(1)} copy-done((bf16[96,3584]{1,0:T(8,128)(2,1)S(1)}, bf16[96,3584]{1,0:T(8,128)(2,1)}, u32[]{:S(2)}) %copy-start.4) | copy-done | bytes 688152
  54.0 3.5 %queries.1.q_ref = bf16[6,4,64,128]{3,2,1,0:T(8,128)(2,1)S(1)} custom-call(s32[4]{0:T(128)S(1)} %pad_add_fusion.meta, bf16[288,3584]{1,0:T(8,128)(2,1)S(1)} %copy-done.1, bf16[96,3584]{1,0:T(8,128)(2,1)S(1)} %copy-done.4, bf16[3600,128]{1,0:T(8,128)(2,1)S(1)} %pad_maximum_fusion.w0, bf16[3600,128]{1,0:T(8,128)(2,1)} %collective-permute-done.9.w1, ...), custom_call_target="tpu_custom_call" | custom-call | tf_op jit(solution)/shard_map/queries/pallas_call | solution.py:154
  57.6 2.5 %collective-permute-done.14.kv3 = bf16[6,64,256]{2,1,0:T(8,128)(2,1)S(1)} collective-permute-done((bf16[6,64,256]{2,1,0:T(8,128)(2,1)S(1)}, bf16[6,64,256]{2,1,0:T(8,128)(2,1)S(1)}, u32[]{:S(2)}, u32[]{:S(2)}) %collective-permute-start.14) | collective-permute-done | bytes 196640 | tf_op jit(solution)/shard_map/ppermute | solution.py:39
  60.1 6.2 %attend.1 = bf16[8,4,64,128]{3,2,1,0:T(8,128)(2,1)S(1)} custom-call(s32[4]{0:T(128)S(1)} %pad_add_fusion.meta, s32[48]{0:T(128)S(1)} %copy-done.8, s32[48]{0:T(128)S(1)} %copy-done.9, bf16[6,4,64,128]{3,2,1,0:T(8,128)(2,1)S(1)} %queries.1.q_ref, bf16[1024,256]{1,0:T(8,128)(2,1)S(1)} %bitcast.25, bf16[1024,256]{1,0:T(8,128)(2,1)S(1)} %collective-permute-done.8.c_other, ...), custom_call_target="tpu_custom_call" | custom-call | tf_op jit(solution)/shard_map/attend/pallas_call | solution.py:203
  66.3 16.6 %all_to_all.10 = bf16[32,64,128]{2,1,0:T(8,128)(2,1)S(1)} all-to-all(bf16[32,64,128]{2,1,0:T(8,128)(2,1)S(1)} %bitcast.26), channel_id=1, replica_groups={{0,1,2,3,16,17,18,19,32,33,34,35,48,49,50,51,64,65,66,67,80,81,82,83,96..., dimensions={0} | all-to-all | bytes 1048576 | tf_op jit(solution)/shard_map/all_to_all | solution.py:282
  82.9 0.9 %copy.12 = bf16[8,4,4,16,128]{4,3,1,2,0:T(8,128)(2,1)} copy(bf16[8,4,4,16,128]{4,3,2,1,0:T(8,128)(2,1)S(1)} %bitcast.39) | data formatting | bytes 1048576 | tf_op jit(solution)/shard_map/reshape | solution.py:285
  (27 shorter events, 0.1 us)
Async XLA Ops:
  0.0 19.7 %copy-start.7 = (s32[48]{0:T(128)S(1)}, s32[48]{0:T(128)}, u32[]{:S(2)}) copy-start(s32[48]{0:T(128)} %dest.1) | copy-start | bytes 580
  0.0 28.2 %collective-permute-start = (bf16[96,3584]{1,0:T(8,128)(2,1)}, bf16[96,3584]{1,0:T(8,128)(2,1)}, u32[]{:S(2)}, u32[]{:S(2)}) collective-permute-start(bf16[96,3584]{1,0:T(8,128)(2,1)} %bitcast.27), channel_id=1, source_target_pairs={{0,4},{16,20},{32,36},{48,52},{64,68},{80,84},{96,100},{112,116},{... | collective-permute-start | bytes 2064392 | tf_op jit(solution)/shard_map/ppermute | solution.py:39
  2.1 28.5 %collective-permute-start.1 = (bf16[96,3584]{1,0:T(8,128)(2,1)}, bf16[96,3584]{1,0:T(8,128)(2,1)}, u32[]{:S(2)}, u32[]{:S(2)}) collective-permute-start(bf16[96,3584]{1,0:T(8,128)(2,1)} %bitcast.28), channel_id=1, source_target_pairs={{0,12},{16,28},{32,44},{48,60},{64,76},{80,92},{96,108},{112,124},... | collective-permute-start | bytes 2064392 | tf_op jit(solution)/shard_map/ppermute | solution.py:39
  3.6 3.7 %collective-permute-start.4 = (bf16[4,128,256]{2,1,0:T(8,128)(2,1)}, bf16[4,128,256]{2,1,0:T(8,128)(2,1)S(1)}, u32[]{:S(2)}, u32[]{:S(2)}) collective-permute-start(bf16[4,128,256]{2,1,0:T(8,128)(2,1)} %bitcast.40), channel_id=1, source_target_pairs={{0,16},{16,0},{32,48},{48,32},{64,80},{80,64},{96,112},{112,96},{4... | collective-permute-start | bytes 786440 | tf_op jit(solution)/shard_map/ppermute | solution.py:39
  8.3 8.4 %collective-permute-start.6 = (bf16[4,128,256]{2,1,0:T(8,128)(2,1)S(1)}, bf16[4,128,256]{2,1,0:T(8,128)(2,1)S(1)}, u32[]{:S(2)}, u32[]{:S(2)}) collective-permute-start(bf16[4,128,256]{2,1,0:T(8,128)(2,1)S(1)} %broadcast_select_fusion), channel_id=1, source_target_pairs={{0,32},{16,112},{32,64},{48,16},{64,96},{80,48},{96,0},{112,80},{4... | collective-permute-start | bytes 786440 | tf_op jit(solution)/shard_map/ppermute | solution.py:51
  13.5 20.4 %collective-permute-start.9 = (bf16[3600,128]{1,0:T(8,128)(2,1)S(1)}, bf16[3600,128]{1,0:T(8,128)(2,1)}, u32[]{:S(2)}, u32[]{:S(2)}) collective-permute-start(bf16[3600,128]{1,0:T(8,128)(2,1)S(1)} %pad_maximum_fusion.w0), channel_id=1, source_target_pairs={{0,1},{16,19},{32,33},{48,51},{64,65},{80,83},{96,97},{112,115},{4... | collective-permute-start | bytes 2764808 | tf_op jit(solution)/shard_map/ppermute | solution.py:51
  16.7 5.5 %collective-permute-start.5 = (bf16[4,64,256]{2,1,0:T(8,128)(2,1)}, bf16[4,64,256]{2,1,0:T(8,128)(2,1)S(1)}, u32[]{:S(2)}, u32[]{:S(2)}) collective-permute-start(bf16[4,64,256]{2,1,0:T(8,128)(2,1)} %constant_dynamic-slice_fusion.1), channel_id=1, source_target_pairs={{0,64},{16,80},{32,96},{48,112},{64,0},{80,16},{96,32},{112,48},{4... | collective-permute-start | bytes 393224 | tf_op jit(solution)/shard_map/ppermute | solution.py:39
  17.3 20.9 %copy-start.5 = (f32[512]{0:T(512)S(1)}, f32[512]{0:T(512)}, u32[]{:S(2)}) copy-start(f32[512]{0:T(512)} %param.16) | copy-start | bytes 6148
  17.3 20.9 %copy-start.6 = (f32[512]{0:T(512)S(1)}, f32[512]{0:T(512)}, u32[]{:S(2)}) copy-start(f32[512]{0:T(512)} %param.18) | copy-start | bytes 6148
  17.3 4.8 %collective-permute-start.7 = (bf16[4,64,256]{2,1,0:T(8,128)(2,1)}, bf16[4,64,256]{2,1,0:T(8,128)(2,1)S(1)}, u32[]{:S(2)}, u32[]{:S(2)}) collective-permute-start(bf16[4,64,256]{2,1,0:T(8,128)(2,1)} %constant_dynamic-slice_fusion), channel_id=1, source_target_pairs={{0,16},{16,0},{32,48},{48,32},{64,80},{80,64},{96,112},{112,96},{4... | collective-permute-start | bytes 393224 | tf_op jit(solution)/shard_map/ppermute | solution.py:39
  23.1 24.2 %all-to-all-start = ((bf16[16,64,256]{2,1,0:T(8,128)(2,1)}), bf16[16,64,256]{2,1,0:T(8,128)(2,1)S(1)}, u32[]{:S(2)}, u32[]{:S(2)}) async-start(bf16[16,64,256]{2,1,0:T(8,128)(2,1)} %bitcast.38), calls=%async_computation | async-start | bytes 1048576 | tf_op jit(solution)/shard_map/all_to_all | solution.py:268
  29.2 15.9 %collective-permute-start.2 = (bf16[48,3584]{1,0:T(8,128)(2,1)S(1)}, bf16[48,3584]{1,0:T(8,128)(2,1)S(1)}, u32[]{:S(2)}, u32[]{:S(2)}) collective-permute-start(bf16[48,3584]{1,0:T(8,128)(2,1)S(1)} %slice.12), channel_id=1, source_target_pairs={{0,4},{16,20},{32,36},{48,52},{64,68},{80,84},{96,100},{112,116},{... | collective-permute-start | bytes 1032200 | tf_op jit(solution)/shard_map/ppermute | solution.py:39
  31.7 13.4 %collective-permute-start.3 = (bf16[48,3584]{1,0:T(8,128)(2,1)S(1)}, bf16[48,3584]{1,0:T(8,128)(2,1)S(1)}, u32[]{:S(2)}, u32[]{:S(2)}) collective-permute-start(bf16[48,3584]{1,0:T(8,128)(2,1)S(1)} %slice.13), channel_id=1, source_target_pairs={{0,12},{16,28},{32,44},{48,60},{64,76},{80,92},{96,108},{112,124},... | collective-permute-start | bytes 1032200 | tf_op jit(solution)/shard_map/ppermute | solution.py:39
  33.9 17.5 %collective-permute-start.10 = (bf16[3600,128]{1,0:T(8,128)(2,1)}, bf16[3600,128]{1,0:T(8,128)(2,1)}, u32[]{:S(2)}, u32[]{:S(2)}) collective-permute-start(bf16[3600,128]{1,0:T(8,128)(2,1)} %collective-permute-done.9.w1), channel_id=1, source_target_pairs={{0,16},{16,0},{32,48},{48,32},{64,80},{80,64},{96,112},{112,96},{4... | collective-permute-start | bytes 2764808 | tf_op jit(solution)/shard_map/ppermute | solution.py:39
  35.2 16.1 %collective-permute-start.11 = (bf16[3600,128]{1,0:T(8,128)(2,1)}, bf16[3600,128]{1,0:T(8,128)(2,1)}, u32[]{:S(2)}, u32[]{:S(2)}) collective-permute-start(bf16[3600,128]{1,0:T(8,128)(2,1)} %collective-permute-done.9.w1), channel_id=1, source_target_pairs={{0,1},{16,19},{32,33},{48,51},{64,65},{80,83},{96,97},{112,115},{4... | collective-permute-start | bytes 2764808 | tf_op jit(solution)/shard_map/ppermute | solution.py:51
  38.3 1.1 %copy-start.2 = (bf16[6,16,3584]{2,1,0:T(8,128)(2,1)S(1)}, bf16[6,16,3584]{2,1,0:T(8,128)(2,1)}, u32[]{:S(2)}) copy-start(bf16[6,16,3584]{2,1,0:T(8,128)(2,1)} %param.11) | copy-start | bytes 2064388
  42.0 1.3 %copy-start = (bf16[288,3584]{1,0:T(8,128)(2,1)}, bf16[288,3584]{1,0:T(8,128)(2,1)S(1)}, u32[]{:S(2)}) copy-start(bf16[288,3584]{1,0:T(8,128)(2,1)S(1)} %get-tuple-element.11.near) | copy-start | bytes 6193156
  46.4 0.9 %copy-start.3 = (bf16[96,3584]{1,0:T(8,128)(2,1)}, bf16[96,3584]{1,0:T(8,128)(2,1)S(1)}, u32[]{:S(2)}) copy-start(bf16[96,3584]{1,0:T(8,128)(2,1)S(1)} %get-tuple-element.16.far) | copy-start | bytes 2064388
  47.3 12.8 %copy-start.8 = (s32[48]{0:T(128)S(1)}, s32[48]{0:T(128)}, u32[]{:S(2)}) copy-start(s32[48]{0:T(128)} %dest.1) | copy-start | bytes 580
  47.3 12.8 %copy-start.9 = (s32[48]{0:T(128)S(1)}, s32[48]{0:T(128)}, u32[]{:S(2)}) copy-start(s32[48]{0:T(128)} %lengths.1) | copy-start | bytes 580
  47.3 3.1 %collective-permute-start.8 = (bf16[1024,256]{1,0:T(8,128)(2,1)S(1)}, bf16[1024,256]{1,0:T(8,128)(2,1)S(1)}, u32[]{:S(2)}, u32[]{:S(2)}) collective-permute-start(bf16[1024,256]{1,0:T(8,128)(2,1)S(1)} %bitcast.24), channel_id=1, source_target_pairs={{0,16},{16,0},{32,48},{48,32},{64,80},{80,64},{96,112},{112,96},{4... | collective-permute-start | bytes 1572872 | tf_op jit(solution)/shard_map/ppermute | solution.py:39
  47.7 9.8 %collective-permute-start.12 = (bf16[6,64,256]{2,1,0:T(8,128)(2,1)S(1)}, bf16[6,64,256]{2,1,0:T(8,128)(2,1)S(1)}, u32[]{:S(2)}, u32[]{:S(2)}) collective-permute-start(bf16[6,64,256]{2,1,0:T(8,128)(2,1)S(1)} %get-tuple-element.14.kv0), channel_id=1, source_target_pairs={{0,1},{16,17},{32,33},{48,49},{64,65},{80,81},{96,97},{112,113},{4... | collective-permute-start | bytes 589832 | tf_op jit(solution)/shard_map/ppermute | solution.py:39
  48.5 9.0 %collective-permute-start.13 = (bf16[6,64,256]{2,1,0:T(8,128)(2,1)S(1)}, bf16[6,64,256]{2,1,0:T(8,128)(2,1)S(1)}, u32[]{:S(2)}, u32[]{:S(2)}) collective-permute-start(bf16[6,64,256]{2,1,0:T(8,128)(2,1)S(1)} %get-tuple-element.14.kv0), channel_id=1, source_target_pairs={{0,3},{16,19},{32,35},{48,51},{64,67},{80,83},{96,99},{112,115},{4... | collective-permute-start | bytes 589832 | tf_op jit(solution)/shard_map/ppermute | solution.py:39
  50.4 9.6 %collective-permute-start.14 = (bf16[6,64,256]{2,1,0:T(8,128)(2,1)S(1)}, bf16[6,64,256]{2,1,0:T(8,128)(2,1)S(1)}, u32[]{:S(2)}, u32[]{:S(2)}) collective-permute-start(bf16[6,64,256]{2,1,0:T(8,128)(2,1)S(1)} %get-tuple-element.14.kv0), channel_id=1, source_target_pairs={{0,2},{16,18},{32,34},{48,50},{64,66},{80,82},{96,98},{112,114},{4... | collective-permute-start | bytes 589832 | tf_op jit(solution)/shard_map/ppermute | solution.py:39
  51.4 1.6 %copy-start.1 = (bf16[288,3584]{1,0:T(8,128)(2,1)S(1)}, bf16[288,3584]{1,0:T(8,128)(2,1)}, u32[]{:S(2)}) copy-start(bf16[288,3584]{1,0:T(8,128)(2,1)} %copy-done) | copy-start | bytes 6193156
  52.9 1.1 %copy-start.4 = (bf16[96,3584]{1,0:T(8,128)(2,1)S(1)}, bf16[96,3584]{1,0:T(8,128)(2,1)}, u32[]{:S(2)}) copy-start(bf16[96,3584]{1,0:T(8,128)(2,1)} %copy-done.3) | copy-start | bytes 2064388

commit v7 on v5

--- a/solution.py
+++ b/solution.py
@@ -59,6 +59,7 @@
 
 
 VMEM_SPEC = pl.BlockSpec(memory_space=pltpu.VMEM)
+ANY_SPEC = pl.BlockSpec(memory_space=pl.ANY)
 SMEM_SPEC = pl.BlockSpec(memory_space=pltpu.SMEM)
 
 
@@ -128,17 +129,25 @@
     )(meta, *chunks, *small)
 
 
-def query_kernel(meta, near, far, w0, w1, w2, w3, cos_ref, sin_ref, q_out, rows):
+def query_kernel(
+    meta, near, far, w0, w1, w2, w3, cos_ref, sin_ref, q_out, rows, buf, sems
+):
     y, c, x = meta[0], meta[1], meta[2]
+    copies = [
+        pltpu.make_async_copy(ref, buf.at[n], sems.at[n]) for n, ref in enumerate((w0, w1, w2, w3))
+    ]
+    for copy in copies:
+        copy.start()
     rows[0 : 3 * CHUNK, :] = near[...]
     rows[3 * CHUNK : 4 * CHUNK, :] = far[...]
-    weights = (w0, w1, w2, w3)
     heads = [lax.rem(x + turn, 4) for turn in (0, 3 - 2 * c, 1 + 2 * c, 2)]
     for lo in (0, 2):
-        w = jnp.concatenate([weights[lo][:D, :], weights[lo + 1][:D, :]], axis=1)
+        copies[lo].wait()
+        copies[lo + 1].wait()
+        w = jnp.concatenate([buf[lo, :D, :], buf[lo + 1, :D, :]], axis=1)
         both = jnp.dot(rows[...], w, preferred_element_type=jnp.float32)
         for n in (lo, lo + 1):
-            tail = weights[n][D : D + BIAS_ROWS, :].astype(jnp.float32)
+            tail = buf[n, D : D + BIAS_ROWS, :].astype(jnp.float32)
             bias = tail[0:1, :] + tail[1:2, :] + tail[2:3, :]
             raw = both[:, (n - lo) * HD : (n - lo + 1) * HD] + bias
             for j in range(4):
@@ -154,10 +163,14 @@
     return pl.pallas_call(
         query_kernel,
         out_shape=jax.ShapeDtypeStruct((RESP, 4, 64, HD), jnp.bfloat16),
-        in_specs=[SMEM_SPEC] + [VMEM_SPEC] * 8,
+        in_specs=[SMEM_SPEC] + [VMEM_SPEC] * 2 + [ANY_SPEC] * 4 + [VMEM_SPEC] * 2,
         out_specs=VMEM_SPEC,
-        scratch_shapes=[pltpu.VMEM((4 * CHUNK, D), jnp.bfloat16)],
-        compiler_params=params(LIMIT),
+        scratch_shapes=[
+            pltpu.VMEM((4 * CHUNK, D), jnp.bfloat16),
+            pltpu.VMEM((4, D + BIAS_ROWS, HD), jnp.bfloat16),
+            pltpu.SemaphoreType.DMA((4,)),
+        ],
+        compiler_params=params(50),
         name="queries",
     )(meta, near, far, *weights, cos, sin)
 

time: 84.4 us -> 84.4 us (level)
  Pallas kernels: 13.6 us -> 16.4 us
  local copies, waits for them, and re-layouts: 13.4 us -> 11.8 us
  waiting for transfers between devices: 6.12 us -> 4.97 us
    pallas_call x1, Pallas kernels: 3.52 us -> 6.32 us  [make_queries(): pl.pallas_call(query_kernel, out_shape=jax.ShapeDtypeStruct((RESP, 4, 64,...]
    unnamed x20 -> x18, local copies, waits for them, and re-layouts: 6.02 us -> 4.42 us
    ppermute x12, waiting for transfers between devices: 6.11 us -> 4.96 us  [shift(): return lax.ppermute(v, AXES, pairs)]
  transfers between devices with their start and end apart: 16 -> 16, of which waited for: 3 -> 3; matrix products, arithmetic and copies ran while one was open for 13% -> 13% of each run, Pallas kernels for 9% -> 12%
where the time goes in v7:
time: 84.4 us; the launch traced here: 83.7 us
  starting transfers between devices  27.3 us (32%)
  blocking collectives  16.5 us (20%)
  Pallas kernels  16.4 us (19%)
  local copies, waits for them, and re-layouts  11.8 us (14%)
  waiting for transfers between devices  4.97 us (6%)
  other arithmetic  4.47 us (5%)
  between operations  2.26 us (3%)
    all_to_all x1, blocking collectives, on_device(): lax.all_to_all(ready.reshape(32, 64, HD), AXES, 0, 0, tiled=True, axis_in...  16.5 us
    ppermute x12, starting transfers between devices, shift(): return lax.ppermute(v, AXES, pairs)  13.6 us
    ppermute x3, starting transfers between devices, both_ways(): return lax.ppermute(v, AXES, pairs)  9.31 us
    pallas_call x1, Pallas kernels, make_queries(): pl.pallas_call(query_kernel, out_shape=jax.ShapeDtypeStruct((RESP, 4, 64,...  6.32 us
    pallas_call x1, Pallas kernels, attend(): pl.pallas_call(attend_kernel, out_shape=jax.ShapeDtypeStruct((GROUPS, 4,...  6.22 us
    ppermute x12, waiting for transfers between devices, shift(): return lax.ppermute(v, AXES, pairs)  4.96 us
    unnamed x18, local copies, waits for them, and re-layouts  4.42 us
    all_to_all x1, starting transfers between devices, on_device(): lax.all_to_all(spread, 'mp', 0, 0, tiled=True).reshape(1024, 2 * HD)  4.35 us
  transfers between devices with their start and end apart: 16, of which 3 were waited for; matrix products, arithmetic and copies ran while one was open for 13% of the time, Pallas kernels for 12%

profile of v7, /device:TPU:1, one launch (start us, length us, event | category | flops | bytes accessed | tf_op | source)
XLA Modules:
  0.0 83.7 jit_solution(9544996682165594284)
XLA Ops:
  0.0 2.1 %collective-permute-start = (bf16[96,3584]{1,0:T(8,128)(2,1)}, bf16[96,3584]{1,0:T(8,128)(2,1)}, u32[]{:S(2)}, u32[]{:S(2)}) collective-permute-start(bf16[96,3584]{1,0:T(8,128)(2,1)} %bitcast.27), channel_id=1, source_target_pairs={{0,4},{16,20},{32,36},{48,52},{64,68},{80,84},{96,100},{112,116},{... | collective-permute-start | bytes 2064392 | tf_op jit(solution)/shard_map/ppermute | solution.py:39
  2.1 1.5 %collective-permute-start.1 = (bf16[96,3584]{1,0:T(8,128)(2,1)}, bf16[96,3584]{1,0:T(8,128)(2,1)}, u32[]{:S(2)}, u32[]{:S(2)}) collective-permute-start(bf16[96,3584]{1,0:T(8,128)(2,1)} %bitcast.28), channel_id=1, source_target_pairs={{0,12},{16,28},{32,44},{48,60},{64,76},{80,92},{96,108},{112,124},... | collective-permute-start | bytes 2064392 | tf_op jit(solution)/shard_map/ppermute | solution.py:39
  3.6 1.0 %collective-permute-start.4 = (bf16[4,128,256]{2,1,0:T(8,128)(2,1)}, bf16[4,128,256]{2,1,0:T(8,128)(2,1)S(1)}, u32[]{:S(2)}, u32[]{:S(2)}) collective-permute-start(bf16[4,128,256]{2,1,0:T(8,128)(2,1)} %bitcast.40), channel_id=1, source_target_pairs={{0,16},{16,0},{32,48},{48,32},{64,80},{80,64},{96,112},{112,96},{4... | collective-permute-start | bytes 786440 | tf_op jit(solution)/shard_map/ppermute | solution.py:39
  6.6 0.7 fusion.8
  7.3 1.0 %broadcast_select_fusion = bf16[4,128,256]{2,1,0:T(8,128)(2,1)S(1)} fusion(bf16[4,128,256]{2,1,0:T(8,128)(2,1)S(1)} %collective-permute-done.4, pred[]{:T(512)S(6)} %eq.23, bf16[1,4,128,256]{3,2,1,0:T(8,128)(2,1)} %param.19), kind=kLoop, calls=%fused_computation.1 | loop fusion | flops 131072 | bytes 786433 | tf_op jit(solution)/shard_map/jit(_where)/select_n | solution.py:267
  8.3 3.9 %collective-permute-start.6 = (bf16[4,128,256]{2,1,0:T(8,128)(2,1)S(1)}, bf16[4,128,256]{2,1,0:T(8,128)(2,1)S(1)}, u32[]{:S(2)}, u32[]{:S(2)}) collective-permute-start(bf16[4,128,256]{2,1,0:T(8,128)(2,1)S(1)} %broadcast_select_fusion), channel_id=1, source_target_pairs={{0,32},{16,112},{32,64},{48,16},{64,96},{80,48},{96,0},{112,80},{4... | collective-permute-start | bytes 786440 | tf_op jit(solution)/shard_map/ppermute | solution.py:51
  12.2 1.2 %pad_maximum_fusion.w0 = bf16[3600,128]{1,0:T(8,128)(2,1)S(1)} fusion(bf16[16,128]{1,0:T(8,128)(2,1)S(1)} %fusion.5, bf16[3584,128]{1,0:T(8,128)(2,1)} %param.13), kind=kLoop, calls=%fused_computation | loop fusion | flops 1843200 | bytes 1843200 | tf_op jit(solution)/shard_map/concatenate | solution.py:259
  13.5 2.5 %collective-permute-start.9 = (bf16[3600,128]{1,0:T(8,128)(2,1)S(1)}, bf16[3600,128]{1,0:T(8,128)(2,1)}, u32[]{:S(2)}, u32[]{:S(2)}) collective-permute-start(bf16[3600,128]{1,0:T(8,128)(2,1)S(1)} %pad_maximum_fusion.w0), channel_id=1, source_target_pairs={{0,1},{16,19},{32,33},{48,51},{64,65},{80,83},{96,97},{112,115},{4... | collective-permute-start | bytes 2764808 | tf_op jit(solution)/shard_map/ppermute | solution.py:51
  16.0 0.7 constant_dynamic-slice_fusion.1
  16.7 0.7 constant_dynamic-slice_fusion
  17.3 0.8 collective-permute-start.7
  18.1 1.6 %constant_dynamic-slice_fusion.2 = (bf16[3584,128]{1,0:T(8,128)(2,1)S(1)}, bf16[3584,128]{1,0:T(8,128)(2,1)S(1)}) fusion(bf16[3584,512]{1,0:T(8,128)(2,1)} %param.17, s32[]{:T(128)S(6)} %select_n.94, bf16[3584,512]{1,0:T(8,128)(2,1)} %param.15), kind=kLoop, calls=%fused_computation.18 | loop fusion | bytes 3670020 | tf_op jit(solution)/shard_map/dynamic_slice | solution.py:251
  19.8 0.5 multiply_exponential_fusion
  20.3 1.9 %collective-permute-done.5 = bf16[4,64,256]{2,1,0:T(8,128)(2,1)S(1)} collective-permute-done((bf16[4,64,256]{2,1,0:T(8,128)(2,1)}, bf16[4,64,256]{2,1,0:T(8,128)(2,1)S(1)}, u32[]{:S(2)}, u32[]{:S(2)}) %collective-permute-start.5) | collective-permute-done | bytes 131104 | tf_op jit(solution)/shard_map/ppermute | solution.py:39
  22.2 0.0 collective-permute-done.7
  22.2 0.1 select_select_fusion
  22.3 0.8 %broadcast_in_dim.2 = bf16[4,4,64,256]{3,2,1,0:T(8,128)(2,1)} broadcast(bf16[4,64,256]{2,1,0:T(8,128)(2,1)S(1)} %select_select_fusion), dimensions={0,2,3} | broadcast | bytes 655360 | tf_op jit(solution)/shard_map/broadcast_in_dim | solution.py:279
  23.1 4.3 %all-to-all-start = ((bf16[16,64,256]{2,1,0:T(8,128)(2,1)}), bf16[16,64,256]{2,1,0:T(8,128)(2,1)S(1)}, u32[]{:S(2)}, u32[]{:S(2)}) async-start(bf16[16,64,256]{2,1,0:T(8,128)(2,1)} %bitcast.38), calls=%async_computation | async-start | bytes 1048576 | tf_op jit(solution)/shard_map/all_to_all | solution.py:280
  27.5 0.7 reshape.59.gain
  28.2 0.0 collective-permute-done.before
  28.2 1.0 %slice.12 = bf16[48,3584]{1,0:T(8,128)(2,1)S(1)} slice(bf16[96,3584]{1,0:T(8,128)(2,1)} %collective-permute-done.before), slice={[0:48], [0:3584]} | slice | bytes 688128 | tf_op jit(solution)/shard_map/slice | solution.py:238
  29.2 1.4 %collective-permute-start.2 = (bf16[48,3584]{1,0:T(8,128)(2,1)S(1)}, bf16[48,3584]{1,0:T(8,128)(2,1)S(1)}, u32[]{:S(2)}, u32[]{:S(2)}) collective-permute-start(bf16[48,3584]{1,0:T(8,128)(2,1)S(1)} %slice.12), channel_id=1, source_target_pairs={{0,4},{16,20},{32,36},{48,52},{64,68},{80,84},{96,100},{112,116},{... | collective-permute-start | bytes 1032200 | tf_op jit(solution)/shard_map/ppermute | solution.py:39
  30.7 0.0 collective-permute-done.1.after
  30.7 1.0 %slice.13 = bf16[48,3584]{1,0:T(8,128)(2,1)S(1)} slice(bf16[96,3584]{1,0:T(8,128)(2,1)} %collective-permute-done.1.after), slice={[48:96], [0:3584]} | slice | bytes 688128 | tf_op jit(solution)/shard_map/slice | solution.py:239
  31.7 1.4 %collective-permute-start.3 = (bf16[48,3584]{1,0:T(8,128)(2,1)S(1)}, bf16[48,3584]{1,0:T(8,128)(2,1)S(1)}, u32[]{:S(2)}, u32[]{:S(2)}) collective-permute-start(bf16[48,3584]{1,0:T(8,128)(2,1)S(1)} %slice.13), channel_id=1, source_target_pairs={{0,12},{16,28},{32,44},{48,60},{64,76},{80,92},{96,108},{112,124},... | collective-permute-start | bytes 1032200 | tf_op jit(solution)/shard_map/ppermute | solution.py:39
  33.1 0.8 fusion
  33.9 0.0 collective-permute-done.9.w1
  33.9 1.3 %collective-permute-start.10 = (bf16[3600,128]{1,0:T(8,128)(2,1)}, bf16[3600,128]{1,0:T(8,128)(2,1)}, u32[]{:S(2)}, u32[]{:S(2)}) collective-permute-start(bf16[3600,128]{1,0:T(8,128)(2,1)} %collective-permute-done.9.w1), channel_id=1, source_target_pairs={{0,16},{16,0},{32,48},{48,32},{64,80},{80,64},{96,112},{112,96},{4... | collective-permute-start | bytes 2764808 | tf_op jit(solution)/shard_map/ppermute | solution.py:39
  35.2 2.8 %collective-permute-start.11 = (bf16[3600,128]{1,0:T(8,128)(2,1)}, bf16[3600,128]{1,0:T(8,128)(2,1)}, u32[]{:S(2)}, u32[]{:S(2)}) collective-permute-start(bf16[3600,128]{1,0:T(8,128)(2,1)} %collective-permute-done.9.w1), channel_id=1, source_target_pairs={{0,1},{16,19},{32,33},{48,51},{64,65},{80,83},{96,97},{112,115},{4... | collective-permute-start | bytes 2764808 | tf_op jit(solution)/shard_map/ppermute | solution.py:51
  38.0 0.1 pad_add_fusion.meta
  38.1 0.1 pad_maximum_fusion.1
  38.2 0.0 copy-start.1
  38.2 1.1 %copy-done.1 = bf16[6,16,3584]{2,1,0:T(8,128)(2,1)S(1)} copy-done((bf16[6,16,3584]{2,1,0:T(8,128)(2,1)S(1)}, bf16[6,16,3584]{2,1,0:T(8,128)(2,1)}, u32[]{:S(2)}) %copy-start.1) | copy-done | bytes 688152
  39.3 2.6 %near_rows.1 = (bf16[6,64,256]{2,1,0:T(8,128)(2,1)S(1)}, bf16[288,3584]{1,0:T(8,128)(2,1)S(1)}) custom-call(s32[4]{0:T(128)S(1)} %pad_add_fusion.meta, bf16[96,3584]{1,0:T(8,128)(2,1)S(1)} %bitcast.29, bf16[96,3584]{1,0:T(8,128)(2,1)} %collective-permute-done.before, bf16[96,3584]{1,0:T(8,128)(2,1)} %collective-permute-done.1.after, ...), custom_call_target="tpu_custom_call" | custom-call | tf_op jit(solution)/shard_map/near_rows/pallas_call | solution.py:119
  42.0 1.3 %copy-done = bf16[288,3584]{1,0:T(8,128)(2,1)} copy-done((bf16[288,3584]{1,0:T(8,128)(2,1)}, bf16[288,3584]{1,0:T(8,128)(2,1)S(1)}, u32[]{:S(2)}) %copy-start) | copy-done | bytes 2064408
  43.3 1.8 %collective-permute-done.2.far_a = bf16[48,3584]{1,0:T(8,128)(2,1)S(1)} collective-permute-done((bf16[48,3584]{1,0:T(8,128)(2,1)S(1)}, bf16[48,3584]{1,0:T(8,128)(2,1)S(1)}, u32[]{:S(2)}, u32[]{:S(2)}) %collective-permute-start.2) | collective-permute-done | bytes 344096 | tf_op jit(solution)/shard_map/ppermute | solution.py:39
  45.1 1.2 %far_rows.1 = (bf16[6,64,256]{2,1,0:T(8,128)(2,1)S(1)}, bf16[96,3584]{1,0:T(8,128)(2,1)S(1)}) custom-call(s32[4]{0:T(128)S(1)} %pad_add_fusion.meta, bf16[6,64,256]{2,1,0:T(8,128)(2,1)S(1)} %get-tuple-element.12.near, bf16[48,3584]{1,0:T(8,128)(2,1)S(1)} %collective-permute-done.2.far_a, bf16[48,3584]{1,0:T(8,128)(2,1)S(1)} %collective-permute-done.3.far_b, ...), custom_call_target="tpu_custom_call" | custom-call | tf_op jit(solution)/shard_map/far_rows/pallas_call | solution.py:119
  46.4 0.9 %copy-done.2 = bf16[96,3584]{1,0:T(8,128)(2,1)} copy-done((bf16[96,3584]{1,0:T(8,128)(2,1)}, bf16[96,3584]{1,0:T(8,128)(2,1)S(1)}, u32[]{:S(2)}) %copy-start.2) | copy-done | bytes 688152
  47.3 0.4 collective-permute-start.8
  47.7 0.8 collective-permute-start.12
  48.5 1.9 %collective-permute-start.13 = (bf16[6,64,256]{2,1,0:T(8,128)(2,1)S(1)}, bf16[6,64,256]{2,1,0:T(8,128)(2,1)S(1)}, u32[]{:S(2)}, u32[]{:S(2)}) collective-permute-start(bf16[6,64,256]{2,1,0:T(8,128)(2,1)S(1)} %get-tuple-element.14.kv0), channel_id=1, source_target_pairs={{0,3},{16,19},{32,35},{48,51},{64,67},{80,83},{96,99},{112,115},{4... | collective-permute-start | bytes 589832 | tf_op jit(solution)/shard_map/ppermute | solution.py:39
  50.4 0.9 %collective-permute-start.14 = (bf16[6,64,256]{2,1,0:T(8,128)(2,1)S(1)}, bf16[6,64,256]{2,1,0:T(8,128)(2,1)S(1)}, u32[]{:S(2)}, u32[]{:S(2)}) collective-permute-start(bf16[6,64,256]{2,1,0:T(8,128)(2,1)S(1)} %get-tuple-element.14.kv0), channel_id=1, source_target_pairs={{0,2},{16,18},{32,34},{48,50},{64,66},{80,82},{96,98},{112,114},{4... | collective-permute-start | bytes 589832 | tf_op jit(solution)/shard_map/ppermute | solution.py:39
  51.4 1.1 %copy-done.3 = bf16[96,3584]{1,0:T(8,128)(2,1)S(1)} copy-done((bf16[96,3584]{1,0:T(8,128)(2,1)S(1)}, bf16[96,3584]{1,0:T(8,128)(2,1)}, u32[]{:S(2)}) %copy-start.3) | copy-done | bytes 688152
  52.5 6.3 %queries.1.q_ref = bf16[6,4,64,128]{3,2,1,0:T(8,128)(2,1)S(1)} custom-call(s32[4]{0:T(128)S(1)} %pad_add_fusion.meta, bf16[288,3584]{1,0:T(8,128)(2,1)} %copy-done, bf16[96,3584]{1,0:T(8,128)(2,1)S(1)} %copy-done.3, bf16[3600,128]{1,0:T(8,128)(2,1)S(1)} %pad_maximum_fusion.w0, bf16[3600,128]{1,0:T(8,128)(2,1)} %collective-permute-done.9.w1, ...), custom_call_target="tpu_custom_call" | custom-call | tf_op jit(solution)/shard_map/queries/pallas_call | solution.py:163
  58.8 1.2 %collective-permute-done.14.kv3 = bf16[6,64,256]{2,1,0:T(8,128)(2,1)S(1)} collective-permute-done((bf16[6,64,256]{2,1,0:T(8,128)(2,1)S(1)}, bf16[6,64,256]{2,1,0:T(8,128)(2,1)S(1)}, u32[]{:S(2)}, u32[]{:S(2)}) %collective-permute-start.14) | collective-permute-done | bytes 196640 | tf_op jit(solution)/shard_map/ppermute | solution.py:39
  60.0 6.2 %attend.1 = bf16[8,4,64,128]{3,2,1,0:T(8,128)(2,1)S(1)} custom-call(s32[4]{0:T(128)S(1)} %pad_add_fusion.meta, s32[48]{0:T(128)S(1)} %copy-done.7, s32[48]{0:T(128)S(1)} %copy-done.8, bf16[6,4,64,128]{3,2,1,0:T(8,128)(2,1)S(1)} %queries.1.q_ref, bf16[1024,256]{1,0:T(8,128)(2,1)S(1)} %bitcast.25, bf16[1024,256]{1,0:T(8,128)(2,1)S(1)} %collective-permute-done.8.c_other, ...), custom_call_target="tpu_custom_call" | custom-call | tf_op jit(solution)/shard_map/attend/pallas_call | solution.py:215
  66.3 16.5 %all_to_all.10 = bf16[32,64,128]{2,1,0:T(8,128)(2,1)S(1)} all-to-all(bf16[32,64,128]{2,1,0:T(8,128)(2,1)S(1)} %bitcast.26), channel_id=1, replica_groups={{0,1,2,3,16,17,18,19,32,33,34,35,48,49,50,51,64,65,66,67,80,81,82,83,96..., dimensions={0} | all-to-all | bytes 1048576 | tf_op jit(solution)/shard_map/all_to_all | solution.py:293
  82.8 0.9 %copy.12 = bf16[8,4,4,16,128]{4,3,1,2,0:T(8,128)(2,1)} copy(bf16[8,4,4,16,128]{4,3,2,1,0:T(8,128)(2,1)S(1)} %bitcast.39) | data formatting | bytes 1048576 | tf_op jit(solution)/shard_map/reshape | solution.py:296
  (25 shorter events, 0.1 us)
Async XLA Ops:
  0.0 19.7 %copy-start.6 = (s32[48]{0:T(128)S(1)}, s32[48]{0:T(128)}, u32[]{:S(2)}) copy-start(s32[48]{0:T(128)} %dest.1) | copy-start | bytes 580
  0.0 28.2 %collective-permute-start = (bf16[96,3584]{1,0:T(8,128)(2,1)}, bf16[96,3584]{1,0:T(8,128)(2,1)}, u32[]{:S(2)}, u32[]{:S(2)}) collective-permute-start(bf16[96,3584]{1,0:T(8,128)(2,1)} %bitcast.27), channel_id=1, source_target_pairs={{0,4},{16,20},{32,36},{48,52},{64,68},{80,84},{96,100},{112,116},{... | collective-permute-start | bytes 2064392 | tf_op jit(solution)/shard_map/ppermute | solution.py:39
  2.1 28.5 %collective-permute-start.1 = (bf16[96,3584]{1,0:T(8,128)(2,1)}, bf16[96,3584]{1,0:T(8,128)(2,1)}, u32[]{:S(2)}, u32[]{:S(2)}) collective-permute-start(bf16[96,3584]{1,0:T(8,128)(2,1)} %bitcast.28), channel_id=1, source_target_pairs={{0,12},{16,28},{32,44},{48,60},{64,76},{80,92},{96,108},{112,124},... | collective-permute-start | bytes 2064392 | tf_op jit(solution)/shard_map/ppermute | solution.py:39
  3.6 3.7 %collective-permute-start.4 = (bf16[4,128,256]{2,1,0:T(8,128)(2,1)}, bf16[4,128,256]{2,1,0:T(8,128)(2,1)S(1)}, u32[]{:S(2)}, u32[]{:S(2)}) collective-permute-start(bf16[4,128,256]{2,1,0:T(8,128)(2,1)} %bitcast.40), channel_id=1, source_target_pairs={{0,16},{16,0},{32,48},{48,32},{64,80},{80,64},{96,112},{112,96},{4... | collective-permute-start | bytes 786440 | tf_op jit(solution)/shard_map/ppermute | solution.py:39
  8.3 8.4 %collective-permute-start.6 = (bf16[4,128,256]{2,1,0:T(8,128)(2,1)S(1)}, bf16[4,128,256]{2,1,0:T(8,128)(2,1)S(1)}, u32[]{:S(2)}, u32[]{:S(2)}) collective-permute-start(bf16[4,128,256]{2,1,0:T(8,128)(2,1)S(1)} %broadcast_select_fusion), channel_id=1, source_target_pairs={{0,32},{16,112},{32,64},{48,16},{64,96},{80,48},{96,0},{112,80},{4... | collective-permute-start | bytes 786440 | tf_op jit(solution)/shard_map/ppermute | solution.py:51
  13.5 20.4 %collective-permute-start.9 = (bf16[3600,128]{1,0:T(8,128)(2,1)S(1)}, bf16[3600,128]{1,0:T(8,128)(2,1)}, u32[]{:S(2)}, u32[]{:S(2)}) collective-permute-start(bf16[3600,128]{1,0:T(8,128)(2,1)S(1)} %pad_maximum_fusion.w0), channel_id=1, source_target_pairs={{0,1},{16,19},{32,33},{48,51},{64,65},{80,83},{96,97},{112,115},{4... | collective-permute-start | bytes 2764808 | tf_op jit(solution)/shard_map/ppermute | solution.py:51
  16.7 5.5 %collective-permute-start.5 = (bf16[4,64,256]{2,1,0:T(8,128)(2,1)}, bf16[4,64,256]{2,1,0:T(8,128)(2,1)S(1)}, u32[]{:S(2)}, u32[]{:S(2)}) collective-permute-start(bf16[4,64,256]{2,1,0:T(8,128)(2,1)} %constant_dynamic-slice_fusion.1), channel_id=1, source_target_pairs={{0,64},{16,80},{32,96},{48,112},{64,0},{80,16},{96,32},{112,48},{4... | collective-permute-start | bytes 393224 | tf_op jit(solution)/shard_map/ppermute | solution.py:39
  17.3 20.9 %copy-start.4 = (f32[512]{0:T(512)S(1)}, f32[512]{0:T(512)}, u32[]{:S(2)}) copy-start(f32[512]{0:T(512)} %param.16) | copy-start | bytes 6148
  17.3 20.9 %copy-start.5 = (f32[512]{0:T(512)S(1)}, f32[512]{0:T(512)}, u32[]{:S(2)}) copy-start(f32[512]{0:T(512)} %param.18) | copy-start | bytes 6148
  17.3 4.9 %collective-permute-start.7 = (bf16[4,64,256]{2,1,0:T(8,128)(2,1)}, bf16[4,64,256]{2,1,0:T(8,128)(2,1)S(1)}, u32[]{:S(2)}, u32[]{:S(2)}) collective-permute-start(bf16[4,64,256]{2,1,0:T(8,128)(2,1)} %constant_dynamic-slice_fusion), channel_id=1, source_target_pairs={{0,16},{16,0},{32,48},{48,32},{64,80},{80,64},{96,112},{112,96},{4... | collective-permute-start | bytes 393224 | tf_op jit(solution)/shard_map/ppermute | solution.py:39
  23.1 24.1 %all-to-all-start = ((bf16[16,64,256]{2,1,0:T(8,128)(2,1)}), bf16[16,64,256]{2,1,0:T(8,128)(2,1)S(1)}, u32[]{:S(2)}, u32[]{:S(2)}) async-start(bf16[16,64,256]{2,1,0:T(8,128)(2,1)} %bitcast.38), calls=%async_computation | async-start | bytes 1048576 | tf_op jit(solution)/shard_map/all_to_all | solution.py:280
  29.2 15.9 %collective-permute-start.2 = (bf16[48,3584]{1,0:T(8,128)(2,1)S(1)}, bf16[48,3584]{1,0:T(8,128)(2,1)S(1)}, u32[]{:S(2)}, u32[]{:S(2)}) collective-permute-start(bf16[48,3584]{1,0:T(8,128)(2,1)S(1)} %slice.12), channel_id=1, source_target_pairs={{0,4},{16,20},{32,36},{48,52},{64,68},{80,84},{96,100},{112,116},{... | collective-permute-start | bytes 1032200 | tf_op jit(solution)/shard_map/ppermute | solution.py:39
  31.7 13.4 %collective-permute-start.3 = (bf16[48,3584]{1,0:T(8,128)(2,1)S(1)}, bf16[48,3584]{1,0:T(8,128)(2,1)S(1)}, u32[]{:S(2)}, u32[]{:S(2)}) collective-permute-start(bf16[48,3584]{1,0:T(8,128)(2,1)S(1)} %slice.13), channel_id=1, source_target_pairs={{0,12},{16,28},{32,44},{48,60},{64,76},{80,92},{96,108},{112,124},... | collective-permute-start | bytes 1032200 | tf_op jit(solution)/shard_map/ppermute | solution.py:39
  33.9 17.5 %collective-permute-start.10 = (bf16[3600,128]{1,0:T(8,128)(2,1)}, bf16[3600,128]{1,0:T(8,128)(2,1)}, u32[]{:S(2)}, u32[]{:S(2)}) collective-permute-start(bf16[3600,128]{1,0:T(8,128)(2,1)} %collective-permute-done.9.w1), channel_id=1, source_target_pairs={{0,16},{16,0},{32,48},{48,32},{64,80},{80,64},{96,112},{112,96},{4... | collective-permute-start | bytes 2764808 | tf_op jit(solution)/shard_map/ppermute | solution.py:39
  35.2 16.2 %collective-permute-start.11 = (bf16[3600,128]{1,0:T(8,128)(2,1)}, bf16[3600,128]{1,0:T(8,128)(2,1)}, u32[]{:S(2)}, u32[]{:S(2)}) collective-permute-start(bf16[3600,128]{1,0:T(8,128)(2,1)} %collective-permute-done.9.w1), channel_id=1, source_target_pairs={{0,1},{16,19},{32,33},{48,51},{64,65},{80,83},{96,97},{112,115},{4... | collective-permute-start | bytes 2764808 | tf_op jit(solution)/shard_map/ppermute | solution.py:51
  38.2 1.1 %copy-start.1 = (bf16[6,16,3584]{2,1,0:T(8,128)(2,1)S(1)}, bf16[6,16,3584]{2,1,0:T(8,128)(2,1)}, u32[]{:S(2)}) copy-start(bf16[6,16,3584]{2,1,0:T(8,128)(2,1)} %param.11) | copy-start | bytes 2064388
  42.0 1.3 %copy-start = (bf16[288,3584]{1,0:T(8,128)(2,1)}, bf16[288,3584]{1,0:T(8,128)(2,1)S(1)}, u32[]{:S(2)}) copy-start(bf16[288,3584]{1,0:T(8,128)(2,1)S(1)} %get-tuple-element.11.near) | copy-start | bytes 6193156
  46.4 0.9 %copy-start.2 = (bf16[96,3584]{1,0:T(8,128)(2,1)}, bf16[96,3584]{1,0:T(8,128)(2,1)S(1)}, u32[]{:S(2)}) copy-start(bf16[96,3584]{1,0:T(8,128)(2,1)S(1)} %get-tuple-element.16.far) | copy-start | bytes 2064388
  47.3 12.8 %copy-start.7 = (s32[48]{0:T(128)S(1)}, s32[48]{0:T(128)}, u32[]{:S(2)}) copy-start(s32[48]{0:T(128)} %dest.1) | copy-start | bytes 580
  47.3 12.8 %copy-start.8 = (s32[48]{0:T(128)S(1)}, s32[48]{0:T(128)}, u32[]{:S(2)}) copy-start(s32[48]{0:T(128)} %lengths.1) | copy-start | bytes 580
  47.3 3.1 %collective-permute-start.8 = (bf16[1024,256]{1,0:T(8,128)(2,1)S(1)}, bf16[1024,256]{1,0:T(8,128)(2,1)S(1)}, u32[]{:S(2)}, u32[]{:S(2)}) collective-permute-start(bf16[1024,256]{1,0:T(8,128)(2,1)S(1)} %bitcast.24), channel_id=1, source_target_pairs={{0,16},{16,0},{32,48},{48,32},{64,80},{80,64},{96,112},{112,96},{4... | collective-permute-start | bytes 1572872 | tf_op jit(solution)/shard_map/ppermute | solution.py:39
  47.7 11.1 %collective-permute-start.12 = (bf16[6,64,256]{2,1,0:T(8,128)(2,1)S(1)}, bf16[6,64,256]{2,1,0:T(8,128)(2,1)S(1)}, u32[]{:S(2)}, u32[]{:S(2)}) collective-permute-start(bf16[6,64,256]{2,1,0:T(8,128)(2,1)S(1)} %get-tuple-element.14.kv0), channel_id=1, source_target_pairs={{0,1},{16,17},{32,33},{48,49},{64,65},{80,81},{96,97},{112,113},{4... | collective-permute-start | bytes 589832 | tf_op jit(solution)/shard_map/ppermute | solution.py:39
  48.5 10.3 %collective-permute-start.13 = (bf16[6,64,256]{2,1,0:T(8,128)(2,1)S(1)}, bf16[6,64,256]{2,1,0:T(8,128)(2,1)S(1)}, u32[]{:S(2)}, u32[]{:S(2)}) collective-permute-start(bf16[6,64,256]{2,1,0:T(8,128)(2,1)S(1)} %get-tuple-element.14.kv0), channel_id=1, source_target_pairs={{0,3},{16,19},{32,35},{48,51},{64,67},{80,83},{96,99},{112,115},{4... | collective-permute-start | bytes 589832 | tf_op jit(solution)/shard_map/ppermute | solution.py:39
  50.4 9.6 %collective-permute-start.14 = (bf16[6,64,256]{2,1,0:T(8,128)(2,1)S(1)}, bf16[6,64,256]{2,1,0:T(8,128)(2,1)S(1)}, u32[]{:S(2)}, u32[]{:S(2)}) collective-permute-start(bf16[6,64,256]{2,1,0:T(8,128)(2,1)S(1)} %get-tuple-element.14.kv0), channel_id=1, source_target_pairs={{0,2},{16,18},{32,34},{48,50},{64,66},{80,82},{96,98},{112,114},{4... | collective-permute-start | bytes 589832 | tf_op jit(solution)/shard_map/ppermute | solution.py:39
  51.4 1.1 %copy-start.3 = (bf16[96,3584]{1,0:T(8,128)(2,1)S(1)}, bf16[96,3584]{1,0:T(8,128)(2,1)}, u32[]{:S(2)}) copy-start(bf16[96,3584]{1,0:T(8,128)(2,1)} %copy-done.2) | copy-start | bytes 2064388
